TPU v7x, 256 devices: a whole 4x4x8 slice. The times are simulated.
256 devices in a mesh: chain: 32 (over z_lo, y, core), tp: 8 (over z_hi, x).
Axes of the slice: x: 4, y: 4, z: 8 (z_hi: 2, z_lo: 4; z = z_hi * 4 + z_lo), core: 2. Of those that a mesh axis runs over, the one named last changes fastest.
Arguments:
- hidden_first: bfloat16 [28672, 8192], P('chain', 'tp')
- hidden_second: bfloat16 [28672, 8192], P('chain', 'tp')
- weight_buffer: bfloat16 [32, 2, 8192, 2048], P('chain', None, 'tp'), may hold values from -0.0625 to 0.0625
- gain_buffer: bfloat16 [32, 2, 8192], P('chain', None, 'tp'), may hold values from 0.25 to 1.75
- loaded_layers: int32 [32], P('chain'), may hold values from 0 to 2, as said below
- positions: int32 [28672], P('chain'), may hold values from 0 to 4542, as said below
Outputs:
- cache_rows: bfloat16 [2, 28672, 2048], P(None, 'chain', 'tp')
Inputs may be any that keep to these rules, and one draw needn't show every extreme that they name: `loaded_layers`: entry 0, the source instance, holds all 2 layers. Each instance's rows are two prompts of 448 tokens; each prompt's positions are consecutive from its own start.
All inputs are finite; a program needn't handle non-finite values.
Results may differ from a plain program's by a relative error of at most 0.018.
Values may be sent and summed in bfloat16 or wider, within the bound.
No kernel may reach another device: no remote copies, remote signals or barrier semaphores. Data moves between devices by JAX's collectives and lax.ppermute only.
A program may use at most 128 MiB of HBM per device.

v0:
```python
import jax
import jax.numpy as jnp
from jax import lax
from jax.sharding import PartitionSpec as P

HD = 128
LAYERS = 2


def spread(block, axis, owner):
    block = jnp.where(lax.axis_index(axis) == owner, block, jnp.zeros_like(block))
    return lax.psum(block, axis)


def rotate(keys, positions):
    half = keys.shape[-1] // 2
    freq = 500000.0 ** (-2.0 * jnp.arange(half, dtype=jnp.float32) / keys.shape[-1])
    angle = positions.astype(jnp.float32)[:, None] * freq[None, :]
    cosine = jnp.cos(angle)[:, None, :]
    sine = jnp.sin(angle)[:, None, :]
    first = keys[..., :half]
    second = keys[..., half:]
    return jnp.concatenate(
        [first * cosine - second * sine, second * cosine + first * sine], axis=-1
    )


def layer_rows(rows, weights, gains, meansq, positions, head_size):
    scaled = (rows.astype(jnp.float32) * gains.astype(jnp.float32)[None, :]).astype(jnp.bfloat16)
    partial_value = jnp.dot(scaled, weights, preferred_element_type=jnp.float32)
    term = partial_value.astype(jnp.bfloat16).astype(jnp.float32)
    mine = lax.psum_scatter(
        term.astype(jnp.bfloat16), "tp", scatter_dimension=1, tiled=True
    ).astype(jnp.float32)
    mixed = mine * lax.rsqrt(meansq + 1e-05)[:, None]
    count = rows.shape[0]
    heads = mixed.reshape(count, mixed.shape[1] // (2 * head_size), 2 * head_size)
    keys = rotate(heads[..., :head_size], positions)
    joined = jnp.concatenate([keys, heads[..., head_size:]], axis=-1)
    return joined.reshape(count, mixed.shape[1]).astype(jnp.bfloat16)


def shards(hidden_first, hidden_second, weight_buffer, gain_buffer, loaded_layers, positions):
    inputs = (hidden_first, hidden_second)
    width = hidden_first.shape[1] * lax.axis_size("tp")
    first_wide = hidden_first.astype(jnp.float32)
    second_wide = hidden_second.astype(jnp.float32)
    squares = lax.psum(
        (jnp.sum(first_wide * first_wide, axis=1), jnp.sum(second_wide * second_wide, axis=1)), "tp"
    )
    resident_count = loaded_layers[0]
    source_w, source_g = (spread(weight_buffer[0], "chain", 0), spread(gain_buffer[0], "chain", 0))
    results = []
    for layer in range(LAYERS):
        layer_w, layer_g = (source_w[layer], source_g[layer])
        resident = resident_count > layer
        weights = jnp.where(resident, weight_buffer[0, layer], layer_w)
        gains = jnp.where(resident, gain_buffer[0, layer], layer_g)
        meansq = squares[layer] / width
        results.append(layer_rows(inputs[layer], weights, gains, meansq, positions, HD))
    return jnp.stack(results, axis=0)


def solution(mesh):
    placed = (
        P("chain", "tp"),
        P("chain", "tp"),
        P("chain", None, "tp", None),
        P("chain", None, "tp"),
        P("chain"),
        P("chain"),
    )
    return jax.shard_map(
        shards, mesh=mesh, in_specs=placed, out_specs=P(None, "chain", "tp"), check_vma=False
    )
```

profile of v0, /device:TPU:6, one launch (start us, length us, event | category | flops | bytes accessed | tf_op | source)
XLA Modules:
  0.0 575.9 jit_solution(8973824507670880411)
XLA Ops:
  6.5 0.0 all-reduce.3.cloned.1.call-start
  6.5 7.1 %select_bitcast_fusion = bf16[2,1024,2048]{2,1,0:T(8,128)(2,1)} fusion(bf16[1,2,1024,2048]{3,2,1,0:T(8,128)(2,1)} %param.8, pred[]{:T(512)S(6)} %eq.4), kind=kLoop, calls=%fused_computation | loop fusion | flops 4194304 | bytes 16777216 | tf_op jit(solution)/shard_map/jit(_where)/select_n | solution.py:11
  13.7 0.0 copy-start.1
  13.7 0.0 copy-start
  13.7 0.0 all-reduce.3.cloned.1.call-update
  13.7 0.0 reduce-scatter.5.cloned.1.call-start
  14.5 0.0 copy-done.1
  14.6 70.6 %psum.28 = bf16[2,1024]{1,0:T(2,128)(2,1)S(1)} all-reduce(bf16[2,1024]{1,0:T(2,128)(2,1)S(1)} %fusion.43), channel_id=1, replica_groups=mesh['chain'=32,'tp'=8] {'chain'}, use_global_device_ids=true, to_apply=%region_0.0 | all-reduce | flops 2048 | bytes 8192 | tf_op jit(solution)/shard_map/psum | solution.py:12
  85.2 229.9 %all-reduce.3.cloned.1.call-done = bf16[2,1024,2048]{2,1,0:T(8,128)(2,1)} async-done(((bf16[2,1024,2048]{2,1,0:T(8,128)(2,1)}), bf16[2,1024,2048]{2,1,0:T(8,128)(2,1)}) %all-reduce.3.cloned.1.call-update) | async-done | bytes 8388624 | tf_op jit(solution)/shard_map/psum | solution.py:12
  315.1 0.0 copy-done
  315.1 9.8 %fusion.19 = bf16[896,2048]{0,1:T(8,128)(2,1)} fusion(bf16[2,1024,2048]{2,1,0:T(8,128)(2,1)} %all-reduce.3.cloned.1.call-done, bf16[1,2,1024,2048]{3,2,1,0:T(8,128)(2,1)} %param.8, pred[]{:T(512)} %bitcast.9, bf16[896,1024]{1,0:T(8,128)(2,1)S(1)} %copy-done, f32[1024]{0:T(1024)S(1)} %bitcast.49), kind=kOutput, calls=%fused_computation.22 | convolution fusion | flops 3764781056 | bytes 13898240 | tf_op jit(solution)/shard_map/dot_general | solution.py:30
  324.9 0.0 reduce-scatter.5.cloned.1.call-update
  324.9 0.0 reduce-scatter.3.cloned.1.call-start
  324.9 10.5 %fusion.16 = bf16[896,2048]{0,1:T(8,128)(2,1)} fusion(bf16[2,1024,2048]{2,1,0:T(8,128)(2,1)} %all-reduce.3.cloned.1.call-done, bf16[1,2,1024,2048]{3,2,1,0:T(8,128)(2,1)} %param.8, pred[]{:T(512)} %bitcast, bf16[896,1024]{1,0:T(8,128)(2,1)} %param.6, f32[1024]{0:T(1024)S(1)} %bitcast.48), kind=kOutput, calls=%fused_computation.21 | convolution fusion | flops 3764781056 | bytes 13898240 | tf_op jit(solution)/shard_map/dot_general | solution.py:30
  335.5 0.0 copy-start.2
  335.5 0.0 reduce-scatter.3.cloned.1.call-update
  335.5 0.7 copy-done.2
  336.2 0.4 fusion.15
  336.6 1.9 fusion.13
  338.5 26.5 %all-reduce = (f32[896]{0:T(1024)S(1)}, f32[896]{0:T(1024)S(1)}) all-reduce(f32[896]{0:T(1024)S(1)} %fusion.15, f32[896]{0:T(1024)S(1)} %fusion.13), channel_id=1, replica_groups=mesh['chain'=32,'tp'=8] {'tp'}, use_global_device_ids=true, to_apply=%region_7.8 | all-reduce | flops 1792 | bytes 14336 | tf_op jit(solution)/shard_map/psum | solution.py:48
  365.0 79.5 %reduce-scatter.5.cloned.1.call-done = bf16[896,256]{0,1:T(8,128)(2,1)} async-done(((bf16[896,2048]{0,1:T(8,128)(2,1)}), bf16[896,256]{0,1:T(8,128)(2,1)}) %reduce-scatter.5.cloned.1.call-update) | async-done | bytes 458768 | tf_op jit(solution)/shard_map/reduce_scatter | solution.py:32
  444.5 1.1 multiply_bitcast_fusion
  445.7 120.1 %reduce-scatter.3.cloned.1.call-done = bf16[896,256]{0,1:T(8,128)(2,1)} async-done(((bf16[896,2048]{0,1:T(8,128)(2,1)}), bf16[896,256]{0,1:T(8,128)(2,1)}) %reduce-scatter.3.cloned.1.call-update) | async-done | bytes 458768 | tf_op jit(solution)/shard_map/reduce_scatter | solution.py:32
  565.8 1.1 multiply_bitcast_fusion.1
  566.9 1.0 fusion.35
  568.0 0.1 pad_maximum_fusion
  568.1 1.3 copy.9
  (9 shorter events, 0.2 us)
Async XLA Ops:
  6.5 308.5 %all-reduce.3.cloned.1.call-start = ((), (), s32[]{:S(2)}) async-start(), calls=%async_computation.2 | async-start | bytes 16777216 | tf_op jit(solution)/shard_map/psum | solution.py:12
  13.7 0.9 copy-start.1
  13.7 301.4 %copy-start = (bf16[896,1024]{1,0:T(8,128)(2,1)S(1)}, bf16[896,1024]{1,0:T(8,128)(2,1)}, u32[]{:S(2)}) copy-start(bf16[896,1024]{1,0:T(8,128)(2,1)} %param.7) | copy-start | bytes 5505028
  13.7 430.8 %reduce-scatter.5.cloned.1.call-start = ((), (), s32[]{:S(2)}) async-start(), calls=%async_computation.4 | async-start | bytes 4128768 | tf_op jit(solution)/shard_map/reduce_scatter | solution.py:32
  324.9 240.9 %reduce-scatter.3.cloned.1.call-start = ((), (), s32[]{:S(2)}) async-start(), calls=%async_computation.3 | async-start | bytes 4128768 | tf_op jit(solution)/shard_map/reduce_scatter | solution.py:32
  335.5 0.7 copy-start.2
Sparse Core Ops, SparseCore 0:
  13.8 301.2 all-reduce.2
  325.0 119.5 reduce-scatter.4
  449.4 116.3 reduce-scatter.2
where the time goes:
time: 577 us; the launch traced here: 576 us
  waiting for transfers between devices  430 us (75%)
  blocking collectives  97.1 us (17%)
  matrix products  20.3 us (4%)
  between operations  14 us (2%)
  other arithmetic  12.9 us (2%)
    psum x1, waiting for transfers between devices, spread(): return lax.psum(block, axis)  230 us
    reduce_scatter x2, waiting for transfers between devices, layer_rows(): lax.psum_scatter(term.astype(jnp.bfloat16), 'tp', scatter_dimension=1, ti...  200 us
    psum x1, blocking collectives, spread(): return lax.psum(block, axis)  70.6 us
    psum x1, blocking collectives, shards(): lax.psum((jnp.sum(first_wide * first_wide, axis=1), jnp.sum(second_wide *...  26.5 us
    dot_general x2, matrix products, layer_rows(): partial_value = jnp.dot(scaled, weights, preferred_element_type=jnp.float32)  20.3 us
  transfers between devices with their start and end apart: 3, of which 3 were waited for; matrix products, arithmetic and copies ran while one was open for 2% of the time, Pallas kernels for 0%

commit v1 on v0

v1 whole, which is shorter than its diff:
```python
import functools

import jax
import jax.numpy as jnp
from jax import lax
from jax.experimental import pallas as pl
from jax.experimental.pallas import tpu as pltpu
from jax.sharding import PartitionSpec as P

HD = 128
LAYERS = 2
NY, NX, NZ = 4, 4, 4
MIB = 1 << 20


def chain_pairs(step):
    pairs = []
    for z in range(NZ):
        for y in range(NY):
            for c in range(2):
                to = step(z, y, c)
                if to is not None:
                    z2, y2, c2 = to
                    pairs.append(((z * NY + y) * 2 + c, (z2 * NY + y2 % NY) * 2 + c2))
    return pairs


def tp_pairs(step):
    pairs = []
    for h in range(2):
        for x in range(NX):
            h2, x2 = step(h, x)
            pairs.append((h * NX + x, (h2 % 2) * NX + x2 % NX))
    return pairs


X_NEXT = tp_pairs(lambda h, x: (h, x + 1))
X_LAST = tp_pairs(lambda h, x: (h, x - 1))
H_SWAP = tp_pairs(lambda h, x: (h + 1, x))
Z_FAR = chain_pairs(lambda z, y, c: (2, y, 0) if (z, c) == (0, 0) else None)
Z_NEAR = chain_pairs(lambda z, y, c: (z + 1, y, 0) if z in (0, 2) and c == 0 else None)
CORE = chain_pairs(lambda z, y, c: (z, y, 1) if c == 0 else None)
ROWS = [[z * NY * 2 + k for k in range(NY * 2)] for z in range(NZ)]


def scatter_pairs(k):
    return chain_pairs(lambda z, y, c: (0, k, 0) if (z, y, c) == (0, 0, 0) else None)


def spread(weights, gains):
    me = lax.axis_index("chain")
    z, y, c = me // (2 * NY), me // 2 % NY, me % 2
    depth = weights.shape[0] // NY

    def piece(k):
        rows = weights[k * depth:(k + 1) * depth].astype(jnp.float32)
        return (rows * gains[k * depth:(k + 1) * depth, None].astype(jnp.float32)).astype(jnp.bfloat16)

    got = {k: lax.ppermute(piece(k), "chain", scatter_pairs(k)) for k in (2, 1, 3)}
    first = jnp.where(y == 0, piece(0), jnp.where(y == 1, got[1], jnp.where(y == 2, got[2], got[3])))
    far = lax.ppermute(first, "chain", Z_FAR)
    second = jnp.where(z == 2, far, first)
    near = lax.ppermute(second, "chain", Z_NEAR)
    mine = jnp.where((z == 1) | (z == 3), near, second)
    other = lax.ppermute(mine[depth // 2:], "chain", CORE)
    half = jnp.where(c == 0, mine[:depth // 2], other)
    return lax.all_gather(half, "chain", axis_index_groups=ROWS, axis=0, tiled=True)


def product_kernel(flags, x_ref, g_ref, own_ref, src_ref, out_ref, scaled):
    @pl.when(pl.program_id(0) == 0)
    def _():
        gain = jnp.where(flags[0] > 0, g_ref[...].astype(jnp.float32), 1.0)
        scaled[...] = (x_ref[...].astype(jnp.float32) * gain).astype(jnp.bfloat16)

    @pl.when(flags[0] > 0)
    def _():
        out_ref[0] = jnp.dot(scaled[...], own_ref[...], preferred_element_type=jnp.float32).astype(jnp.bfloat16)

    @pl.when(flags[0] == 0)
    def _():
        out_ref[0] = jnp.dot(scaled[...], src_ref[...], preferred_element_type=jnp.float32).astype(jnp.bfloat16)


def product(flags, x, gain, own, layer, src, blocks):
    tokens, depth = x.shape
    wide = 2 * HD
    return pl.pallas_call(
        product_kernel,
        out_shape=jax.ShapeDtypeStruct((blocks, tokens, wide), jnp.bfloat16),
        grid_spec=pltpu.PrefetchScalarGridSpec(
            num_scalar_prefetch=1,
            grid=(blocks,),
            in_specs=[
                pl.BlockSpec((tokens, depth), lambda j, f: (0, 0)),
                pl.BlockSpec((1, depth), lambda j, f: (0, 0)),
                pl.BlockSpec((None, None, depth, wide), lambda j, f: (0, layer, 0, f[1 + j] * f[0])),
                pl.BlockSpec((depth, wide), lambda j, f: (0, f[1 + j] * (1 - f[0]))),
            ],
            out_specs=pl.BlockSpec((1, tokens, wide), lambda j, f: (j, 0, 0)),
            scratch_shapes=[pltpu.VMEM((tokens, depth), jnp.bfloat16)],
        ),
        compiler_params=pltpu.CompilerParams(vmem_limit_bytes=32 * MIB),
        cost_estimate=pl.CostEstimate(
            flops=2 * tokens * depth * wide * blocks,
            bytes_accessed=2 * (tokens * depth + blocks * wide * (depth + tokens)),
            transcendentals=0,
        ),
    )(flags, x, gain, own, src)


def add(*terms):
    return sum(t.astype(jnp.float32) for t in terms)


def reduce_x(first, second):
    low = jnp.bfloat16
    plus = lax.ppermute(first[0:2], "tp", X_NEXT)
    minus = lax.ppermute(first[2:4], "tp", X_LAST)
    plus2 = lax.ppermute(add(second[0], plus[0]).astype(low), "tp", X_NEXT)
    minus2 = lax.ppermute(add(second[1], minus[0]).astype(low), "tp", X_LAST)
    away = add(second[2], minus[1], plus2).astype(low)
    mine = add(second[3], plus[1], minus2)
    return mine, lax.ppermute(away, "tp", H_SWAP)


def block_order():
    me = lax.axis_index("tp")
    h, x = me // NX, me % NX
    mine, other = h * NX, (1 - h) * NX
    nxt, last, far = (x + 1) % NX, (x + 3) % NX, (x + 2) % NX
    first = [other + far, mine + nxt, mine + far, other + last]
    second = [other + nxt, mine + last, other + x, mine + x]
    return first, second


def shards(hidden_first, hidden_second, weight_buffer, gain_buffer, loaded_layers, positions):
    inputs = (hidden_first, hidden_second)
    width = hidden_first.shape[1] * lax.axis_size("tp")
    tokens = hidden_first.shape[0]
    squares = jnp.stack([jnp.sum(jnp.square(v.astype(jnp.float32)), axis=1) for v in inputs])
    for pairs in (tp_pairs(lambda h, x: (h, x ^ 1)), tp_pairs(lambda h, x: (h, x ^ 2)), H_SWAP):
        squares = squares + lax.ppermute(squares, "tp", pairs)
    scale = lax.rsqrt(squares / width + 1e-05)
    half = HD // 2
    freq = 500000.0 ** (-2.0 * jnp.arange(half, dtype=jnp.float32) / HD)
    angle = positions.astype(jnp.float32)[:, None] * freq[None, :]
    cosine, sine = jnp.cos(angle), jnp.sin(angle)
    orders = block_order()
    results = []
    for layer in range(LAYERS):
        src = spread(weight_buffer[0, layer], gain_buffer[0, layer])
        own = (loaded_layers[0] > layer).astype(jnp.int32)
        parts = [
            product(jnp.stack([own] + order).astype(jnp.int32), inputs[layer], gain_buffer[0, layer][None, :], weight_buffer, layer, src, len(order))
            for order in orders
        ]
        mine, came = reduce_x(*parts)
        mixed = add(mine, came) * scale[layer][:, None]
        a, e, v = mixed[:, :half], mixed[:, half:HD], mixed[:, HD:]
        results.append(jnp.concatenate([a * cosine - e * sine, e * cosine + a * sine, v], axis=1).astype(jnp.bfloat16))
    return jnp.stack(results, axis=0)


def solution(mesh):
    placed = (
        P("chain", "tp"),
        P("chain", "tp"),
        P("chain", None, "tp", None),
        P("chain", None, "tp"),
        P("chain"),
        P("chain"),
    )
    return jax.shard_map(
        shards, mesh=mesh, in_specs=placed, out_specs=P(None, "chain", "tp"), check_vma=False
    )
```

time: 577 us -> 280 us (0.49)
  waiting for transfers between devices: 430 us -> 160 us
  blocking collectives: 97.1 us -> 0 us
  starting transfers between devices: 0.09 us -> 54.7 us
  matrix products: 20.3 us -> 0 us
  Pallas kernels: 0 us -> 15.8 us
  local copies, waits for them, and re-layouts: 2.02 us -> 15.4 us
  other arithmetic: 12.9 us -> 19.4 us
    psum x1 -> x0, waiting for transfers between devices: 230 us -> none  [spread(): return lax.psum(block, axis)]
    reduce_scatter x2 -> x0, waiting for transfers between devices: 200 us -> none  [layer_rows(): lax.psum_scatter(term.astype(jnp.bfloat16), 'tp', scatter_dimension=1, ti...]
    ppermute x0 -> x25, waiting for transfers between devices: none -> 133 us  [the longest x6 33.5 us: spread(): lax.ppermute(piece(k), 'chain', scatter_pairs(k))]
    psum x2 -> x0, blocking collectives: 97.1 us -> none  [the longest x1 70.6 us: spread(): return lax.psum(block, axis)]
    ppermute x0 -> x25, starting transfers between devices: none -> 54.7 us  [the longest x6 16 us: spread(): lax.ppermute(piece(k), 'chain', scatter_pairs(k))]
    all_gather x0 -> x2, waiting for transfers between devices: none -> 26.5 us  [spread(): lax.all_gather(half, 'chain', axis_index_groups=ROWS, axis=0, tiled=True)]
    dot_general x2 -> x0, matrix products: 20.3 us -> none  [layer_rows(): partial_value = jnp.dot(scaled, weights, preferred_element_type=jnp.float32)]
    pallas_call x0 -> x4, Pallas kernels: none -> 15.8 us  [product(): pl.pallas_call(product_kernel, out_shape=jax.ShapeDtypeStruct((blocks, to...]
  transfers between devices with their start and end apart: 3 -> 27, of which waited for: 3 -> 17; matrix products, arithmetic and copies ran while one was open for 2% -> 3% of each run, Pallas kernels for 0% -> 6%
where the time goes in v1:
time: 280 us
  waiting for transfers between devices  160 us (57%)
  starting transfers between devices  54.7 us (20%)
  other arithmetic  19.4 us (7%)
  Pallas kernels  15.8 us (6%)
  local copies, waits for them, and re-layouts  15.4 us (6%)
  between operations  14.3 us (5%)
    ppermute x6, waiting for transfers between devices, spread(): lax.ppermute(piece(k), 'chain', scatter_pairs(k))  33.5 us
    ppermute x2, waiting for transfers between devices, reduce_x(): return (mine, lax.ppermute(away, 'tp', H_SWAP))  32.6 us
    all_gather x2, waiting for transfers between devices, spread(): lax.all_gather(half, 'chain', axis_index_groups=ROWS, axis=0, tiled=True)  26.5 us
    ppermute x2, waiting for transfers between devices, spread(): far = lax.ppermute(first, 'chain', Z_FAR)  23.6 us
    ppermute x2, waiting for transfers between devices, spread(): near = lax.ppermute(second, 'chain', Z_NEAR)  23.6 us
    ppermute x6, starting transfers between devices, spread(): lax.ppermute(piece(k), 'chain', scatter_pairs(k))  16 us
    pallas_call x4, Pallas kernels, product(): pl.pallas_call(product_kernel, out_shape=jax.ShapeDtypeStruct((blocks, to...  15.8 us
    unnamed x20, local copies, waits for them, and re-layouts  13.8 us
  transfers between devices with their start and end apart: 27, of which 17 were waited for; matrix products, arithmetic and copies ran while one was open for 3% of the time, Pallas kernels for 6%

profile of v1, /device:TPU:6, one launch (start us, length us, event | category | flops | bytes accessed | tf_op | source)
XLA Modules:
  0.0 279.7 jit_solution(7112724918546145744)
XLA Ops:
  6.5 0.8 slice_convert_fusion.9
  7.3 4.4 %fusion.4 = (bf16[256,2048]{1,0:T(8,128)(2,1)S(1)}, bf16[256,2048]{1,0:T(8,128)(2,1)S(1)}, bf16[256,2048]{1,0:T(8,128)(2,1)}, bf16[256,2048]{1,0:T(8,128)(2,1)},...) fusion(f32[256]{0:T(256)S(1)} %bitcast.87, bf16[1,2,1024,2048]{3,2,1,0:T(8,128)(2,1)} %own_ref.7, ...), kind=kLoop, calls=%fused_computation.11 | loop fusion | flops 9437184 | bytes 12589056 | tf_op jit(solution)/shard_map/convert_element_type | solution.py:57
  11.7 3.5 %collective-permute-start = (bf16[256,2048]{1,0:T(8,128)(2,1)S(1)}, bf16[256,2048]{1,0:T(8,128)(2,1)S(1)}, u32[]{:S(2)}, u32[]{:S(2)}) collective-permute-start(bf16[256,2048]{1,0:T(8,128)(2,1)S(1)} %get-tuple-element.14), channel_id=1, source_target_pairs={{0,16},{1,17},{2,18},{3,19},{4,20},{5,21},{6,22},{7,23}} | collective-permute-start | bytes 3145736 | tf_op jit(solution)/shard_map/ppermute | solution.py:59
  15.3 3.3 %collective-permute-start.1 = (bf16[256,2048]{1,0:T(8,128)(2,1)}, bf16[256,2048]{1,0:T(8,128)(2,1)}, u32[]{:S(2)}, u32[]{:S(2)}) collective-permute-start(bf16[256,2048]{1,0:T(8,128)(2,1)} %get-tuple-element.13), channel_id=1, source_target_pairs={{0,32},{1,33},{2,34},{3,35},{4,36},{5,37},{6,38},{7,39}} | collective-permute-start | bytes 3145736 | tf_op jit(solution)/shard_map/ppermute | solution.py:59
  18.6 2.3 collective-permute-start.14
  20.9 2.2 collective-permute-start.15
  23.1 2.4 collective-permute-start.16
  25.5 2.0 collective-permute-done
  27.5 2.3 collective-permute-start.2
  29.8 9.0 %collective-permute-done.1 = bf16[256,2048]{1,0:T(8,128)(2,1)} collective-permute-done((bf16[256,2048]{1,0:T(8,128)(2,1)}, bf16[256,2048]{1,0:T(8,128)(2,1)}, u32[]{:S(2)}, u32[]{:S(2)}) %collective-permute-start.1) | collective-permute-done | bytes 1048608 | tf_op jit(solution)/shard_map/ppermute | solution.py:59
  38.9 11.2 %collective-permute-done.14 = bf16[256,2048]{1,0:T(8,128)(2,1)} collective-permute-done((bf16[256,2048]{1,0:T(8,128)(2,1)}, bf16[256,2048]{1,0:T(8,128)(2,1)}, u32[]{:S(2)}, u32[]{:S(2)}) %collective-permute-start.14) | collective-permute-done | bytes 1048608 | tf_op jit(solution)/shard_map/ppermute | solution.py:59
  50.1 11.2 %collective-permute-done.15 = bf16[256,2048]{1,0:T(8,128)(2,1)} collective-permute-done((bf16[256,2048]{1,0:T(8,128)(2,1)}, bf16[256,2048]{1,0:T(8,128)(2,1)}, u32[]{:S(2)}, u32[]{:S(2)}) %collective-permute-start.15) | collective-permute-done | bytes 1048608 | tf_op jit(solution)/shard_map/ppermute | solution.py:59
  61.3 2.9 %fusion.8 = (bf16[256,2048]{1,0:T(8,128)(2,1)S(1)}, bf16[256,2048]{1,0:T(8,128)(2,1)S(1)}) fusion(bf16[256,2048]{1,0:T(8,128)(2,1)S(1)} %collective-permute-done, bf16[256,2048]{1,0:T(8,128)(2,1)} %collective-permute-done.1, bf16[256,2048]{1,0:T(8,128)(2,1)} %collective-permute-done.2, f32[256]{0:T(256)S(1)} %bitcast.84, ...), kind=kLoop, calls=%fused_computation.18 | loop fusion | flops 6291456 | bytes 10487811 | tf_op jit(solution)/shard_map/jit(_where)/select_n | solution.py:60
  64.2 2.3 collective-permute-start.3
  66.5 11.3 %collective-permute-done.3 = bf16[256,2048]{1,0:T(8,128)(2,1)} collective-permute-done((bf16[256,2048]{1,0:T(8,128)(2,1)S(1)}, bf16[256,2048]{1,0:T(8,128)(2,1)}, u32[]{:S(2)}, u32[]{:S(2)}) %collective-permute-start.3) | collective-permute-done | bytes 1048608 | tf_op jit(solution)/shard_map/ppermute | solution.py:61
  77.9 2.3 collective-permute-start.4
  80.2 11.3 %collective-permute-done.4 = bf16[256,2048]{1,0:T(8,128)(2,1)} collective-permute-done((bf16[256,2048]{1,0:T(8,128)(2,1)S(1)}, bf16[256,2048]{1,0:T(8,128)(2,1)}, u32[]{:S(2)}, u32[]{:S(2)}) %collective-permute-start.4) | collective-permute-done | bytes 1048608 | tf_op jit(solution)/shard_map/ppermute | solution.py:63
  91.7 1.3 collective-permute-start.5
  93.0 1.5 collective-permute-done.5
  94.5 0.8 slice_select_fusion.1
  95.4 6.7 %collective-permute-start.17 = (bf16[256,2048]{1,0:T(8,128)(2,1)S(1)}, bf16[256,2048]{1,0:T(8,128)(2,1)S(1)}, u32[]{:S(2)}, u32[]{:S(2)}) collective-permute-start(bf16[256,2048]{1,0:T(8,128)(2,1)S(1)} %get-tuple-element.8), channel_id=1, source_target_pairs={{0,128},{16,144},{32,160},{48,176},{1,129},{17,145},{33,161},{49,1... | collective-permute-start | bytes 3145736 | tf_op jit(solution)/shard_map/ppermute | solution.py:61
  102.1 12.2 %collective-permute-done.17 = bf16[256,2048]{1,0:T(8,128)(2,1)S(1)} collective-permute-done((bf16[256,2048]{1,0:T(8,128)(2,1)S(1)}, bf16[256,2048]{1,0:T(8,128)(2,1)S(1)}, u32[]{:S(2)}, u32[]{:S(2)}) %collective-permute-start.17) | collective-permute-done | bytes 1048608 | tf_op jit(solution)/shard_map/ppermute | solution.py:61
  114.5 1.4 collective-permute-start.18
  115.8 12.2 %collective-permute-done.18 = bf16[256,2048]{1,0:T(8,128)(2,1)S(1)} collective-permute-done((bf16[256,2048]{1,0:T(8,128)(2,1)S(1)}, bf16[256,2048]{1,0:T(8,128)(2,1)S(1)}, u32[]{:S(2)}, u32[]{:S(2)}) %collective-permute-start.18) | collective-permute-done | bytes 1048608 | tf_op jit(solution)/shard_map/ppermute | solution.py:63
  128.3 1.5 collective-permute-start.19
  129.7 1.5 collective-permute-done.19
  131.2 0.9 slice_select_fusion
  132.1 0.4 multiply_reduce_fusion.1
  132.6 1.1 copy-done.6
  133.6 0.4 multiply_reduce_fusion
  134.1 0.9 collective-permute-start.11
  135.8 2.9 %all-gather.3.cloned.1.call-done.src_ref = bf16[1024,2048]{1,0:T(8,128)(2,1)} async-done(((bf16[128,2048]{1,0:T(8,128)(2,1)}), bf16[1024,2048]{1,0:T(8,128)(2,1)}) %all-gather.3.cloned.1.call-update) | async-done | bytes 4194320 | tf_op jit(solution)/shard_map/all_gather | solution.py:67
  138.6 3.4 %copy-done = bf16[1,2,1024,2048]{3,2,1,0:T(8,128)(2,1)S(1)} copy-done((bf16[1,2,1024,2048]{3,2,1,0:T(8,128)(2,1)S(1)}, bf16[1,2,1024,2048]{3,2,1,0:T(8,128)(2,1)}, u32[]{:S(2)}) %copy-start) | copy-done | bytes 8388632
  142.0 2.2 copy-done.2
  144.2 4.0 %shard_map.65 = bf16[4,896,256]{2,1,0:T(8,128)(2,1)S(1)} custom-call(s32[5]{0:T(128)S(1)} %stack.71.flags, bf16[896,1024]{1,0:T(8,128)(2,1)S(1)} %copy-done.5, bf16[1,1024]{1,0:T(2,128)(2,1)S(1)} %get-tuple-element.37.g_ref, bf16[1,2,1024,2048]{3,2,1,0:T(8,128)(2,1)S(1)} %copy-done, bf16[1024,2048]{1,0:T(8,128)(2,1)S(1)} %copy-done.2), custom_call_target="tpu_custom_call" | custom-call | flops 1879048192 | bytes 5767168 | tf_op jit(solution)/shard_map/pallas_call | solution.py:88
  148.2 1.0 fusion.43
  149.2 0.5 collective-permute-start.6
  149.8 1.5 collective-permute-start.7
  151.5 23.7 %all-gather.5.cloned.1.call-done.src_ref = bf16[1024,2048]{1,0:T(8,128)(2,1)} async-done(((bf16[128,2048]{1,0:T(8,128)(2,1)}), bf16[1024,2048]{1,0:T(8,128)(2,1)}) %all-gather.5.cloned.1.call-update) | async-done | bytes 4194320 | tf_op jit(solution)/shard_map/all_gather | solution.py:67
  175.2 3.4 %copy-done.1 = bf16[1,2,1024,2048]{3,2,1,0:T(8,128)(2,1)S(1)} copy-done((bf16[1,2,1024,2048]{3,2,1,0:T(8,128)(2,1)S(1)}, bf16[1,2,1024,2048]{3,2,1,0:T(8,128)(2,1)}, u32[]{:S(2)}) %copy-start.1) | copy-done | bytes 8388632
  178.6 2.2 copy-done.4
  180.8 1.5 copy-done.7
  182.3 4.0 %shard_map.67 = bf16[4,896,256]{2,1,0:T(8,128)(2,1)S(1)} custom-call(s32[5]{0:T(128)S(1)} %stack.76.flags, bf16[896,1024]{1,0:T(8,128)(2,1)S(1)} %copy-done.7, bf16[1,1024]{1,0:T(2,128)(2,1)S(1)} %get-tuple-element.38.g_ref, bf16[1,2,1024,2048]{3,2,1,0:T(8,128)(2,1)S(1)} %copy-done.1, bf16[1024,2048]{1,0:T(8,128)(2,1)S(1)} %copy-done.4), custom_call_target="tpu_custom_call" | custom-call | flops 1879048192 | bytes 5767168 | tf_op jit(solution)/shard_map/pallas_call | solution.py:88
  186.4 0.6 collective-permute-start.20
  187.0 1.5 collective-permute-start.21
  188.5 1.7 collective-permute-start.12
  190.2 4.0 %shard_map.64 = bf16[4,896,256]{2,1,0:T(8,128)(2,1)S(1)} custom-call(s32[5]{0:T(128)S(1)} %stack.66.flags, bf16[896,1024]{1,0:T(8,128)(2,1)S(1)} %copy-done.5, bf16[1,1024]{1,0:T(2,128)(2,1)S(1)} %get-tuple-element.37.g_ref, bf16[1,2,1024,2048]{3,2,1,0:T(8,128)(2,1)S(1)} %copy-done.1, bf16[1024,2048]{1,0:T(8,128)(2,1)S(1)} %copy-done.3), custom_call_target="tpu_custom_call" | custom-call | flops 1879048192 | bytes 5767168 | tf_op jit(solution)/shard_map/pallas_call | solution.py:88
  194.2 1.4 fusion.32
  195.6 2.2 collective-permute-start.9
  197.8 12.6 %collective-permute-done.12 = f32[2,896]{1,0:T(2,128)S(1)} collective-permute-done((f32[2,896]{1,0:T(2,128)S(1)}, f32[2,896]{1,0:T(2,128)S(1)}, u32[]{:S(2)}, u32[]{:S(2)}) %collective-permute-start.12) | collective-permute-done | bytes 7200 | tf_op jit(solution)/shard_map/ppermute | solution.py:143
  210.4 5.8 %collective-permute-start.13 = (f32[2,896]{1,0:T(2,128)S(1)}, f32[2,896]{1,0:T(2,128)S(1)}, u32[]{:S(2)}, u32[]{:S(2)}) collective-permute-start(f32[2,896]{1,0:T(2,128)S(1)} %fusion.45), channel_id=1, source_target_pairs={{0,4},{1,5},{2,6},{3,7},{4,0},{5,1},{6,2},{7,3},{8,12},{9,13},{10,... | collective-permute-start | bytes 21512 | tf_op jit(solution)/shard_map/ppermute | solution.py:143
  216.2 4.0 %shard_map.66 = bf16[4,896,256]{2,1,0:T(8,128)(2,1)S(1)} custom-call(s32[5]{0:T(128)S(1)} %stack.75.flags, bf16[896,1024]{1,0:T(8,128)(2,1)S(1)} %copy-done.7, bf16[1,1024]{1,0:T(2,128)(2,1)S(1)} %get-tuple-element.38.g_ref, bf16[1,2,1024,2048]{3,2,1,0:T(8,128)(2,1)S(1)} %copy-done.1, bf16[1024,2048]{1,0:T(8,128)(2,1)S(1)} %copy-done.4), custom_call_target="tpu_custom_call" | custom-call | flops 1879048192 | bytes 5767168 | tf_op jit(solution)/shard_map/pallas_call | solution.py:88
  220.2 0.3 collective-permute-start.8
  220.8 3.1 %collective-permute-start.23 = (bf16[896,256]{1,0:T(8,128)(2,1)S(1)}, bf16[896,256]{1,0:T(8,128)(2,1)S(1)}, u32[]{:S(2)}, u32[]{:S(2)}) collective-permute-start(bf16[896,256]{1,0:T(8,128)(2,1)S(1)} %get-tuple-element.20), channel_id=1, source_target_pairs={{0,1},{1,2},{2,3},{3,0},{4,5},{5,6},{6,7},{7,4},{8,9},{9,10},{10,1... | collective-permute-start | bytes 1376264 | tf_op jit(solution)/shard_map/ppermute | solution.py:120
  223.8 1.2 fusion.13
  225.0 1.6 collective-permute-start.10
  226.7 0.9 collective-permute-start.22
  227.6 4.3 %collective-permute-done.23 = bf16[896,256]{1,0:T(8,128)(2,1)S(1)} collective-permute-done((bf16[896,256]{1,0:T(8,128)(2,1)S(1)}, bf16[896,256]{1,0:T(8,128)(2,1)S(1)}, u32[]{:S(2)}, u32[]{:S(2)}) %collective-permute-start.23) | collective-permute-done | bytes 458784 | tf_op jit(solution)/shard_map/ppermute | solution.py:120
  232.1 2.7 collective-permute-start.24
  234.9 25.6 %collective-permute-done.10 = bf16[896,256]{1,0:T(8,128)(2,1)S(1)} collective-permute-done((bf16[896,256]{1,0:T(8,128)(2,1)S(1)}, bf16[896,256]{1,0:T(8,128)(2,1)S(1)}, u32[]{:S(2)}, u32[]{:S(2)}) %collective-permute-start.10) | collective-permute-done | bytes 458784 | tf_op jit(solution)/shard_map/ppermute | solution.py:124
  260.5 1.3 fusion.15
  261.8 7.1 %collective-permute-done.24 = bf16[896,256]{1,0:T(8,128)(2,1)S(1)} collective-permute-done((bf16[896,256]{1,0:T(8,128)(2,1)S(1)}, bf16[896,256]{1,0:T(8,128)(2,1)S(1)}, u32[]{:S(2)}, u32[]{:S(2)}) %collective-permute-start.24) | collective-permute-done | bytes 458784 | tf_op jit(solution)/shard_map/ppermute | solution.py:124
  269.2 2.3 fusion.41
  271.5 1.3 maximum_maximum_fusion
  (55 shorter events, 2.1 us)
Async XLA Ops:
  6.5 132.1 %all-gather.3.cloned.1.call-start = ((), (), s32[]{:S(2)}) async-start(), calls=%async_computation | async-start | bytes 4718592 | tf_op jit(solution)/shard_map/all_gather | solution.py:67
  11.7 15.8 %collective-permute-start = (bf16[256,2048]{1,0:T(8,128)(2,1)S(1)}, bf16[256,2048]{1,0:T(8,128)(2,1)S(1)}, u32[]{:S(2)}, u32[]{:S(2)}) collective-permute-start(bf16[256,2048]{1,0:T(8,128)(2,1)S(1)} %get-tuple-element.14), channel_id=1, source_target_pairs={{0,16},{1,17},{2,18},{3,19},{4,20},{5,21},{6,22},{7,23}} | collective-permute-start | bytes 3145736 | tf_op jit(solution)/shard_map/ppermute | solution.py:59
  15.3 23.6 %collective-permute-start.1 = (bf16[256,2048]{1,0:T(8,128)(2,1)}, bf16[256,2048]{1,0:T(8,128)(2,1)}, u32[]{:S(2)}, u32[]{:S(2)}) collective-permute-start(bf16[256,2048]{1,0:T(8,128)(2,1)} %get-tuple-element.13), channel_id=1, source_target_pairs={{0,32},{1,33},{2,34},{3,35},{4,36},{5,37},{6,38},{7,39}} | collective-permute-start | bytes 3145736 | tf_op jit(solution)/shard_map/ppermute | solution.py:59
  18.6 31.5 %collective-permute-start.14 = (bf16[256,2048]{1,0:T(8,128)(2,1)}, bf16[256,2048]{1,0:T(8,128)(2,1)}, u32[]{:S(2)}, u32[]{:S(2)}) collective-permute-start(bf16[256,2048]{1,0:T(8,128)(2,1)} %get-tuple-element.12), channel_id=1, source_target_pairs={{0,16},{1,17},{2,18},{3,19},{4,20},{5,21},{6,22},{7,23}} | collective-permute-start | bytes 3145736 | tf_op jit(solution)/shard_map/ppermute | solution.py:59
  20.9 40.5 %collective-permute-start.15 = (bf16[256,2048]{1,0:T(8,128)(2,1)}, bf16[256,2048]{1,0:T(8,128)(2,1)}, u32[]{:S(2)}, u32[]{:S(2)}) collective-permute-start(bf16[256,2048]{1,0:T(8,128)(2,1)} %get-tuple-element.11), channel_id=1, source_target_pairs={{0,32},{1,33},{2,34},{3,35},{4,36},{5,37},{6,38},{7,39}} | collective-permute-start | bytes 3145736 | tf_op jit(solution)/shard_map/ppermute | solution.py:59
  23.1 38.2 %collective-permute-start.16 = (bf16[256,2048]{1,0:T(8,128)(2,1)S(1)}, bf16[256,2048]{1,0:T(8,128)(2,1)}, u32[]{:S(2)}, u32[]{:S(2)}) collective-permute-start(bf16[256,2048]{1,0:T(8,128)(2,1)S(1)} %get-tuple-element.10), channel_id=1, source_target_pairs={{0,48},{1,49},{2,50},{3,51},{4,52},{5,53},{6,54},{7,55}} | collective-permute-start | bytes 3145736 | tf_op jit(solution)/shard_map/ppermute | solution.py:59
  27.5 33.8 %collective-permute-start.2 = (bf16[256,2048]{1,0:T(8,128)(2,1)S(1)}, bf16[256,2048]{1,0:T(8,128)(2,1)}, u32[]{:S(2)}, u32[]{:S(2)}) collective-permute-start(bf16[256,2048]{1,0:T(8,128)(2,1)S(1)} %get-tuple-element.9), channel_id=1, source_target_pairs={{0,48},{1,49},{2,50},{3,51},{4,52},{5,53},{6,54},{7,55}} | collective-permute-start | bytes 3145736 | tf_op jit(solution)/shard_map/ppermute | solution.py:59
  64.2 13.6 %collective-permute-start.3 = (bf16[256,2048]{1,0:T(8,128)(2,1)S(1)}, bf16[256,2048]{1,0:T(8,128)(2,1)}, u32[]{:S(2)}, u32[]{:S(2)}) collective-permute-start(bf16[256,2048]{1,0:T(8,128)(2,1)S(1)} %get-tuple-element.7), channel_id=1, source_target_pairs={{0,128},{16,144},{32,160},{48,176},{1,129},{17,145},{33,161},{49,1... | collective-permute-start | bytes 3145736 | tf_op jit(solution)/shard_map/ppermute | solution.py:61
  77.9 13.6 %collective-permute-start.4 = (bf16[256,2048]{1,0:T(8,128)(2,1)S(1)}, bf16[256,2048]{1,0:T(8,128)(2,1)}, u32[]{:S(2)}, u32[]{:S(2)}) collective-permute-start(bf16[256,2048]{1,0:T(8,128)(2,1)S(1)} %broadcast_select_fusion.1), channel_id=1, source_target_pairs={{0,64},{16,80},{32,96},{48,112},{128,192},{144,208},{160,224},{176... | collective-permute-start | bytes 3145736 | tf_op jit(solution)/shard_map/ppermute | solution.py:63
  91.7 2.8 %collective-permute-start.5 = (bf16[128,2048]{1,0:T(8,128)(2,1)S(1)}, bf16[128,2048]{1,0:T(8,128)(2,1)S(1)}, u32[]{:S(2)}, u32[]{:S(2)}) collective-permute-start(bf16[128,2048]{1,0:T(8,128)(2,1)S(1)} %slice.241), channel_id=1, source_target_pairs={{0,8},{16,24},{32,40},{48,56},{64,72},{80,88},{96,104},{112,120},{... | collective-permute-start | bytes 1572872 | tf_op jit(solution)/shard_map/ppermute | solution.py:65
  95.4 79.8 %all-gather.5.cloned.1.call-start = ((), (), s32[]{:S(2)}) async-start(), calls=%async_computation.1 | async-start | bytes 4718592 | tf_op jit(solution)/shard_map/all_gather | solution.py:67
  95.4 18.9 %collective-permute-start.17 = (bf16[256,2048]{1,0:T(8,128)(2,1)S(1)}, bf16[256,2048]{1,0:T(8,128)(2,1)S(1)}, u32[]{:S(2)}, u32[]{:S(2)}) collective-permute-start(bf16[256,2048]{1,0:T(8,128)(2,1)S(1)} %get-tuple-element.8), channel_id=1, source_target_pairs={{0,128},{16,144},{32,160},{48,176},{1,129},{17,145},{33,161},{49,1... | collective-permute-start | bytes 3145736 | tf_op jit(solution)/shard_map/ppermute | solution.py:61
  114.5 13.6 %collective-permute-start.18 = (bf16[256,2048]{1,0:T(8,128)(2,1)S(1)}, bf16[256,2048]{1,0:T(8,128)(2,1)S(1)}, u32[]{:S(2)}, u32[]{:S(2)}) collective-permute-start(bf16[256,2048]{1,0:T(8,128)(2,1)S(1)} %broadcast_select_fusion), channel_id=1, source_target_pairs={{0,64},{16,80},{32,96},{48,112},{128,192},{144,208},{160,224},{176... | collective-permute-start | bytes 3145736 | tf_op jit(solution)/shard_map/ppermute | solution.py:63
  128.2 3.9 %copy-start.5 = (bf16[896,1024]{1,0:T(8,128)(2,1)S(1)}, bf16[896,1024]{1,0:T(8,128)(2,1)}, u32[]{:S(2)}) copy-start(bf16[896,1024]{1,0:T(8,128)(2,1)} %x_ref.5) | copy-start | bytes 5505028
  128.3 2.9 %collective-permute-start.19 = (bf16[128,2048]{1,0:T(8,128)(2,1)S(1)}, bf16[128,2048]{1,0:T(8,128)(2,1)S(1)}, u32[]{:S(2)}, u32[]{:S(2)}) collective-permute-start(bf16[128,2048]{1,0:T(8,128)(2,1)S(1)} %slice.257), channel_id=1, source_target_pairs={{0,8},{16,24},{32,40},{48,56},{64,72},{80,88},{96,104},{112,120},{... | collective-permute-start | bytes 1572872 | tf_op jit(solution)/shard_map/ppermute | solution.py:65
  132.1 3.7 %copy-start.8 = (bf16[1,2,1024]{2,1,0:T(2,128)(2,1)S(1)}, bf16[1,2,1024]{2,1,0:T(2,128)(2,1)}, u32[]{:S(2)}) copy-start(bf16[1,2,1024]{2,1,0:T(2,128)(2,1)} %param.9) | copy-start | bytes 12292
  132.1 1.5 copy-start.6
  134.1 54.4 %collective-permute-start.11 = (f32[2,896]{1,0:T(2,128)S(1)}, f32[2,896]{1,0:T(2,128)S(1)}, u32[]{:S(2)}, u32[]{:S(2)}) collective-permute-start(f32[2,896]{1,0:T(2,128)S(1)} %pad_maximum_fusion), channel_id=1, source_target_pairs={{0,1},{1,0},{2,3},{3,2},{4,5},{5,4},{6,7},{7,6},{8,9},{9,8},{10,11... | collective-permute-start | bytes 21512 | tf_op jit(solution)/shard_map/ppermute | solution.py:143
  138.6 3.4 %copy-start = (bf16[1,2,1024,2048]{3,2,1,0:T(8,128)(2,1)S(1)}, bf16[1,2,1024,2048]{3,2,1,0:T(8,128)(2,1)}, u32[]{:S(2)}) copy-start(bf16[1,2,1024,2048]{3,2,1,0:T(8,128)(2,1)} %own_ref.7) | copy-start | bytes 25165828
  142.0 2.2 copy-start.2
  148.2 3.3 %copy-start.9 = (s32[896]{0:T(1024)S(1)}, s32[896]{0:T(1024)}, u32[]{:S(2)}) copy-start(s32[896]{0:T(1024)} %param.11) | copy-start | bytes 10756
  149.2 44.9 %collective-permute-start.6 = (bf16[2,896,256]{2,1,0:T(8,128)(2,1)}, bf16[2,896,256]{2,1,0:T(8,128)(2,1)}, u32[]{:S(2)}, u32[]{:S(2)}) collective-permute-start(bf16[2,896,256]{2,1,0:T(8,128)(2,1)} %get-tuple-element.18), channel_id=1, source_target_pairs={{0,1},{1,2},{2,3},{3,0},{4,5},{5,6},{6,7},{7,4},{8,9},{9,10},{10,1... | collective-permute-start | bytes 2752520 | tf_op jit(solution)/shard_map/ppermute | solution.py:118
  149.8 44.4 %collective-permute-start.7 = (bf16[2,896,256]{2,1,0:T(8,128)(2,1)S(1)}, bf16[2,896,256]{2,1,0:T(8,128)(2,1)}, u32[]{:S(2)}, u32[]{:S(2)}) collective-permute-start(bf16[2,896,256]{2,1,0:T(8,128)(2,1)S(1)} %get-tuple-element.17), channel_id=1, source_target_pairs={{0,3},{1,0},{2,1},{3,2},{4,7},{5,4},{6,5},{7,6},{8,11},{9,8},{10,9... | collective-permute-start | bytes 2752520 | tf_op jit(solution)/shard_map/ppermute | solution.py:119
  175.2 3.4 %copy-start.1 = (bf16[1,2,1024,2048]{3,2,1,0:T(8,128)(2,1)S(1)}, bf16[1,2,1024,2048]{3,2,1,0:T(8,128)(2,1)}, u32[]{:S(2)}) copy-start(bf16[1,2,1024,2048]{3,2,1,0:T(8,128)(2,1)} %own_ref.7) | copy-start | bytes 25165828
  178.6 2.2 copy-start.4
  180.8 1.5 copy-start.7
  182.3 7.9 %copy-start.3 = (bf16[1024,2048]{1,0:T(8,128)(2,1)S(1)}, bf16[1024,2048]{1,0:T(8,128)(2,1)}, u32[]{:S(2)}) copy-start(bf16[1024,2048]{1,0:T(8,128)(2,1)} %all-gather.3.cloned.1.call-done.src_ref) | copy-start | bytes 12582916
  186.4 34.1 %collective-permute-start.20 = (bf16[2,896,256]{2,1,0:T(8,128)(2,1)S(1)}, bf16[2,896,256]{2,1,0:T(8,128)(2,1)S(1)}, u32[]{:S(2)}, u32[]{:S(2)}) collective-permute-start(bf16[2,896,256]{2,1,0:T(8,128)(2,1)S(1)} %get-tuple-element.22), channel_id=1, source_target_pairs={{0,1},{1,2},{2,3},{3,0},{4,5},{5,6},{6,7},{7,4},{8,9},{9,10},{10,1... | collective-permute-start | bytes 2752520 | tf_op jit(solution)/shard_map/ppermute | solution.py:118
  187.0 33.5 %collective-permute-start.21 = (bf16[2,896,256]{2,1,0:T(8,128)(2,1)S(1)}, bf16[2,896,256]{2,1,0:T(8,128)(2,1)S(1)}, u32[]{:S(2)}, u32[]{:S(2)}) collective-permute-start(bf16[2,896,256]{2,1,0:T(8,128)(2,1)S(1)} %get-tuple-element.21), channel_id=1, source_target_pairs={{0,3},{1,0},{2,1},{3,2},{4,7},{5,4},{6,5},{7,6},{8,11},{9,8},{10,9... | collective-permute-start | bytes 2752520 | tf_op jit(solution)/shard_map/ppermute | solution.py:119
  188.5 21.9 %collective-permute-start.12 = (f32[2,896]{1,0:T(2,128)S(1)}, f32[2,896]{1,0:T(2,128)S(1)}, u32[]{:S(2)}, u32[]{:S(2)}) collective-permute-start(f32[2,896]{1,0:T(2,128)S(1)} %fusion.42), channel_id=1, source_target_pairs={{0,2},{1,3},{2,0},{3,1},{4,6},{5,7},{6,4},{7,5},{8,10},{9,11},{10,... | collective-permute-start | bytes 21512 | tf_op jit(solution)/shard_map/ppermute | solution.py:143
  195.6 28.2 %collective-permute-start.9 = (bf16[896,256]{1,0:T(8,128)(2,1)S(1)}, bf16[896,256]{1,0:T(8,128)(2,1)S(1)}, u32[]{:S(2)}, u32[]{:S(2)}) collective-permute-start(bf16[896,256]{1,0:T(8,128)(2,1)S(1)} %get-tuple-element.16), channel_id=1, source_target_pairs={{0,1},{1,2},{2,3},{3,0},{4,5},{5,6},{6,7},{7,4},{8,9},{9,10},{10,1... | collective-permute-start | bytes 1376264 | tf_op jit(solution)/shard_map/ppermute | solution.py:120
  210.4 16.3 %collective-permute-start.13 = (f32[2,896]{1,0:T(2,128)S(1)}, f32[2,896]{1,0:T(2,128)S(1)}, u32[]{:S(2)}, u32[]{:S(2)}) collective-permute-start(f32[2,896]{1,0:T(2,128)S(1)} %fusion.45), channel_id=1, source_target_pairs={{0,4},{1,5},{2,6},{3,7},{4,0},{5,1},{6,2},{7,3},{8,12},{9,13},{10,... | collective-permute-start | bytes 21512 | tf_op jit(solution)/shard_map/ppermute | solution.py:143
  220.2 14.7 %collective-permute-start.8 = (bf16[896,256]{1,0:T(8,128)(2,1)S(1)}, bf16[896,256]{1,0:T(8,128)(2,1)S(1)}, u32[]{:S(2)}, u32[]{:S(2)}) collective-permute-start(bf16[896,256]{1,0:T(8,128)(2,1)S(1)} %get-tuple-element.15), channel_id=1, source_target_pairs={{0,3},{1,0},{2,1},{3,2},{4,7},{5,4},{6,5},{7,6},{8,11},{9,8},{10,9... | collective-permute-start | bytes 1376264 | tf_op jit(solution)/shard_map/ppermute | solution.py:121
  220.8 11.2 %collective-permute-start.23 = (bf16[896,256]{1,0:T(8,128)(2,1)S(1)}, bf16[896,256]{1,0:T(8,128)(2,1)S(1)}, u32[]{:S(2)}, u32[]{:S(2)}) collective-permute-start(bf16[896,256]{1,0:T(8,128)(2,1)S(1)} %get-tuple-element.20), channel_id=1, source_target_pairs={{0,1},{1,2},{2,3},{3,0},{4,5},{5,6},{6,7},{7,4},{8,9},{9,10},{10,1... | collective-permute-start | bytes 1376264 | tf_op jit(solution)/shard_map/ppermute | solution.py:120
  225.0 35.4 %collective-permute-start.10 = (bf16[896,256]{1,0:T(8,128)(2,1)S(1)}, bf16[896,256]{1,0:T(8,128)(2,1)S(1)}, u32[]{:S(2)}, u32[]{:S(2)}) collective-permute-start(bf16[896,256]{1,0:T(8,128)(2,1)S(1)} %fusion.13), channel_id=1, source_target_pairs={{0,4},{1,5},{2,6},{3,7},{4,0},{5,1},{6,2},{7,3},{8,12},{9,13},{10,... | collective-permute-start | bytes 1376264 | tf_op jit(solution)/shard_map/ppermute | solution.py:124
  226.7 35.1 %collective-permute-start.22 = (bf16[896,256]{1,0:T(8,128)(2,1)S(1)}, bf16[896,256]{1,0:T(8,128)(2,1)S(1)}, u32[]{:S(2)}, u32[]{:S(2)}) collective-permute-start(bf16[896,256]{1,0:T(8,128)(2,1)S(1)} %get-tuple-element.19), channel_id=1, source_target_pairs={{0,3},{1,0},{2,1},{3,2},{4,7},{5,4},{6,5},{7,6},{8,11},{9,8},{10,9... | collective-permute-start | bytes 1376264 | tf_op jit(solution)/shard_map/ppermute | solution.py:121
  232.1 36.7 %collective-permute-start.24 = (bf16[896,256]{1,0:T(8,128)(2,1)S(1)}, bf16[896,256]{1,0:T(8,128)(2,1)S(1)}, u32[]{:S(2)}, u32[]{:S(2)}) collective-permute-start(bf16[896,256]{1,0:T(8,128)(2,1)S(1)} %fusion.10), channel_id=1, source_target_pairs={{0,4},{1,5},{2,6},{3,7},{4,0},{5,1},{6,2},{7,3},{8,12},{9,13},{10,... | collective-permute-start | bytes 1376264 | tf_op jit(solution)/shard_map/ppermute | solution.py:124
Sparse Core Ops, SparseCore 0:
  95.5 43.0 all-gather.2
  140.5 34.6 all-gather.4

commit v2 on v1

v2 whole, which is shorter than its diff:
```python
import jax
import jax.numpy as jnp
from jax import lax
from jax.experimental import pallas as pl
from jax.experimental.pallas import tpu as pltpu
from jax.sharding import PartitionSpec as P

HD = 128
WIDE = 2 * HD
LAYERS = 2
NY, NX, NZ = 4, 4, 4
VMEM = 56 << 20
TILES = 4
LOW = jnp.bfloat16


def flat(z, y, c, h, x):
    return ((z * NY + y % NY) * 2 + c) * 2 * NX + h * NX + x % NX


def tp_pairs(step):
    pairs = []
    for h in range(2):
        for x in range(NX):
            h2, x2 = step(h, x)
            pairs.append((h * NX + x, (h2 % 2) * NX + x2 % NX))
    return pairs


def chain_pairs(step):
    pairs = []
    for z in range(NZ):
        for y in range(NY):
            for c in range(2):
                to = step(z, y, c)
                if to is not None:
                    z2, y2, c2 = to
                    pairs.append(((z * NY + y) * 2 + c, (z2 * NY + y2 % NY) * 2 + c2))
    return pairs


X_NEXT = tp_pairs(lambda h, x: (h, x + 1))
X_LAST = tp_pairs(lambda h, x: (h, x - 1))
H_SWAP = tp_pairs(lambda h, x: (h + 1, x))
Z_FAR = chain_pairs(lambda z, y, c: (2, y, 0) if (z, c) == (0, 0) else None)
Z_NEAR = chain_pairs(lambda z, y, c: (z + 1, y, 0) if z in (0, 2) and c == 0 else None)
CORE = chain_pairs(lambda z, y, c: (z, y, 1) if c == 0 else None)
ROWS = [[z * NY * 2 + k for k in range(NY * 2)] for z in range(NZ)]


def diagonal(d):
    return [(flat(0, 0, 0, h, x), flat(0, d, 0, h, x - d)) for h in range(2) for x in range(NX)]


def after(value, *earlier):
    return lax.optimization_barrier((value, earlier))[0]


def place():
    tp, chain = lax.axis_index("tp"), lax.axis_index("chain")
    return tp // NX, tp % NX, chain // (2 * NY), chain // 2 % NY, chain % 2


def pieces(weights, gains, layers, head_row):
    x = lax.axis_index("tp") % NX
    out = []
    for d in range(NX):
        column = (head_row * NX + (x - d) % NX) * WIDE
        parts = []
        for layer in layers:
            block = lax.dynamic_slice_in_dim(weights[0, layer], column, WIDE, 1).astype(jnp.float32)
            parts.append((block * gains[0, layer][:, None].astype(jnp.float32)).astype(LOW))
        out.append(jnp.stack(parts))
    return out


def scatter(parts):
    _, _, _, y, _ = place()
    got = {d: lax.ppermute(parts[d], ("chain", "tp"), diagonal(d)) for d in (2, 1, 3)}
    return jnp.where(y == 0, parts[0], jnp.where(y == 1, got[1], jnp.where(y == 2, got[2], got[3])))


def down(first):
    _, _, z, _, c = place()
    far = lax.ppermute(first, "chain", Z_FAR)
    second = jnp.where(z == 2, far, first)
    near = lax.ppermute(second, "chain", Z_NEAR)
    mine = jnp.where((z == 1) | (z == 3), near, second)
    cut = mine.shape[1] // 2
    other = lax.ppermute(mine[:, cut:], "chain", CORE)
    return jnp.where(c == 0, mine[:, :cut], other)


def gather(half):
    return lax.all_gather(half, "chain", axis_index_groups=ROWS, axis=0)


def scaled_of(x, gain):
    return (x.astype(jnp.float32) * gain.astype(jnp.float32)).astype(LOW)


def dot(a, b):
    return jnp.dot(a, b, preferred_element_type=jnp.float32)


def build_kernel(flags, x_ref, g_ref, own_ref, plus_ref, minus_ref, scaled):
    j = pl.program_id(0)
    held = flags[0] > 0

    @pl.when(held & (j == 0))
    def _():
        scaled[...] = scaled_of(x_ref[...], g_ref[...])

    def put(out_ref):
        @pl.when(held)
        def _():
            out_ref[0] = dot(scaled[...], own_ref[...]).astype(LOW)

        for slot in range(NX):
            @pl.when(jnp.logical_not(held) & (j % NX == slot))
            def _():
                out_ref[0] = x_ref[:, slot * WIDE:(slot + 1) * WIDE]

    @pl.when(j < NX)
    def _():
        put(plus_ref)

    @pl.when(j >= NX)
    def _():
        put(minus_ref)


def build(held, x, gain, own, layer):
    tokens, depth = x.shape
    h, here, _, _, _ = place()
    mine, other = h * NX, (1 - h) * NX
    nxt, last, far = (here + 1) % NX, (here + 3) % NX, (here + 2) % NX
    order = [other + nxt, mine + nxt, other + far, other + far, mine + far, mine + far, other + last, mine + last]
    flags = jnp.stack([held] + order).astype(jnp.int32)
    shape = jax.ShapeDtypeStruct((NX, tokens, WIDE), LOW)
    return pl.pallas_call(
        build_kernel,
        out_shape=(shape, shape),
        grid_spec=pltpu.PrefetchScalarGridSpec(
            num_scalar_prefetch=1,
            grid=(2 * NX,),
            in_specs=[
                pl.BlockSpec((tokens, depth), lambda j, f: (0, 0)),
                pl.BlockSpec((1, depth), lambda j, f: (0, 0)),
                pl.BlockSpec((None, None, depth, WIDE), lambda j, f: (0, layer, 0, f[1 + j] * f[0])),
            ],
            out_specs=(
                pl.BlockSpec((1, tokens, WIDE), lambda j, f: (jnp.minimum(j, NX - 1), 0, 0)),
                pl.BlockSpec((1, tokens, WIDE), lambda j, f: (jnp.maximum(j - NX, 0), 0, 0)),
            ),
            scratch_shapes=[pltpu.VMEM((tokens, depth), LOW)],
        ),
        compiler_params=pltpu.CompilerParams(vmem_limit_bytes=VMEM),
        cost_estimate=pl.CostEstimate(
            flops=2 * tokens * depth * WIDE * 2 * NX, bytes_accessed=12 * tokens * depth, transcendentals=0
        ),
    )(flags, x, gain, own)


def head_sum(mine, flags, refs, scaled):
    x_ref, g_ref, own_ref, plus_ref, minus_ref, pass_plus, pass_minus, src_ref, acc = refs

    @pl.when(flags[0] > 0)
    def _():
        total = dot(scaled_of(x_ref[...], g_ref[...]), own_ref[...])
        late = pass_minus if mine else pass_plus
        for term in (plus_ref[1 if mine else 0], minus_ref[3 if mine else 2], late[0]):
            total += term.astype(jnp.float32)
        acc[...] = total

    @pl.when(flags[0] == 0)
    def _():
        total = dot(x_ref[:, :2 * WIDE], src_ref[0]) + dot(x_ref[:, 2 * WIDE:], src_ref[1])
        blocks = [minus_ref[s] for s in range(NX)]
        blocks += [pass_minus[0], pass_minus[1], pass_plus[0], pass_plus[1]]
        blocks += [plus_ref[s] for s in range(NX)]
        for k, block in enumerate(blocks):
            total += dot(block, src_ref[2 + k // 2, (k % 2) * WIDE:(k % 2 + 1) * WIDE, :])
        acc[...] = total


def away_kernel(flags, *refs):
    *head, out_ref, acc = refs
    head_sum(False, flags, (*head, acc), None)
    out_ref[...] = acc[...].astype(LOW)


def mine_kernel(flags, *refs):
    *head, came_ref, scale_ref, cos_ref, sin_ref, _, out_ref, acc = refs
    head_sum(True, flags, (*head, acc), None)
    mixed = (acc[...] + came_ref[...].astype(jnp.float32)) * scale_ref[...]
    key = mixed[:, :HD]
    out_ref[:, :HD] = (key * cos_ref[...] + pltpu.roll(key, HD // 2, 1) * sin_ref[...]).astype(LOW)
    out_ref[:, HD:] = mixed[:, HD:].astype(LOW)


def finish(held, x, gain, own, layer, moved, src, src_layer, rest=None):
    tokens, depth = x.shape
    tile = tokens // TILES
    h, here, _, _, _ = place()
    head = (h if rest is not None else 1 - h) * NX + here
    flags = jnp.stack([held, head]).astype(jnp.int32)
    slots = pl.BlockSpec((NX, tile, WIDE), lambda i, f: (0, i, 0))
    passed = pl.BlockSpec((2, tile, WIDE), lambda i, f: (0, i, 0))
    in_specs = [
        pl.BlockSpec((tile, depth), lambda i, f: (i, 0)),
        pl.BlockSpec((1, depth), lambda i, f: (0, 0)),
        pl.BlockSpec((None, None, depth, WIDE), lambda i, f: (0, layer, 0, f[1])),
        slots,
        slots,
        passed,
        passed,
        pl.BlockSpec((2 * NY, None, depth // 2, WIDE), lambda i, f: (0, src_layer, 0, 0)),
    ]
    args = [x, gain, own, *moved, src]
    aliases = {}
    if rest is None:
        kernel = away_kernel
        out_shape = jax.ShapeDtypeStruct((tokens, WIDE), LOW)
        out_specs = pl.BlockSpec((tile, WIDE), lambda i, f: (i, 0))
    else:
        kernel = mine_kernel
        came, scale, cosine, sine, out = rest
        wide = pl.BlockSpec((tile, HD), lambda i, f: (i, 0))
        in_specs += [
            pl.BlockSpec((tile, WIDE), lambda i, f: (i, 0)),
            pl.BlockSpec((tile, 1), lambda i, f: (i, 0)),
            wide,
            wide,
            pl.BlockSpec(memory_space=pl.ANY),
        ]
        args += [came, scale, cosine, sine, out]
        out_shape = jax.ShapeDtypeStruct((LAYERS, tokens, WIDE), LOW)
        out_specs = pl.BlockSpec((None, tile, WIDE), lambda i, f: (layer, i, 0))
        if layer > 0:
            aliases = {len(args): 0}
    return pl.pallas_call(
        kernel,
        out_shape=out_shape,
        grid_spec=pltpu.PrefetchScalarGridSpec(
            num_scalar_prefetch=1,
            grid=(TILES,),
            in_specs=in_specs,
            out_specs=out_specs,
            scratch_shapes=[pltpu.VMEM((tile, WIDE), jnp.float32)],
        ),
        input_output_aliases=aliases,
        compiler_params=pltpu.CompilerParams(vmem_limit_bytes=VMEM),
        cost_estimate=pl.CostEstimate(
            flops=2 * tokens * 4 * depth * WIDE, bytes_accessed=10 * tokens * depth, transcendentals=0
        ),
    )(flags, *args)


def ring_start(sent):
    plus, minus = sent
    return lax.ppermute(plus, "tp", X_NEXT), lax.ppermute(minus, "tp", X_LAST)


def ring_pass(got):
    plus, minus = got
    return lax.ppermute(plus[2:], "tp", X_NEXT), lax.ppermute(minus[:2], "tp", X_LAST)


def shards(hidden_first, hidden_second, weight_buffer, gain_buffer, loaded_layers, positions):
    inputs = (hidden_first, hidden_second)
    width = hidden_first.shape[1] * lax.axis_size("tp")
    h = lax.axis_index("tp") // NX
    held = [(loaded_layers[0] > layer).astype(jnp.int32) for layer in range(LAYERS)]
    gains = [gain_buffer[0, layer][None, :] for layer in range(LAYERS)]

    swap0 = scatter(pieces(weight_buffer, gain_buffer, (0,), 1 - h))
    sent0 = build(held[0], inputs[0], gains[0], weight_buffer, 0)
    got0 = ring_start(sent0)
    sent1 = build(held[1], inputs[1], gains[1], weight_buffer, 1)

    squares = jnp.stack([jnp.sum(jnp.square(v.astype(jnp.float32)), axis=1) for v in inputs])
    for pairs in (tp_pairs(lambda h, x: (h, x ^ 1)), tp_pairs(lambda h, x: (h, x ^ 2)), H_SWAP):
        squares = squares + lax.ppermute(squares, "tp", pairs)
    scale = lax.rsqrt(squares / width + 1e-05)
    half = HD // 2
    freq = 500000.0 ** (-2.0 * jnp.arange(half, dtype=jnp.float32) / HD)
    angle = positions.astype(jnp.float32)[:, None] * freq[None, :]
    cosine, sine = jnp.cos(angle), jnp.sin(angle)
    cosine, sine = jnp.concatenate([cosine, cosine], 1), jnp.concatenate([-sine, sine], 1)

    weights1, gains1 = after((weight_buffer, gain_buffer), swap0)
    swap1 = scatter(pieces(weights1, gains1, (1,), 1 - h))
    half0 = down(swap0)
    src0 = gather(half0)
    weights2, gains2 = after((weight_buffer, gain_buffer), swap1)
    keep = scatter(pieces(weights2, gains2, (0, 1), h))
    half1 = down(swap1)
    src1 = gather(half1)
    passed0 = ring_pass(after(got0, half0))
    got1 = ring_start(after(sent1, passed0))
    half2 = down(keep)
    src2 = gather(half2)
    passed1 = ring_pass(after(got1, half2))

    away0 = finish(held[0], inputs[0], gains[0], weight_buffer, 0, (*got0, *passed0), src0, 0)
    came0 = lax.ppermute(away0, "tp", H_SWAP)
    away1 = finish(held[1], inputs[1], gains[1], weight_buffer, 1, (*got1, *passed1), src1, 0)
    came1 = lax.ppermute(away1, "tp", H_SWAP)
    out = jnp.zeros((8, 128), LOW)
    for layer, (got, passed, came) in enumerate(((got0, passed0, came0), (got1, passed1, came1))):
        rest = (came, scale[layer][:, None], cosine, sine, out)
        out = finish(held[layer], inputs[layer], gains[layer], weight_buffer, layer, (*got, *passed), src2, layer, rest)
    return out


def solution(mesh):
    placed = (
        P("chain", "tp"),
        P("chain", "tp"),
        P("chain", None, "tp", None),
        P("chain", None, "tp"),
        P("chain"),
        P("chain"),
    )
    return jax.shard_map(
        shards, mesh=mesh, in_specs=placed, out_specs=P(None, "chain", "tp"), check_vma=False
    )
```

time: 280 us -> 373 us (1.33)
  waiting for transfers between devices: 160 us -> 202 us
  Pallas kernels: 15.8 us -> 49.5 us
  starting transfers between devices: 54.7 us -> 64.4 us
  local copies, waits for them, and re-layouts: 15.4 us -> 22.3 us
    ppermute x22 -> x28, waiting for transfers between devices: 121 us -> 186 us  [the longest x4 77.9 us: ring_start(): return (lax.ppermute(plus, 'tp', X_NEXT), lax.ppermute(minus, 'tp', X_LAST))]
    pallas_call x4 -> x6, Pallas kernels: 15.8 us -> 49.5 us  [the longest x4 27.5 us: finish(): pl.pallas_call(kernel, out_shape=out_shape, grid_spec=pltpu.PrefetchScala...]
    all_gather x2 -> x3, waiting for transfers between devices: 26.5 us -> 0.02 us  [gather(): return lax.all_gather(half, 'chain', axis_index_groups=ROWS, axis=0)]
    slice x5 -> x10, local copies, waits for them, and re-layouts: 1.26 us -> 16.1 us  [the longest x3 11.6 us: pieces(): weights[0, layer]]
    unnamed x20 -> x26, local copies, waits for them, and re-layouts: 13.8 us -> 2.26 us
    ppermute x22 -> x28, starting transfers between devices: 46.2 us -> 56.2 us  [the longest x9 30.1 us: scatter(): lax.ppermute(parts[d], ('chain', 'tp'), diagonal(d))]
    convert_element_type x6, other arithmetic: 8.31 us -> 4.21 us  [the longest x3 2.83 us: pieces(): (block * gains[0, layer][:, None].astype(jnp.float32)).astype(LOW)]
  transfers between devices with their start and end apart: 27 -> 34, of which waited for: 17 -> 23; matrix products, arithmetic and copies ran while one was open for 3% -> 8% of each run, Pallas kernels for 6% -> 11%
where the time goes in v2:
time: 373 us; the launch traced here: 371 us
  waiting for transfers between devices  202 us (54%)
  starting transfers between devices  64.4 us (17%)
  Pallas kernels  49.5 us (13%)
  local copies, waits for them, and re-layouts  22.3 us (6%)
  other arithmetic  18.3 us (5%)
  between operations  14.4 us (4%)
    ppermute x4, waiting for transfers between devices, ring_start(): return (lax.ppermute(plus, 'tp', X_NEXT), lax.ppermute(minus, 'tp', X_LAST))  77.9 us
    ppermute x9, waiting for transfers between devices, scatter(): lax.ppermute(parts[d], ('chain', 'tp'), diagonal(d))  40.7 us
    ppermute x9, starting transfers between devices, scatter(): lax.ppermute(parts[d], ('chain', 'tp'), diagonal(d))  30.1 us
    pallas_call x4, Pallas kernels, finish(): pl.pallas_call(kernel, out_shape=out_shape, grid_spec=pltpu.PrefetchScala...  27.5 us
    pallas_call x2, Pallas kernels, build(): pl.pallas_call(build_kernel, out_shape=(shape, shape), grid_spec=pltpu.Pr...  21.9 us
    ppermute x3, waiting for transfers between devices, down(): far = lax.ppermute(first, 'chain', Z_FAR)  18.9 us
    ppermute x3, waiting for transfers between devices, down(): near = lax.ppermute(second, 'chain', Z_NEAR)  17.2 us
    ppermute x3, waiting for transfers between devices, shards(): squares = squares + lax.ppermute(squares, 'tp', pairs)  15.9 us
  transfers between devices with their start and end apart: 34, of which 23 were waited for; matrix products, arithmetic and copies ran while one was open for 8% of the time, Pallas kernels for 11%

profile of v2, /device:TPU:6, one launch (start us, length us, event | category | flops | bytes accessed | tf_op | source)
XLA Modules:
  0.0 370.7 jit_solution(5101498834088630322)
XLA Ops:
  6.5 1.4 slice_convert_fusion.3
  7.9 4.8 %slice.44 = bf16[1,1,1024,2048]{3,2,1,0:T(8,128)(2,1)} slice(bf16[1,2,1024,2048]{3,2,1,0:T(8,128)(2,1)} %refs_2_.7), slice={[0:1], [0:1], [0:1024], [0:2048]} | slice | bytes 8388608 | tf_op jit(solution)/shard_map/slice | solution.py:71
  12.7 1.7 fusion.12
  14.4 3.8 %collective-permute-start.2 = (bf16[1,1024,256]{2,1,0:T(8,128)(2,1)S(1)}, bf16[1,1024,256]{2,1,0:T(8,128)(2,1)S(1)}, u32[]{:S(2)}, u32[]{:S(2)}) collective-permute-start(bf16[1,1024,256]{2,1,0:T(8,128)(2,1)S(1)} %get-tuple-element.48), channel_id=1, source_target_pairs={{0,19},{1,16},{2,17},{3,18},{4,23},{5,20},{6,21},{7,22}} | collective-permute-start | bytes 1572872 | tf_op jit(solution)/shard_map/ppermute | solution.py:79
  18.1 2.9 collective-permute-start.3
  21.0 1.3 collective-permute-start.4
  22.4 3.1 collective-permute-done.2
  25.5 5.6 %collective-permute-done.3 = bf16[1,1024,256]{2,1,0:T(8,128)(2,1)S(1)} collective-permute-done((bf16[1,1024,256]{2,1,0:T(8,128)(2,1)S(1)}, bf16[1,1024,256]{2,1,0:T(8,128)(2,1)S(1)}, u32[]{:S(2)}, u32[]{:S(2)}) %collective-permute-start.3) | collective-permute-done | bytes 524320 | tf_op jit(solution)/shard_map/ppermute | solution.py:79
  31.2 1.5 collective-permute-done.4
  32.7 1.4 fusion.16
  34.0 1.3 collective-permute-start.5
  35.4 6.6 %collective-permute-done.5 = bf16[1,1024,256]{2,1,0:T(8,128)(2,1)S(1)} collective-permute-done((bf16[1,1024,256]{2,1,0:T(8,128)(2,1)S(1)}, bf16[1,1024,256]{2,1,0:T(8,128)(2,1)S(1)}, u32[]{:S(2)}, u32[]{:S(2)}) %collective-permute-start.5) | collective-permute-done | bytes 524320 | tf_op jit(solution)/shard_map/ppermute | solution.py:85
  42.1 1.3 collective-permute-start.6
  43.4 2.5 slice.95
  46.0 4.1 %collective-permute-done.6 = bf16[1,1024,256]{2,1,0:T(8,128)(2,1)S(1)} collective-permute-done((bf16[1,1024,256]{2,1,0:T(8,128)(2,1)S(1)}, bf16[1,1024,256]{2,1,0:T(8,128)(2,1)S(1)}, u32[]{:S(2)}, u32[]{:S(2)}) %collective-permute-start.6) | collective-permute-done | bytes 524320 | tf_op jit(solution)/shard_map/ppermute | solution.py:87
  50.1 1.3 collective-permute-start.7
  51.8 1.3 collective-permute-start.12
  53.1 6.2 %collective-permute-start.13 = (bf16[1,1024,256]{2,1,0:T(8,128)(2,1)S(1)}, bf16[1,1024,256]{2,1,0:T(8,128)(2,1)S(1)}, u32[]{:S(2)}, u32[]{:S(2)}) collective-permute-start(bf16[1,1024,256]{2,1,0:T(8,128)(2,1)S(1)} %get-tuple-element.44), channel_id=1, source_target_pairs={{0,34},{1,35},{2,32},{3,33},{4,38},{5,39},{6,36},{7,37}} | collective-permute-start | bytes 1572872 | tf_op jit(solution)/shard_map/ppermute | solution.py:79
  59.4 1.6 collective-permute-start.14
  61.8 4.2 %collective-permute-done.13 = bf16[1,1024,256]{2,1,0:T(8,128)(2,1)S(1)} collective-permute-done((bf16[1,1024,256]{2,1,0:T(8,128)(2,1)S(1)}, bf16[1,1024,256]{2,1,0:T(8,128)(2,1)S(1)}, u32[]{:S(2)}, u32[]{:S(2)}) %collective-permute-start.13) | collective-permute-done | bytes 524320 | tf_op jit(solution)/shard_map/ppermute | solution.py:79
  66.1 4.1 %collective-permute-done.14 = bf16[1,1024,256]{2,1,0:T(8,128)(2,1)S(1)} collective-permute-done((bf16[1,1024,256]{2,1,0:T(8,128)(2,1)S(1)}, bf16[1,1024,256]{2,1,0:T(8,128)(2,1)S(1)}, u32[]{:S(2)}, u32[]{:S(2)}) %collective-permute-start.14) | collective-permute-done | bytes 524320 | tf_op jit(solution)/shard_map/ppermute | solution.py:79
  70.2 1.4 fusion.17
  71.5 1.3 collective-permute-start.23
  72.8 4.4 %fusion.20 = (bf16[1,1,1024,2048]{3,2,1,0:T(8,128)(2,1)S(1)}, bf16[1,1,1024,2048]{3,2,1,0:T(8,128)(2,1)S(1)}) fusion(bf16[1,2,1024,2048]{3,2,1,0:T(8,128)(2,1)} %refs_2_.7), kind=kLoop, calls=%fused_computation.70 | loop fusion | bytes 16777216 | tf_op jit(solution)/shard_map/slice | solution.py:71
  78.1 8.4 %collective-permute-start.17 = (bf16[2,1024,256]{2,1,0:T(8,128)(2,1)S(1)}, bf16[2,1024,256]{2,1,0:T(8,128)(2,1)}, u32[]{:S(2)}, u32[]{:S(2)}) collective-permute-start(bf16[2,1024,256]{2,1,0:T(8,128)(2,1)S(1)} %pad_maximum_fusion.2), channel_id=1, source_target_pairs={{0,49},{1,50},{2,51},{3,48},{4,53},{5,54},{6,55},{7,52}} | collective-permute-start | bytes 3145736 | tf_op jit(solution)/shard_map/ppermute | solution.py:79
  86.6 1.3 collective-permute-start.24
  88.0 2.3 collective-permute-start.16
  91.4 2.3 collective-permute-start.15
  94.7 1.3 collective-permute-start.25
  96.0 1.1 collective-permute-done.25
  97.9 3.7 %collective-permute-done.16 = bf16[2,1024,256]{2,1,0:T(8,128)(2,1)} collective-permute-done((bf16[2,1024,256]{2,1,0:T(8,128)(2,1)S(1)}, bf16[2,1024,256]{2,1,0:T(8,128)(2,1)}, u32[]{:S(2)}, u32[]{:S(2)}) %collective-permute-start.16) | collective-permute-done | bytes 1048608 | tf_op jit(solution)/shard_map/ppermute | solution.py:79
  101.7 18.4 %collective-permute-done.15 = bf16[2,1024,256]{2,1,0:T(8,128)(2,1)} collective-permute-done((bf16[2,1024,256]{2,1,0:T(8,128)(2,1)}, bf16[2,1024,256]{2,1,0:T(8,128)(2,1)}, u32[]{:S(2)}, u32[]{:S(2)}) %collective-permute-start.15) | collective-permute-done | bytes 1048608 | tf_op jit(solution)/shard_map/ppermute | solution.py:79
  120.1 1.4 maximum_select_fusion
  121.5 1.4 collective-permute-start.18
  122.9 12.2 %collective-permute-done.18 = bf16[2,1024,256]{2,1,0:T(8,128)(2,1)S(1)} collective-permute-done((bf16[2,1024,256]{2,1,0:T(8,128)(2,1)S(1)}, bf16[2,1024,256]{2,1,0:T(8,128)(2,1)S(1)}, u32[]{:S(2)}, u32[]{:S(2)}) %collective-permute-start.18) | collective-permute-done | bytes 1048608 | tf_op jit(solution)/shard_map/ppermute | solution.py:85
  135.3 1.4 collective-permute-start.19
  136.6 12.2 %collective-permute-done.19 = bf16[2,1024,256]{2,1,0:T(8,128)(2,1)S(1)} collective-permute-done((bf16[2,1024,256]{2,1,0:T(8,128)(2,1)S(1)}, bf16[2,1024,256]{2,1,0:T(8,128)(2,1)S(1)}, u32[]{:S(2)}, u32[]{:S(2)}) %collective-permute-start.19) | collective-permute-done | bytes 1048608 | tf_op jit(solution)/shard_map/ppermute | solution.py:87
  149.0 1.3 collective-permute-start.20
  150.3 1.5 collective-permute-done.20
  154.1 10.8 %shard_map.65 = (bf16[4,896,256]{2,1,0:T(8,128)(2,1)}, bf16[4,896,256]{2,1,0:T(8,128)(2,1)}) custom-call(s32[9]{0:T(128)} %stack.51.flags, bf16[896,1024]{1,0:T(8,128)(2,1)} %refs_0_.6, bf16[1,1024]{1,0:T(2,128)(2,1)} %get-tuple-element.57.g_ref.refs_1_, bf16[1,2,1024,2048]{3,2,1,0:T(8,128)(2,1)} %refs_2_.7), custom_call_target="tpu_custom_call" | custom-call | flops 3758096384 | bytes 11010048 | tf_op jit(solution)/shard_map/pallas_call | solution.py:141
  164.9 2.0 collective-permute-start.1
  166.9 40.5 %collective-permute-done.refs_3_ = bf16[4,896,256]{2,1,0:T(8,128)(2,1)S(1)} collective-permute-done((bf16[4,896,256]{2,1,0:T(8,128)(2,1)}, bf16[4,896,256]{2,1,0:T(8,128)(2,1)S(1)}, u32[]{:S(2)}, u32[]{:S(2)}) %collective-permute-start) | collective-permute-done | bytes 1835040 | tf_op jit(solution)/shard_map/ppermute | solution.py:262
  207.4 1.4 collective-permute-done.1.refs_4_
  208.9 1.8 collective-permute-start.8
  212.6 11.2 %shard_map.64 = (bf16[4,896,256]{2,1,0:T(8,128)(2,1)}, bf16[4,896,256]{2,1,0:T(8,128)(2,1)}) custom-call(s32[9]{0:T(128)} %stack.50.flags, bf16[896,1024]{1,0:T(8,128)(2,1)} %refs_0_.7, bf16[1,1024]{1,0:T(2,128)(2,1)} %get-tuple-element.58.g_ref.refs_1_, bf16[1,2,1024,2048]{3,2,1,0:T(8,128)(2,1)} %refs_2_.7), custom_call_target="tpu_custom_call" | custom-call | flops 3758096384 | bytes 11010048 | tf_op jit(solution)/shard_map/pallas_call | solution.py:141
  223.8 6.9 %collective-permute-done.8.refs_5_ = bf16[2,896,256]{2,1,0:T(8,128)(2,1)S(1)} collective-permute-done((bf16[2,896,256]{2,1,0:T(8,128)(2,1)S(1)}, bf16[2,896,256]{2,1,0:T(8,128)(2,1)S(1)}, u32[]{:S(2)}, u32[]{:S(2)}) %collective-permute-start.8) | collective-permute-done | bytes 917536 | tf_op jit(solution)/shard_map/ppermute | solution.py:267
  230.8 3.6 collective-permute-done.9.refs_6_
  234.9 1.5 collective-permute-start.11
  237.5 1.7 fusion.18
  239.2 1.3 pad_maximum_fusion.3
  240.4 34.4 %collective-permute-done.10.refs_3_ = bf16[4,896,256]{2,1,0:T(8,128)(2,1)} collective-permute-done((bf16[4,896,256]{2,1,0:T(8,128)(2,1)}, bf16[4,896,256]{2,1,0:T(8,128)(2,1)}, u32[]{:S(2)}, u32[]{:S(2)}) %collective-permute-start.10) | collective-permute-done | bytes 1835040 | tf_op jit(solution)/shard_map/ppermute | solution.py:262
  274.8 1.6 collective-permute-done.11.refs_4_
  276.4 1.2 slice.103
  278.3 2.2 slice.104
  280.5 1.5 collective-permute-start.22
  284.7 15.8 %collective-permute-done.28 = f32[2,896]{1,0:T(2,128)S(1)} collective-permute-done((f32[2,896]{1,0:T(2,128)S(1)}, f32[2,896]{1,0:T(2,128)S(1)}, u32[]{:S(2)}, u32[]{:S(2)}) %collective-permute-start.28) | collective-permute-done | bytes 7200 | tf_op jit(solution)/shard_map/ppermute | solution.py:284
  300.5 7.2 %collective-permute-start.29 = (f32[2,896]{1,0:T(2,128)S(1)}, f32[2,896]{1,0:T(2,128)S(1)}, u32[]{:S(2)}, u32[]{:S(2)}) collective-permute-start(f32[2,896]{1,0:T(2,128)S(1)} %fusion.21), channel_id=1, source_target_pairs={{0,4},{1,5},{2,6},{3,7},{4,0},{5,1},{6,2},{7,3},{8,12},{9,13},{10,... | collective-permute-start | bytes 21512 | tf_op jit(solution)/shard_map/ppermute | solution.py:284
  307.8 6.5 %shard_map.67 = bf16[896,256]{1,0:T(8,128)(2,1)} custom-call(s32[2]{0:T(128)} %pad_add_fusion.3.flags, bf16[896,1024]{1,0:T(8,128)(2,1)} %refs_0_.6, bf16[1,1024]{1,0:T(2,128)(2,1)} %get-tuple-element.57.g_ref.refs_1_, bf16[1,2,1024,2048]{3,2,1,0:T(8,128)(2,1)} %refs_2_.7, bf16[4,896,256]{2,1,0:T(8,128)(2,1)} %copy-done.2, bf16[4,896,256]{2,1,0:T(8,128)(2,1)} %copy-done.3, ...), custom_call_target="tpu_custom_call" | custom-call | flops 1879048192 | bytes 9175040 | tf_op jit(solution)/shard_map/pallas_call | solution.py:242
  315.6 6.5 %shard_map.66 = bf16[896,256]{1,0:T(8,128)(2,1)} custom-call(s32[2]{0:T(128)} %pad_add_fusion.2.flags, bf16[896,1024]{1,0:T(8,128)(2,1)} %refs_0_.7, bf16[1,1024]{1,0:T(2,128)(2,1)} %get-tuple-element.58.g_ref.refs_1_, bf16[1,2,1024,2048]{3,2,1,0:T(8,128)(2,1)} %refs_2_.7, bf16[4,896,256]{2,1,0:T(8,128)(2,1)} %collective-permute-done.10.refs_3_, ...), custom_call_target="tpu_custom_call" | custom-call | flops 1879048192 | bytes 9175040 | tf_op jit(solution)/shard_map/pallas_call | solution.py:242
  322.2 5.9 %collective-permute-start.26 = (bf16[896,256]{1,0:T(8,128)(2,1)}, bf16[896,256]{1,0:T(8,128)(2,1)S(1)}, u32[]{:S(2)}, u32[]{:S(2)}) collective-permute-start(bf16[896,256]{1,0:T(8,128)(2,1)} %shard_map.66), channel_id=1, source_target_pairs={{0,4},{1,5},{2,6},{3,7},{4,0},{5,1},{6,2},{7,3},{8,12},{9,13},{10,... | collective-permute-start | bytes 1376264 | tf_op jit(solution)/shard_map/ppermute | solution.py:309
  330.1 5.6 %collective-permute-done.30.refs_8_ = bf16[896,256]{1,0:T(8,128)(2,1)S(1)} collective-permute-done((bf16[896,256]{1,0:T(8,128)(2,1)}, bf16[896,256]{1,0:T(8,128)(2,1)S(1)}, u32[]{:S(2)}, u32[]{:S(2)}) %collective-permute-start.30) | collective-permute-done | bytes 458784 | tf_op jit(solution)/shard_map/ppermute | solution.py:307
  336.4 7.2 %shard_map.68.refs_12_ = bf16[2,896,256]{2,1,0:T(8,128)(2,1)} custom-call(s32[2]{0:T(128)} %get-tuple-element.59.flags, bf16[896,1024]{1,0:T(8,128)(2,1)} %refs_0_.6, bf16[1,1024]{1,0:T(2,128)(2,1)} %get-tuple-element.57.g_ref.refs_1_, bf16[1,2,1024,2048]{3,2,1,0:T(8,128)(2,1)} %refs_2_.7, bf16[4,896,256]{2,1,0:T(8,128)(2,1)} %copy-done.2, ...), custom_call_target="tpu_custom_call" | custom-call | flops 1879048192 | bytes 9175040 | tf_op jit(solution)/shard_map/pallas_call | solution.py:242
  343.7 12.5 %collective-permute-done.26.refs_8_ = bf16[896,256]{1,0:T(8,128)(2,1)S(1)} collective-permute-done((bf16[896,256]{1,0:T(8,128)(2,1)}, bf16[896,256]{1,0:T(8,128)(2,1)S(1)}, u32[]{:S(2)}, u32[]{:S(2)}) %collective-permute-start.26) | collective-permute-done | bytes 458784 | tf_op jit(solution)/shard_map/ppermute | solution.py:309
  356.9 7.2 %shard_map.69 = bf16[2,896,256]{2,1,0:T(8,128)(2,1)} custom-call(s32[2]{0:T(128)} %get-tuple-element.60.flags, bf16[896,1024]{1,0:T(8,128)(2,1)} %refs_0_.7, bf16[1,1024]{1,0:T(2,128)(2,1)} %get-tuple-element.58.g_ref.refs_1_, bf16[1,2,1024,2048]{3,2,1,0:T(8,128)(2,1)} %refs_2_.7, ...), custom_call_target="tpu_custom_call", output_to_operand_aliasing={{}: (13, {})} | custom-call | flops 1879048192 | bytes 9175040 | tf_op jit(solution)/shard_map/pallas_call | solution.py:242
  (91 shorter events, 18.8 us)
Async XLA Ops:
  6.5 301.2 %all-gather.11.cloned.1.call-start = ((), (), s32[]{:S(2)}) async-start(), calls=%async_computation.2 | async-start | bytes 2359296 | tf_op jit(solution)/shard_map/all_gather | solution.py:95
  14.4 11.2 %collective-permute-start.2 = (bf16[1,1024,256]{2,1,0:T(8,128)(2,1)S(1)}, bf16[1,1024,256]{2,1,0:T(8,128)(2,1)S(1)}, u32[]{:S(2)}, u32[]{:S(2)}) collective-permute-start(bf16[1,1024,256]{2,1,0:T(8,128)(2,1)S(1)} %get-tuple-element.48), channel_id=1, source_target_pairs={{0,19},{1,16},{2,17},{3,18},{4,23},{5,20},{6,21},{7,22}} | collective-permute-start | bytes 1572872 | tf_op jit(solution)/shard_map/ppermute | solution.py:79
  18.1 13.0 %collective-permute-start.3 = (bf16[1,1024,256]{2,1,0:T(8,128)(2,1)S(1)}, bf16[1,1024,256]{2,1,0:T(8,128)(2,1)S(1)}, u32[]{:S(2)}, u32[]{:S(2)}) collective-permute-start(bf16[1,1024,256]{2,1,0:T(8,128)(2,1)S(1)} %get-tuple-element.47), channel_id=1, source_target_pairs={{0,34},{1,35},{2,32},{3,33},{4,38},{5,39},{6,36},{7,37}} | collective-permute-start | bytes 1572872 | tf_op jit(solution)/shard_map/ppermute | solution.py:79
  21.0 11.6 %collective-permute-start.4 = (bf16[1,1024,256]{2,1,0:T(8,128)(2,1)S(1)}, bf16[1,1024,256]{2,1,0:T(8,128)(2,1)S(1)}, u32[]{:S(2)}, u32[]{:S(2)}) collective-permute-start(bf16[1,1024,256]{2,1,0:T(8,128)(2,1)S(1)} %get-tuple-element.46), channel_id=1, source_target_pairs={{0,49},{1,50},{2,51},{3,48},{4,53},{5,54},{6,55},{7,52}} | collective-permute-start | bytes 1572872 | tf_op jit(solution)/shard_map/ppermute | solution.py:79
  34.0 8.0 %collective-permute-start.5 = (bf16[1,1024,256]{2,1,0:T(8,128)(2,1)S(1)}, bf16[1,1024,256]{2,1,0:T(8,128)(2,1)S(1)}, u32[]{:S(2)}, u32[]{:S(2)}) collective-permute-start(bf16[1,1024,256]{2,1,0:T(8,128)(2,1)S(1)} %fusion.16), channel_id=1, source_target_pairs={{0,128},{16,144},{32,160},{48,176},{1,129},{17,145},{33,161},{49,1... | collective-permute-start | bytes 1572872 | tf_op jit(solution)/shard_map/ppermute | solution.py:85
  42.1 8.0 %collective-permute-start.6 = (bf16[1,1024,256]{2,1,0:T(8,128)(2,1)S(1)}, bf16[1,1024,256]{2,1,0:T(8,128)(2,1)S(1)}, u32[]{:S(2)}, u32[]{:S(2)}) collective-permute-start(bf16[1,1024,256]{2,1,0:T(8,128)(2,1)S(1)} %broadcast_select_fusion.3), channel_id=1, source_target_pairs={{0,64},{16,80},{32,96},{48,112},{128,192},{144,208},{160,224},{176... | collective-permute-start | bytes 1572872 | tf_op jit(solution)/shard_map/ppermute | solution.py:87
  43.4 2.5 copy-start.11
  45.9 5.5 %copy-start.4 = (bf16[1,1,1024,2048]{3,2,1,0:T(8,128)(2,1)}, bf16[1,1,1024,2048]{3,2,1,0:T(8,128)(2,1)S(1)}, u32[]{:S(2)}) copy-start(bf16[1,1,1024,2048]{3,2,1,0:T(8,128)(2,1)S(1)} %slice.95) | copy-start | bytes 12582916
  50.1 10.8 %collective-permute-start.7 = (bf16[1,512,256]{2,1,0:T(8,128)(2,1)S(1)}, bf16[1,512,256]{2,1,0:T(8,128)(2,1)S(1)}, u32[]{:S(2)}, u32[]{:S(2)}) collective-permute-start(bf16[1,512,256]{2,1,0:T(8,128)(2,1)S(1)} %slice.110), channel_id=1, source_target_pairs={{0,8},{16,24},{32,40},{48,56},{64,72},{80,88},{96,104},{112,120},{... | collective-permute-start | bytes 786440 | tf_op jit(solution)/shard_map/ppermute | solution.py:90
  51.8 10.0 %collective-permute-start.12 = (bf16[1,1024,256]{2,1,0:T(8,128)(2,1)S(1)}, bf16[1,1024,256]{2,1,0:T(8,128)(2,1)S(1)}, u32[]{:S(2)}, u32[]{:S(2)}) collective-permute-start(bf16[1,1024,256]{2,1,0:T(8,128)(2,1)S(1)} %get-tuple-element.45), channel_id=1, source_target_pairs={{0,19},{1,16},{2,17},{3,18},{4,23},{5,20},{6,21},{7,22}} | collective-permute-start | bytes 1572872 | tf_op jit(solution)/shard_map/ppermute | solution.py:79
  53.1 12.9 %collective-permute-start.13 = (bf16[1,1024,256]{2,1,0:T(8,128)(2,1)S(1)}, bf16[1,1024,256]{2,1,0:T(8,128)(2,1)S(1)}, u32[]{:S(2)}, u32[]{:S(2)}) collective-permute-start(bf16[1,1024,256]{2,1,0:T(8,128)(2,1)S(1)} %get-tuple-element.44), channel_id=1, source_target_pairs={{0,34},{1,35},{2,32},{3,33},{4,38},{5,39},{6,36},{7,37}} | collective-permute-start | bytes 1572872 | tf_op jit(solution)/shard_map/ppermute | solution.py:79
  59.4 10.8 %collective-permute-start.14 = (bf16[1,1024,256]{2,1,0:T(8,128)(2,1)S(1)}, bf16[1,1024,256]{2,1,0:T(8,128)(2,1)S(1)}, u32[]{:S(2)}, u32[]{:S(2)}) collective-permute-start(bf16[1,1024,256]{2,1,0:T(8,128)(2,1)S(1)} %get-tuple-element.43), channel_id=1, source_target_pairs={{0,49},{1,50},{2,51},{3,48},{4,53},{5,54},{6,55},{7,52}} | collective-permute-start | bytes 1572872 | tf_op jit(solution)/shard_map/ppermute | solution.py:79
  61.8 252.6 %all-gather.9.cloned.1.call-start = ((), (), s32[]{:S(2)}) async-start(), calls=%async_computation.1 | async-start | bytes 2359296 | tf_op jit(solution)/shard_map/all_gather | solution.py:95
  71.5 15.0 %collective-permute-start.23 = (bf16[1,1024,256]{2,1,0:T(8,128)(2,1)S(1)}, bf16[1,1024,256]{2,1,0:T(8,128)(2,1)S(1)}, u32[]{:S(2)}, u32[]{:S(2)}) collective-permute-start(bf16[1,1024,256]{2,1,0:T(8,128)(2,1)S(1)} %fusion.17), channel_id=1, source_target_pairs={{0,128},{16,144},{32,160},{48,176},{1,129},{17,145},{33,161},{49,1... | collective-permute-start | bytes 1572872 | tf_op jit(solution)/shard_map/ppermute | solution.py:85
  78.1 19.8 %collective-permute-start.17 = (bf16[2,1024,256]{2,1,0:T(8,128)(2,1)S(1)}, bf16[2,1024,256]{2,1,0:T(8,128)(2,1)}, u32[]{:S(2)}, u32[]{:S(2)}) collective-permute-start(bf16[2,1024,256]{2,1,0:T(8,128)(2,1)S(1)} %pad_maximum_fusion.2), channel_id=1, source_target_pairs={{0,49},{1,50},{2,51},{3,48},{4,53},{5,54},{6,55},{7,52}} | collective-permute-start | bytes 3145736 | tf_op jit(solution)/shard_map/ppermute | solution.py:79
  86.6 8.0 %collective-permute-start.24 = (bf16[1,1024,256]{2,1,0:T(8,128)(2,1)S(1)}, bf16[1,1024,256]{2,1,0:T(8,128)(2,1)S(1)}, u32[]{:S(2)}, u32[]{:S(2)}) collective-permute-start(bf16[1,1024,256]{2,1,0:T(8,128)(2,1)S(1)} %broadcast_select_fusion.2), channel_id=1, source_target_pairs={{0,64},{16,80},{32,96},{48,112},{128,192},{144,208},{160,224},{176... | collective-permute-start | bytes 1572872 | tf_op jit(solution)/shard_map/ppermute | solution.py:87
  88.0 13.6 %collective-permute-start.16 = (bf16[2,1024,256]{2,1,0:T(8,128)(2,1)S(1)}, bf16[2,1024,256]{2,1,0:T(8,128)(2,1)}, u32[]{:S(2)}, u32[]{:S(2)}) collective-permute-start(bf16[2,1024,256]{2,1,0:T(8,128)(2,1)S(1)} %pad_maximum_fusion.1), channel_id=1, source_target_pairs={{0,34},{1,35},{2,32},{3,33},{4,38},{5,39},{6,36},{7,37}} | collective-permute-start | bytes 3145736 | tf_op jit(solution)/shard_map/ppermute | solution.py:79
  91.4 28.7 %collective-permute-start.15 = (bf16[2,1024,256]{2,1,0:T(8,128)(2,1)}, bf16[2,1024,256]{2,1,0:T(8,128)(2,1)}, u32[]{:S(2)}, u32[]{:S(2)}) collective-permute-start(bf16[2,1024,256]{2,1,0:T(8,128)(2,1)} %pad_maximum_fusion), channel_id=1, source_target_pairs={{0,19},{1,16},{2,17},{3,18},{4,23},{5,20},{6,21},{7,22}} | collective-permute-start | bytes 3145736 | tf_op jit(solution)/shard_map/ppermute | solution.py:79
  94.7 2.4 collective-permute-start.25
  97.9 237.8 %all-gather.7.cloned.1.call-start = ((), (), s32[]{:S(2)}) async-start(), calls=%async_computation | async-start | bytes 4718592 | tf_op jit(solution)/shard_map/all_gather | solution.py:95
  121.5 13.6 %collective-permute-start.18 = (bf16[2,1024,256]{2,1,0:T(8,128)(2,1)S(1)}, bf16[2,1024,256]{2,1,0:T(8,128)(2,1)S(1)}, u32[]{:S(2)}, u32[]{:S(2)}) collective-permute-start(bf16[2,1024,256]{2,1,0:T(8,128)(2,1)S(1)} %maximum_select_fusion), channel_id=1, source_target_pairs={{0,128},{16,144},{32,160},{48,176},{1,129},{17,145},{33,161},{49,1... | collective-permute-start | bytes 3145736 | tf_op jit(solution)/shard_map/ppermute | solution.py:85
  135.3 13.6 %collective-permute-start.19 = (bf16[2,1024,256]{2,1,0:T(8,128)(2,1)S(1)}, bf16[2,1024,256]{2,1,0:T(8,128)(2,1)S(1)}, u32[]{:S(2)}, u32[]{:S(2)}) collective-permute-start(bf16[2,1024,256]{2,1,0:T(8,128)(2,1)S(1)} %broadcast_select_fusion), channel_id=1, source_target_pairs={{0,64},{16,80},{32,96},{48,112},{128,192},{144,208},{160,224},{176... | collective-permute-start | bytes 3145736 | tf_op jit(solution)/shard_map/ppermute | solution.py:87
  149.0 2.8 collective-permute-start.20
  164.9 42.5 %collective-permute-start = (bf16[4,896,256]{2,1,0:T(8,128)(2,1)}, bf16[4,896,256]{2,1,0:T(8,128)(2,1)S(1)}, u32[]{:S(2)}, u32[]{:S(2)}) collective-permute-start(bf16[4,896,256]{2,1,0:T(8,128)(2,1)} %get-tuple-element.21), channel_id=1, source_target_pairs={{0,1},{1,2},{2,3},{3,0},{4,5},{5,6},{6,7},{7,4},{8,9},{9,10},{10,1... | collective-permute-start | bytes 5505032 | tf_op jit(solution)/shard_map/ppermute | solution.py:262
  164.9 43.9 %collective-permute-start.1 = (bf16[4,896,256]{2,1,0:T(8,128)(2,1)}, bf16[4,896,256]{2,1,0:T(8,128)(2,1)S(1)}, u32[]{:S(2)}, u32[]{:S(2)}) collective-permute-start(bf16[4,896,256]{2,1,0:T(8,128)(2,1)} %get-tuple-element.22), channel_id=1, source_target_pairs={{0,3},{1,0},{2,1},{3,2},{4,7},{5,4},{6,5},{7,6},{8,11},{9,8},{10,9... | collective-permute-start | bytes 5505032 | tf_op jit(solution)/shard_map/ppermute | solution.py:262
  207.4 1.4 copy-start.2
  208.8 1.9 copy-start.3
  208.9 21.9 %collective-permute-start.8 = (bf16[2,896,256]{2,1,0:T(8,128)(2,1)S(1)}, bf16[2,896,256]{2,1,0:T(8,128)(2,1)S(1)}, u32[]{:S(2)}, u32[]{:S(2)}) collective-permute-start(bf16[2,896,256]{2,1,0:T(8,128)(2,1)S(1)} %slice.93), channel_id=1, source_target_pairs={{0,1},{1,2},{2,3},{3,0},{4,5},{5,6},{6,7},{7,4},{8,9},{9,10},{10,1... | collective-permute-start | bytes 2752520 | tf_op jit(solution)/shard_map/ppermute | solution.py:267
  211.7 22.7 %collective-permute-start.9 = (bf16[2,896,256]{2,1,0:T(8,128)(2,1)}, bf16[2,896,256]{2,1,0:T(8,128)(2,1)S(1)}, u32[]{:S(2)}, u32[]{:S(2)}) collective-permute-start(bf16[2,896,256]{2,1,0:T(8,128)(2,1)} %slice.94), channel_id=1, source_target_pairs={{0,3},{1,0},{2,1},{3,2},{4,7},{5,4},{6,5},{7,6},{8,11},{9,8},{10,9... | collective-permute-start | bytes 2752520 | tf_op jit(solution)/shard_map/ppermute | solution.py:267
  212.6 23.8 %copy-start = (bf16[896,1024]{1,0:T(8,128)(2,1)S(1)}, bf16[896,1024]{1,0:T(8,128)(2,1)}, u32[]{:S(2)}) copy-start(bf16[896,1024]{1,0:T(8,128)(2,1)} %refs_0_.6) | copy-start | bytes 5505028
  212.6 24.2 %copy-start.1 = (bf16[896,1024]{1,0:T(8,128)(2,1)S(1)}, bf16[896,1024]{1,0:T(8,128)(2,1)}, u32[]{:S(2)}) copy-start(bf16[896,1024]{1,0:T(8,128)(2,1)} %refs_0_.7) | copy-start | bytes 5505028
  223.8 13.6 %copy-start.12 = (s32[896]{0:T(1024)S(1)}, s32[896]{0:T(1024)}, u32[]{:S(2)}) copy-start(s32[896]{0:T(1024)} %param.11) | copy-start | bytes 10756
  230.7 9.7 %copy-start.5 = (bf16[2,896,256]{2,1,0:T(8,128)(2,1)}, bf16[2,896,256]{2,1,0:T(8,128)(2,1)S(1)}, u32[]{:S(2)}) copy-start(bf16[2,896,256]{2,1,0:T(8,128)(2,1)S(1)} %collective-permute-done.8.refs_5_) | copy-start | bytes 2752516
  234.4 6.0 %copy-start.6 = (bf16[2,896,256]{2,1,0:T(8,128)(2,1)}, bf16[2,896,256]{2,1,0:T(8,128)(2,1)S(1)}, u32[]{:S(2)}) copy-start(bf16[2,896,256]{2,1,0:T(8,128)(2,1)S(1)} %collective-permute-done.9.refs_6_) | copy-start | bytes 2752516
  234.4 40.4 %collective-permute-start.10 = (bf16[4,896,256]{2,1,0:T(8,128)(2,1)}, bf16[4,896,256]{2,1,0:T(8,128)(2,1)}, u32[]{:S(2)}, u32[]{:S(2)}) collective-permute-start(bf16[4,896,256]{2,1,0:T(8,128)(2,1)} %get-tuple-element.25), channel_id=1, source_target_pairs={{0,1},{1,2},{2,3},{3,0},{4,5},{5,6},{6,7},{7,4},{8,9},{9,10},{10,1... | collective-permute-start | bytes 5505032 | tf_op jit(solution)/shard_map/ppermute | solution.py:262
  234.9 41.5 %collective-permute-start.11 = (bf16[4,896,256]{2,1,0:T(8,128)(2,1)}, bf16[4,896,256]{2,1,0:T(8,128)(2,1)}, u32[]{:S(2)}, u32[]{:S(2)}) collective-permute-start(bf16[4,896,256]{2,1,0:T(8,128)(2,1)} %get-tuple-element.26), channel_id=1, source_target_pairs={{0,3},{1,0},{2,1},{3,2},{4,7},{5,4},{6,5},{7,6},{8,11},{9,8},{10,9... | collective-permute-start | bytes 5505032 | tf_op jit(solution)/shard_map/ppermute | solution.py:262
  237.3 45.9 %collective-permute-start.27 = (f32[2,896]{1,0:T(2,128)S(1)}, f32[2,896]{1,0:T(2,128)S(1)}, u32[]{:S(2)}, u32[]{:S(2)}) collective-permute-start(f32[2,896]{1,0:T(2,128)S(1)} %pad_maximum_fusion.5), channel_id=1, source_target_pairs={{0,1},{1,0},{2,3},{3,2},{4,5},{5,4},{6,7},{7,6},{8,9},{9,8},{10,11... | collective-permute-start | bytes 21512 | tf_op jit(solution)/shard_map/ppermute | solution.py:284
  277.7 36.7 %collective-permute-start.21 = (bf16[2,896,256]{2,1,0:T(8,128)(2,1)S(1)}, bf16[2,896,256]{2,1,0:T(8,128)(2,1)S(1)}, u32[]{:S(2)}, u32[]{:S(2)}) collective-permute-start(bf16[2,896,256]{2,1,0:T(8,128)(2,1)S(1)} %slice.103), channel_id=1, source_target_pairs={{0,1},{1,2},{2,3},{3,0},{4,5},{5,6},{6,7},{7,4},{8,9},{9,10},{10,1... | collective-permute-start | bytes 2752520 | tf_op jit(solution)/shard_map/ppermute | solution.py:267
  280.5 33.9 %collective-permute-start.22 = (bf16[2,896,256]{2,1,0:T(8,128)(2,1)}, bf16[2,896,256]{2,1,0:T(8,128)(2,1)S(1)}, u32[]{:S(2)}, u32[]{:S(2)}) collective-permute-start(bf16[2,896,256]{2,1,0:T(8,128)(2,1)} %slice.104), channel_id=1, source_target_pairs={{0,3},{1,0},{2,1},{3,2},{4,7},{5,4},{6,5},{7,6},{8,11},{9,8},{10,9... | collective-permute-start | bytes 2752520 | tf_op jit(solution)/shard_map/ppermute | solution.py:267
  283.3 17.3 %collective-permute-start.28 = (f32[2,896]{1,0:T(2,128)S(1)}, f32[2,896]{1,0:T(2,128)S(1)}, u32[]{:S(2)}, u32[]{:S(2)}) collective-permute-start(f32[2,896]{1,0:T(2,128)S(1)} %fusion.19), channel_id=1, source_target_pairs={{0,2},{1,3},{2,0},{3,1},{4,6},{5,7},{6,4},{7,5},{8,10},{9,11},{10,... | collective-permute-start | bytes 21512 | tf_op jit(solution)/shard_map/ppermute | solution.py:284
  300.5 27.5 %collective-permute-start.29 = (f32[2,896]{1,0:T(2,128)S(1)}, f32[2,896]{1,0:T(2,128)S(1)}, u32[]{:S(2)}, u32[]{:S(2)}) collective-permute-start(f32[2,896]{1,0:T(2,128)S(1)} %fusion.21), channel_id=1, source_target_pairs={{0,4},{1,5},{2,6},{3,7},{4,0},{5,1},{6,2},{7,3},{8,12},{9,13},{10,... | collective-permute-start | bytes 21512 | tf_op jit(solution)/shard_map/ppermute | solution.py:284
  314.3 21.3 %collective-permute-start.30 = (bf16[896,256]{1,0:T(8,128)(2,1)}, bf16[896,256]{1,0:T(8,128)(2,1)S(1)}, u32[]{:S(2)}, u32[]{:S(2)}) collective-permute-start(bf16[896,256]{1,0:T(8,128)(2,1)} %shard_map.67), channel_id=1, source_target_pairs={{0,4},{1,5},{2,6},{3,7},{4,0},{5,1},{6,2},{7,3},{8,12},{9,13},{10,... | collective-permute-start | bytes 1376264 | tf_op jit(solution)/shard_map/ppermute | solution.py:307
  314.3 1.0 copy-start.7
  314.3 1.3 copy-start.8
  322.2 34.0 %collective-permute-start.26 = (bf16[896,256]{1,0:T(8,128)(2,1)}, bf16[896,256]{1,0:T(8,128)(2,1)S(1)}, u32[]{:S(2)}, u32[]{:S(2)}) collective-permute-start(bf16[896,256]{1,0:T(8,128)(2,1)} %shard_map.66), channel_id=1, source_target_pairs={{0,4},{1,5},{2,6},{3,7},{4,0},{5,1},{6,2},{7,3},{8,12},{9,13},{10,... | collective-permute-start | bytes 1376264 | tf_op jit(solution)/shard_map/ppermute | solution.py:309
  335.6 0.8 copy-start.9
  356.2 0.8 copy-start.10
Sparse Core Ops, SparseCore 0:
  61.9 36.1 all-gather.10
  100.0 26.8 all-gather.8
  152.9 40.0 all-gather.6

commit v3 on v0

v3 whole, which is shorter than its diff:
```python
import functools

import jax
import jax.numpy as jnp
from jax import lax
from jax.experimental import pallas as pl
from jax.experimental.pallas import tpu as pltpu
from jax.sharding import PartitionSpec as P

HD = 128
WIDE = 2 * HD
LAYERS = 2
NY, NX, NZ = 4, 4, 4
VMEM = 56 << 20
LOW = jnp.bfloat16
COLUMNS = LAYERS


def tp_pairs(step):
    pairs = []
    for h in range(2):
        for x in range(NX):
            h2, x2 = step(h, x)
            pairs.append((h * NX + x, (h2 % 2) * NX + x2 % NX))
    return pairs


def chain_pairs(step):
    pairs = []
    for z in range(NZ):
        for y in range(NY):
            for c in range(2):
                to = step(z, y, c)
                if to is not None:
                    z2, y2, c2 = to
                    pairs.append(((z * NY + y) * 2 + c, (z2 * NY + y2 % NY) * 2 + c2))
    return pairs


X_NEXT = tp_pairs(lambda h, x: (h, x + 1))
X_LAST = tp_pairs(lambda h, x: (h, x - 1))
X_ONE = tp_pairs(lambda h, x: (h, x ^ 1))
X_TWO = tp_pairs(lambda h, x: (h, x ^ 2))
H_SWAP = tp_pairs(lambda h, x: (h + 1, x))
Z_FAR = chain_pairs(lambda z, y, c: (2, y, 0) if (z, c) == (0, 0) else None)
Z_NEAR = chain_pairs(lambda z, y, c: (z + 1, y, 0) if z in (0, 2) and c == 0 else None)
CORE = chain_pairs(lambda z, y, c: (z, y, 1) if c == 0 else None)
ROWS = [[z * NY * 2 + k for k in range(NY * 2)] for z in range(NZ)]


def from_source(k):
    return chain_pairs(lambda z, y, c: (0, k, 0) if (z, y, c) == (0, 0, 0) else None)


def after(value, *earlier):
    return lax.optimization_barrier((value, earlier))[0]


def place():
    tp, chain = lax.axis_index("tp"), lax.axis_index("chain")
    return tp // NX, tp % NX, chain // (2 * NY), chain // 2 % NY, chain % 2


def dot(a, b):
    return jnp.dot(a, b, preferred_element_type=jnp.float32)


def pieces_kernel(flags, w_ref, g_ref, *out_refs):
    for layer in range(LAYERS):
        row = g_ref[layer:layer + 1, :].astype(jnp.float32)
        gain = jnp.broadcast_to(row, (HD, row.shape[1])).T
        depth = row.shape[1] // NY
        for y, out_ref in enumerate(out_refs):
            rows = slice(y * depth, (y + 1) * depth)
            for at in range(0, w_ref.shape[2], HD):
                out_ref[layer, :, at:at + HD] = (w_ref[layer, rows, at:at + HD].astype(jnp.float32) * gain[rows]).astype(LOW)


def pieces(flags, weights, gains, which):
    depth, wide = weights.shape[2], weights.shape[3] // 2
    return pl.pallas_call(
        pieces_kernel,
        out_shape=tuple(jax.ShapeDtypeStruct((LAYERS, depth // NY, wide), LOW) for _ in range(NY)),
        grid_spec=pltpu.PrefetchScalarGridSpec(
            num_scalar_prefetch=1,
            grid=(1,),
            in_specs=[
                pl.BlockSpec((None, LAYERS, depth, wide), lambda i, f: (0, 0, 0, f[COLUMNS + which * NX] // NX)),
                pl.BlockSpec((None, LAYERS, depth), lambda i, f: (0, 0, 0)),
            ],
            out_specs=tuple(pl.BlockSpec((LAYERS, depth // NY, wide), lambda i, f: (0, 0, 0)) for _ in range(NY)),
        ),
        compiler_params=pltpu.CompilerParams(vmem_limit_bytes=VMEM),
        cost_estimate=pl.CostEstimate(
            flops=LAYERS * depth * wide, bytes_accessed=4 * LAYERS * depth * wide, transcendentals=0
        ),
    )(flags, weights, gains)


def scatter(parts):
    y = place()[3]
    got = {k: lax.ppermute(parts[k], "chain", from_source(k)) for k in (2, 1, 3)}
    return jnp.where(y == 0, parts[0], jnp.where(y == 1, got[1], jnp.where(y == 2, got[2], got[3])))


def down(first):
    z = place()[2]
    far = lax.ppermute(first, "chain", Z_FAR)
    second = jnp.where(z == 2, far, first)
    near = lax.ppermute(second, "chain", Z_NEAR)
    return jnp.where((z == 1) | (z == 3), near, second)


def across(mine):
    cut = mine.shape[1] // 2
    other = lax.ppermute(mine[:, cut:], "chain", CORE)
    return jnp.where(place()[4] == 0, mine[:, :cut], other)


def gather(half):
    return lax.all_gather(half, "chain", axis_index_groups=ROWS, axis=0)


def product_kernel(layer, flags, x_ref, g_ref, own_ref, src_ref, plus_ref, minus_ref, keep_ref, scaled):
    j = pl.program_id(0)
    held = flags[layer] > 0
    cut = x_ref.shape[0] // 2

    @pl.when(j == 0)
    def _():
        gain = jnp.where(held, g_ref[layer:layer + 1, :].astype(jnp.float32), 1.0)
        scaled[...] = (x_ref[...].astype(jnp.float32) * gain).astype(LOW)

    def put(weights):
        total = dot(scaled[...], weights).astype(LOW)
        low, high = total[:cut], total[cut:]

        @pl.when(j == 0)
        def _():
            plus_ref[0] = low
            minus_ref[0] = high

        @pl.when(j == 1)
        def _():
            plus_ref[1] = high
            keep_ref[0] = low

        @pl.when(j == 2)
        def _():
            minus_ref[1] = low
            keep_ref[1] = high

        @pl.when(j == 3)
        def _():
            keep_ref[2] = low
            keep_ref[3] = high

    @pl.when(held)
    def _():
        put(own_ref[...])

    @pl.when(jnp.logical_not(held))
    def _():
        put(src_ref[...].reshape(own_ref.shape))


def product(flags, x, gain, own, layer, src, which):
    tokens, depth = x.shape
    first = COLUMNS + which * NX

    def whole(*shape):
        return pl.BlockSpec(shape, lambda j, f: (0,) * len(shape))

    shapes = [(2, tokens // 2, WIDE), (2, tokens // 2, WIDE), (4, tokens // 2, WIDE)]
    return pl.pallas_call(
        functools.partial(product_kernel, layer),
        out_shape=tuple(jax.ShapeDtypeStruct(shape, LOW) for shape in shapes),
        grid_spec=pltpu.PrefetchScalarGridSpec(
            num_scalar_prefetch=1,
            grid=(NX,),
            in_specs=[
                whole(tokens, depth),
                pl.BlockSpec((None, LAYERS, depth), lambda j, f: (0, 0, 0)),
                pl.BlockSpec((None, None, depth, WIDE), lambda j, f: (0, layer, 0, f[first + j * f[layer]])),
                pl.BlockSpec((2 * NY, None, depth // (2 * NY), WIDE), lambda j, f: (0, layer, 0, f[first + j * (1 - f[layer])] % NX)),
            ],
            out_specs=tuple(whole(*shape) for shape in shapes),
            scratch_shapes=[pltpu.VMEM((tokens, depth), LOW)],
        ),
        compiler_params=pltpu.CompilerParams(vmem_limit_bytes=VMEM),
        cost_estimate=pl.CostEstimate(
            flops=2 * tokens * depth * WIDE * NX,
            bytes_accessed=2 * (tokens * depth + NX * WIDE * (depth + tokens)),
            transcendentals=0,
        ),
    )(flags, x, gain, own, src)


def add(*terms):
    return sum(t.astype(jnp.float32) for t in terms)


def round_x(plus, minus, keep):
    plus1 = lax.ppermute(plus, "tp", X_NEXT)
    minus1 = lax.ppermute(minus, "tp", X_LAST)
    plus2 = lax.ppermute(add(keep[0], plus1[0]).astype(LOW), "tp", X_NEXT)
    minus2 = lax.ppermute(add(keep[1], minus1[0]).astype(LOW), "tp", X_LAST)
    return keep, plus1, minus1, plus2, minus2


def swapped(keep, plus1, minus1, plus2, minus2):
    low = add(keep[2], plus2, minus1[1])
    high = add(keep[3], minus2, plus1[1])
    return lax.ppermute(jnp.stack([low, high]).astype(LOW), "tp", H_SWAP)


def close_kernel(keep_ref, plus1, minus1, plus2, minus2, came_ref, cos_ref, sin_ref, scale_ref, *refs):
    out_ref = refs[-1]
    cut = keep_ref.shape[1]
    for i, (one, two) in enumerate(((minus1, plus2), (plus1, minus2))):
        rows = slice(i * cut, (i + 1) * cut)
        total = add(keep_ref[2 + i], one[1], two[...], came_ref[i])
        key = total[:, :HD]
        turned = key * cos_ref[rows, :] + pltpu.roll(key, HD // 2, 1) * sin_ref[rows, :]
        out_ref[rows, :HD] = turned.astype(LOW)
        out_ref[rows, HD:] = (total[:, HD:] * scale_ref[rows, :]).astype(LOW)


def close(layer, terms, came, turns, out):
    tokens = turns[0].shape[0]
    args = [*terms, came, *turns]
    in_specs = [pl.BlockSpec(a.shape, lambda i, n=a.ndim: (0,) * n) for a in args]
    aliases = {}
    if out is not None:
        aliases = {len(args): 0}
        args.append(out)
        in_specs.append(pl.BlockSpec(memory_space=pl.ANY))
    return pl.pallas_call(
        close_kernel,
        out_shape=jax.ShapeDtypeStruct((LAYERS, tokens, WIDE), LOW),
        grid=(1,),
        in_specs=in_specs,
        out_specs=pl.BlockSpec((None, tokens, WIDE), lambda i: (layer, 0, 0)),
        input_output_aliases=aliases,
        compiler_params=pltpu.CompilerParams(vmem_limit_bytes=VMEM),
        cost_estimate=pl.CostEstimate(flops=8 * tokens * WIDE, bytes_accessed=16 * tokens * WIDE, transcendentals=0),
    )(*args)


def flags_of(loaded_layers):
    h, x = place()[:2]
    flags = [(loaded_layers[0] > layer).astype(jnp.int32) for layer in range(LAYERS)]
    flags += [row * NX + (x + d) % NX for row in (1 - h, h) for d in (2, 1, 3, 0)]
    return jnp.stack(flags).astype(jnp.int32)


def turns_of(squares, width, positions):
    scale = lax.rsqrt(squares / width + 1e-05)[:, :, None]
    half = HD // 2
    freq = 500000.0 ** (-2.0 * jnp.arange(half, dtype=jnp.float32) / HD)
    angle = positions.astype(jnp.float32)[:, None] * freq[None, :]
    cosine, sine = jnp.cos(angle), jnp.sin(angle)
    cosine, sine = jnp.concatenate([cosine, cosine], 1), jnp.concatenate([-sine, sine], 1)
    return [(cosine * s, sine * s, jnp.broadcast_to(s, cosine.shape)) for s in scale]


def shards(hidden_first, hidden_second, weight_buffer, gain_buffer, loaded_layers, positions):
    inputs = (hidden_first, hidden_second)
    width = hidden_first.shape[1] * lax.axis_size("tp")
    flags = flags_of(loaded_layers)
    swap_parts = pieces(flags, weight_buffer, gain_buffer, 0)
    swap = scatter(swap_parts)
    keep_parts = pieces(flags, weight_buffer, gain_buffer, 1)
    squares = jnp.stack([jnp.sum(jnp.square(v.astype(jnp.float32)), axis=1) for v in inputs])

    swap, keep_parts, squares = lax.optimization_barrier((swap, keep_parts, squares))
    keep = scatter(keep_parts)
    swap = down(swap)
    swap, keep, squares = lax.optimization_barrier((swap, keep, squares))
    swap_half = across(swap)
    swap_src = gather(swap_half)
    keep = down(after(keep, swap_half))
    for pairs in (X_ONE, X_TWO, H_SWAP):
        squares = squares + lax.ppermute(squares, "tp", pairs)
    turns = turns_of(squares, width, positions)
    keep, turns = lax.optimization_barrier((keep, turns))
    keep_src = gather(across(keep))

    def sums(layer, src, which):
        return product(flags, inputs[layer], gain_buffer, weight_buffer, layer, src, which)

    came = [swapped(*round_x(*sums(layer, swap_src, 0))) for layer in range(LAYERS)]
    out = None
    for layer in range(LAYERS):
        out = close(layer, round_x(*sums(layer, keep_src, 1)), came[layer], turns[layer], out)
    return out


def solution(mesh):
    placed = (
        P("chain", "tp"),
        P("chain", "tp"),
        P("chain", None, "tp", None),
        P("chain", None, "tp"),
        P("chain"),
        P("chain"),
    )
    return jax.shard_map(
        shards, mesh=mesh, in_specs=placed, out_specs=P(None, "chain", "tp"), check_vma=False
    )
```

time: 577 us -> 219 us (0.38)
  waiting for transfers between devices: 430 us -> 69 us
  blocking collectives: 97.1 us -> 0 us
  starting transfers between devices: 0.09 us -> 66.3 us
  Pallas kernels: 0 us -> 47.3 us
  matrix products: 20.3 us -> 0 us
    psum x1 -> x0, waiting for transfers between devices: 230 us -> none  [spread(): return lax.psum(block, axis)]
    reduce_scatter x2 -> x0, waiting for transfers between devices: 200 us -> none  [layer_rows(): lax.psum_scatter(term.astype(jnp.bfloat16), 'tp', scatter_dimension=1, ti...]
    psum x2 -> x0, blocking collectives: 97.1 us -> none  [the longest x1 70.6 us: spread(): return lax.psum(block, axis)]
    ppermute x0 -> x33, waiting for transfers between devices: none -> 69 us  [the longest x6 20.7 us: scatter(): lax.ppermute(parts[k], 'chain', from_source(k))]
    ppermute x0 -> x33, starting transfers between devices: none -> 66.3 us  [the longest x6 19.8 us: scatter(): lax.ppermute(parts[k], 'chain', from_source(k))]
    pallas_call x0 -> x8, Pallas kernels: none -> 47.3 us  [the longest x4 29.6 us: product(): pl.pallas_call(functools.partial(product_kernel, layer), out_shape=tuple(...]
    dot_general x2 -> x0, matrix products: 20.3 us -> none  [layer_rows(): partial_value = jnp.dot(scaled, weights, preferred_element_type=jnp.float32)]
  transfers between devices with their start and end apart: 3 -> 35, of which waited for: 3 -> 17; matrix products, arithmetic and copies ran while one was open for 2% -> 6% of each run, Pallas kernels for 0% -> 18%
where the time goes in v3:
time: 219 us; the launch traced here: 215 us
  waiting for transfers between devices  69 us (32%)
  starting transfers between devices  66.3 us (30%)
  Pallas kernels  47.3 us (22%)
  between operations  14.4 us (7%)
  other arithmetic  13.2 us (6%)
  local copies, waits for them, and re-layouts  4.91 us (2%)
    pallas_call x4, Pallas kernels, product(): pl.pallas_call(functools.partial(product_kernel, layer), out_shape=tuple(...  29.6 us
    ppermute x6, waiting for transfers between devices, scatter(): lax.ppermute(parts[k], 'chain', from_source(k))  20.7 us
    ppermute x6, starting transfers between devices, scatter(): lax.ppermute(parts[k], 'chain', from_source(k))  19.8 us
    ppermute x4, waiting for transfers between devices, round_x(): plus1 = lax.ppermute(plus, 'tp', X_NEXT)  14.4 us
    ppermute x2, waiting for transfers between devices, down(): far = lax.ppermute(first, 'chain', Z_FAR)  13.8 us
    pallas_call x2, Pallas kernels, pieces(): pl.pallas_call(pieces_kernel, out_shape=tuple((jax.ShapeDtypeStruct((LAYE...  11.1 us
    ppermute x3, starting transfers between devices, shards(): squares = squares + lax.ppermute(squares, 'tp', pairs)  9.51 us
    ppermute x3, waiting for transfers between devices, shards(): squares = squares + lax.ppermute(squares, 'tp', pairs)  8.84 us
  transfers between devices with their start and end apart: 35, of which 17 were waited for; matrix products, arithmetic and copies ran while one was open for 6% of the time, Pallas kernels for 18%

profile of v3, /device:TPU:6, one launch (start us, length us, event | category | flops | bytes accessed | tf_op | source)
XLA Modules:
  0.0 215.1 jit_solution(3343063380943112566)
XLA Ops:
  7.8 5.6 %shard_map.64 = (bf16[2,256,1024]{2,1,0:T(8,128)(2,1)}, bf16[2,256,1024]{2,1,0:T(8,128)(2,1)}, bf16[2,256,1024]{2,1,0:T(8,128)(2,1)}, bf16[2,256,1024]{2,1,0:T(8,128)(2,1)}) custom-call(s32[10]{0:T(128)} %stack.70.flags, bf16[1,2,1024,2048]{3,2,1,0:T(8,128)(2,1)} %own_ref.7, bf16[1,2,1024]{2,1,0:T(2,128)(2,1)} %g_ref.11), custom_call_target="tpu_custom_call" | custom-call | flops 2097152 | bytes 8388608 | tf_op jit(solution)/shard_map/pallas_call | solution.py:81
  13.4 3.5 %collective-permute-start = (bf16[2,256,1024]{2,1,0:T(8,128)(2,1)}, bf16[2,256,1024]{2,1,0:T(8,128)(2,1)S(1)}, u32[]{:S(2)}, u32[]{:S(2)}) collective-permute-start(bf16[2,256,1024]{2,1,0:T(8,128)(2,1)} %get-tuple-element.43), channel_id=1, source_target_pairs={{0,16},{1,17},{2,18},{3,19},{4,20},{5,21},{6,22},{7,23}} | collective-permute-start | bytes 3145736 | tf_op jit(solution)/shard_map/ppermute | solution.py:102
  17.0 3.3 %collective-permute-start.1 = (bf16[2,256,1024]{2,1,0:T(8,128)(2,1)}, bf16[2,256,1024]{2,1,0:T(8,128)(2,1)}, u32[]{:S(2)}, u32[]{:S(2)}) collective-permute-start(bf16[2,256,1024]{2,1,0:T(8,128)(2,1)} %get-tuple-element.44), channel_id=1, source_target_pairs={{0,32},{1,33},{2,34},{3,35},{4,36},{5,37},{6,38},{7,39}} | collective-permute-start | bytes 3145736 | tf_op jit(solution)/shard_map/ppermute | solution.py:102
  20.2 2.3 %collective-permute-start.2 = (bf16[2,256,1024]{2,1,0:T(8,128)(2,1)}, bf16[2,256,1024]{2,1,0:T(8,128)(2,1)}, u32[]{:S(2)}, u32[]{:S(2)}) collective-permute-start(bf16[2,256,1024]{2,1,0:T(8,128)(2,1)} %get-tuple-element.45), channel_id=1, source_target_pairs={{0,48},{1,49},{2,50},{3,51},{4,52},{5,53},{6,54},{7,55}} | collective-permute-start | bytes 3145736 | tf_op jit(solution)/shard_map/ppermute | solution.py:102
  22.9 1.9 multiply_reduce_fusion
  24.9 5.6 %shard_map.65 = (bf16[2,256,1024]{2,1,0:T(8,128)(2,1)}, bf16[2,256,1024]{2,1,0:T(8,128)(2,1)}, bf16[2,256,1024]{2,1,0:T(8,128)(2,1)}, bf16[2,256,1024]{2,1,0:T(8,128)(2,1)}) custom-call(s32[10]{0:T(128)} %stack.70.flags, bf16[1,2,1024,2048]{3,2,1,0:T(8,128)(2,1)} %own_ref.7, bf16[1,2,1024]{2,1,0:T(2,128)(2,1)} %g_ref.11), custom_call_target="tpu_custom_call" | custom-call | flops 2097152 | bytes 8388608 | tf_op jit(solution)/shard_map/pallas_call | solution.py:81
  30.4 10.3 %collective-permute-done.1 = bf16[2,256,1024]{2,1,0:T(8,128)(2,1)} collective-permute-done((bf16[2,256,1024]{2,1,0:T(8,128)(2,1)}, bf16[2,256,1024]{2,1,0:T(8,128)(2,1)}, u32[]{:S(2)}, u32[]{:S(2)}) %collective-permute-start.1) | collective-permute-done | bytes 1048608 | tf_op jit(solution)/shard_map/ppermute | solution.py:102
  40.7 1.4 select_select_fusion.1
  42.2 1.4 collective-permute-start.3
  43.5 2.3 %collective-permute-start.5 = (bf16[2,256,1024]{2,1,0:T(8,128)(2,1)}, bf16[2,256,1024]{2,1,0:T(8,128)(2,1)}, u32[]{:S(2)}, u32[]{:S(2)}) collective-permute-start(bf16[2,256,1024]{2,1,0:T(8,128)(2,1)} %get-tuple-element.52), channel_id=1, source_target_pairs={{0,16},{1,17},{2,18},{3,19},{4,20},{5,21},{6,22},{7,23}} | collective-permute-start | bytes 3145736 | tf_op jit(solution)/shard_map/ppermute | solution.py:102
  45.8 6.2 %collective-permute-start.6 = (bf16[2,256,1024]{2,1,0:T(8,128)(2,1)}, bf16[2,256,1024]{2,1,0:T(8,128)(2,1)}, u32[]{:S(2)}, u32[]{:S(2)}) collective-permute-start(bf16[2,256,1024]{2,1,0:T(8,128)(2,1)} %get-tuple-element.53), channel_id=1, source_target_pairs={{0,32},{1,33},{2,34},{3,35},{4,36},{5,37},{6,38},{7,39}} | collective-permute-start | bytes 3145736 | tf_op jit(solution)/shard_map/ppermute | solution.py:102
  52.1 2.3 %collective-permute-start.7 = (bf16[2,256,1024]{2,1,0:T(8,128)(2,1)}, bf16[2,256,1024]{2,1,0:T(8,128)(2,1)}, u32[]{:S(2)}, u32[]{:S(2)}) collective-permute-start(bf16[2,256,1024]{2,1,0:T(8,128)(2,1)} %get-tuple-element.54), channel_id=1, source_target_pairs={{0,48},{1,49},{2,50},{3,51},{4,52},{5,53},{6,54},{7,55}} | collective-permute-start | bytes 3145736 | tf_op jit(solution)/shard_map/ppermute | solution.py:102
  54.3 1.4 collective-permute-done.3
  55.9 2.4 %collective-permute-start.4 = (bf16[2,256,1024]{2,1,0:T(8,128)(2,1)S(1)}, bf16[2,256,1024]{2,1,0:T(8,128)(2,1)}, u32[]{:S(2)}, u32[]{:S(2)}) collective-permute-start(bf16[2,256,1024]{2,1,0:T(8,128)(2,1)S(1)} %broadcast_select_fusion.1), channel_id=1, source_target_pairs={{0,64},{16,80},{32,96},{48,112},{128,192},{144,208},{160,224},{176... | collective-permute-start | bytes 3145736 | tf_op jit(solution)/shard_map/ppermute | solution.py:110
  58.2 10.4 %collective-permute-done.6 = bf16[2,256,1024]{2,1,0:T(8,128)(2,1)} collective-permute-done((bf16[2,256,1024]{2,1,0:T(8,128)(2,1)}, bf16[2,256,1024]{2,1,0:T(8,128)(2,1)}, u32[]{:S(2)}, u32[]{:S(2)}) %collective-permute-start.6) | collective-permute-done | bytes 1048608 | tf_op jit(solution)/shard_map/ppermute | solution.py:102
  68.7 1.7 select_select_fusion
  70.6 1.3 collective-permute-start.8
  71.9 1.5 collective-permute-done.8
  73.4 0.8 slice_select_fusion.1
  74.3 4.4 %collective-permute-start.9 = (bf16[2,256,1024]{2,1,0:T(8,128)(2,1)S(1)}, bf16[2,256,1024]{2,1,0:T(8,128)(2,1)S(1)}, u32[]{:S(2)}, u32[]{:S(2)}) collective-permute-start(bf16[2,256,1024]{2,1,0:T(8,128)(2,1)S(1)} %select_select_fusion), channel_id=1, source_target_pairs={{0,128},{16,144},{32,160},{48,176},{1,129},{17,145},{33,161},{49,1... | collective-permute-start | bytes 3145736 | tf_op jit(solution)/shard_map/ppermute | solution.py:108
  78.7 12.4 %collective-permute-done.9 = bf16[2,256,1024]{2,1,0:T(8,128)(2,1)S(1)} collective-permute-done((bf16[2,256,1024]{2,1,0:T(8,128)(2,1)S(1)}, bf16[2,256,1024]{2,1,0:T(8,128)(2,1)S(1)}, u32[]{:S(2)}, u32[]{:S(2)}) %collective-permute-start.9) | collective-permute-done | bytes 1048608 | tf_op jit(solution)/shard_map/ppermute | solution.py:108
  91.3 1.4 collective-permute-start.10
  92.6 0.9 collective-permute-start.11
  93.6 2.8 %collective-permute-done.11 = f32[2,896]{1,0:T(2,128)S(1)} collective-permute-done((f32[2,896]{1,0:T(2,128)S(1)}, f32[2,896]{1,0:T(2,128)S(1)}, u32[]{:S(2)}, u32[]{:S(2)}) %collective-permute-start.11) | collective-permute-done | bytes 7200 | tf_op jit(solution)/shard_map/ppermute | solution.py:284
  96.4 1.4 collective-permute-start.12
  97.8 3.7 %collective-permute-done.12 = f32[2,896]{1,0:T(2,128)S(1)} collective-permute-done((f32[2,896]{1,0:T(2,128)S(1)}, f32[2,896]{1,0:T(2,128)S(1)}, u32[]{:S(2)}, u32[]{:S(2)}) %collective-permute-start.12) | collective-permute-done | bytes 7200 | tf_op jit(solution)/shard_map/ppermute | solution.py:284
  101.5 7.2 %collective-permute-start.13 = (f32[2,896]{1,0:T(2,128)S(1)}, f32[2,896]{1,0:T(2,128)S(1)}, u32[]{:S(2)}, u32[]{:S(2)}) collective-permute-start(f32[2,896]{1,0:T(2,128)S(1)} %add.157), channel_id=1, source_target_pairs={{0,4},{1,5},{2,6},{3,7},{4,0},{5,1},{6,2},{7,3},{8,12},{9,13},{10,... | collective-permute-start | bytes 21512 | tf_op jit(solution)/shard_map/ppermute | solution.py:284
  108.7 1.7 fusion.18
  110.4 2.3 %collective-permute-done.13 = f32[2,896]{1,0:T(2,128)S(1)} collective-permute-done((f32[2,896]{1,0:T(2,128)S(1)}, f32[2,896]{1,0:T(2,128)S(1)}, u32[]{:S(2)}, u32[]{:S(2)}) %collective-permute-start.13) | collective-permute-done | bytes 7200 | tf_op jit(solution)/shard_map/ppermute | solution.py:284
  112.7 1.8 fusion.4
  114.6 1.0 mul.66.scale_ref
  115.6 0.9 mul.70.scale_ref
  116.6 1.3 collective-permute-start.14
  118.0 1.5 collective-permute-done.14
  119.4 0.9 slice_select_fusion
  120.4 7.4 %shard_map.69 = (bf16[2,448,256]{2,1,0:T(8,128)(2,1)}, bf16[2,448,256]{2,1,0:T(8,128)(2,1)}, bf16[4,448,256]{2,1,0:T(8,128)(2,1)}) custom-call(s32[10]{0:T(128)} %stack.70.flags, bf16[896,1024]{1,0:T(8,128)(2,1)} %x_ref.7, bf16[1,2,1024]{2,1,0:T(2,128)(2,1)} %g_ref.11, bf16[1,2,1024,2048]{3,2,1,0:T(8,128)(2,1)} %own_ref.7, bf16[8,2,128,1024]{3,2,1,0:T(8,128)(2,1)} %bitcast.66), custom_call_target="tpu_custom_call" | custom-call | flops 1879048192 | bytes 5767168 | tf_op jit(solution)/shard_map/pallas_call | solution.py:175
  128.3 1.5 collective-permute-start.30
  129.8 7.4 %shard_map.67 = (bf16[2,448,256]{2,1,0:T(8,128)(2,1)}, bf16[2,448,256]{2,1,0:T(8,128)(2,1)}, bf16[4,448,256]{2,1,0:T(8,128)(2,1)}) custom-call(s32[10]{0:T(128)} %stack.70.flags, bf16[896,1024]{1,0:T(8,128)(2,1)} %x_ref.5, bf16[1,2,1024]{2,1,0:T(2,128)(2,1)} %g_ref.11, bf16[1,2,1024,2048]{3,2,1,0:T(8,128)(2,1)} %own_ref.7, bf16[8,2,128,1024]{3,2,1,0:T(8,128)(2,1)} %bitcast.67), custom_call_target="tpu_custom_call" | custom-call | flops 1879048192 | bytes 5767168 | tf_op jit(solution)/shard_map/pallas_call | solution.py:175
  137.2 1.8 collective-permute-start.19
  139.3 2.1 collective-permute-done.28
  141.3 0.9 collective-permute-done.30
  142.3 1.1 collective-permute-start.29
  143.4 1.0 collective-permute-start.31
  144.4 6.8 %collective-permute-done.19 = bf16[2,448,256]{2,1,0:T(8,128)(2,1)S(1)} collective-permute-done((bf16[2,448,256]{2,1,0:T(8,128)(2,1)}, bf16[2,448,256]{2,1,0:T(8,128)(2,1)S(1)}, u32[]{:S(2)}, u32[]{:S(2)}) %collective-permute-start.19) | collective-permute-done | bytes 458784 | tf_op jit(solution)/shard_map/ppermute | solution.py:204
  151.2 2.8 %collective-permute-done.21 = bf16[2,448,256]{2,1,0:T(8,128)(2,1)S(1)} collective-permute-done((bf16[2,448,256]{2,1,0:T(8,128)(2,1)}, bf16[2,448,256]{2,1,0:T(8,128)(2,1)S(1)}, u32[]{:S(2)}, u32[]{:S(2)}) %collective-permute-start.21) | collective-permute-done | bytes 458784 | tf_op jit(solution)/shard_map/ppermute | solution.py:205
  153.9 1.2 fusion.8
  155.2 2.0 collective-permute-start.22
  157.2 0.8 collective-permute-done.31
  158.2 3.4 %collective-permute-start.32 = (bf16[2,448,256]{2,1,0:T(8,128)(2,1)S(1)}, bf16[2,448,256]{2,1,0:T(8,128)(2,1)S(1)}, u32[]{:S(2)}, u32[]{:S(2)}) collective-permute-start(bf16[2,448,256]{2,1,0:T(8,128)(2,1)S(1)} %pad_maximum_fusion.3), channel_id=1, source_target_pairs={{0,4},{1,5},{2,6},{3,7},{4,0},{5,1},{6,2},{7,3},{8,12},{9,13},{10,... | collective-permute-start | bytes 1376264 | tf_op jit(solution)/shard_map/ppermute | solution.py:214
  161.7 7.4 %shard_map.68 = (bf16[2,448,256]{2,1,0:T(8,128)(2,1)}, bf16[2,448,256]{2,1,0:T(8,128)(2,1)}, bf16[4,448,256]{2,1,0:T(8,128)(2,1)}) custom-call(s32[10]{0:T(128)} %stack.70.flags, bf16[896,1024]{1,0:T(8,128)(2,1)} %x_ref.7, bf16[1,2,1024]{2,1,0:T(2,128)(2,1)} %g_ref.11, bf16[1,2,1024,2048]{3,2,1,0:T(8,128)(2,1)} %own_ref.7, bf16[8,2,128,1024]{3,2,1,0:T(8,128)(2,1)} %bitcast.68), custom_call_target="tpu_custom_call" | custom-call | flops 1879048192 | bytes 5767168 | tf_op jit(solution)/shard_map/pallas_call | solution.py:175
  169.7 1.5 collective-permute-start.25
  171.1 7.4 %shard_map.66 = (bf16[2,448,256]{2,1,0:T(8,128)(2,1)}, bf16[2,448,256]{2,1,0:T(8,128)(2,1)}, bf16[4,448,256]{2,1,0:T(8,128)(2,1)}) custom-call(s32[10]{0:T(128)} %stack.70.flags, bf16[896,1024]{1,0:T(8,128)(2,1)} %x_ref.5, bf16[1,2,1024]{2,1,0:T(2,128)(2,1)} %g_ref.11, bf16[1,2,1024,2048]{3,2,1,0:T(8,128)(2,1)} %own_ref.7, bf16[8,2,128,1024]{3,2,1,0:T(8,128)(2,1)} %bitcast.69), custom_call_target="tpu_custom_call" | custom-call | flops 1879048192 | bytes 5767168 | tf_op jit(solution)/shard_map/pallas_call | solution.py:175
  178.5 1.8 collective-permute-start.15
  180.9 2.7 %collective-permute-start.23 = (bf16[2,448,256]{2,1,0:T(8,128)(2,1)S(1)}, bf16[2,448,256]{2,1,0:T(8,128)(2,1)S(1)}, u32[]{:S(2)}, u32[]{:S(2)}) collective-permute-start(bf16[2,448,256]{2,1,0:T(8,128)(2,1)S(1)} %pad_maximum_fusion.2), channel_id=1, source_target_pairs={{0,4},{1,5},{2,6},{3,7},{4,0},{5,1},{6,2},{7,3},{8,12},{9,13},{10,... | collective-permute-start | bytes 1376264 | tf_op jit(solution)/shard_map/ppermute | solution.py:214
  183.7 3.0 %collective-permute-start.26 = (bf16[448,256]{1,0:T(8,128)(2,1)S(1)}, bf16[448,256]{1,0:T(8,128)(2,1)S(1)}, u32[]{:S(2)}, u32[]{:S(2)}) collective-permute-start(bf16[448,256]{1,0:T(8,128)(2,1)S(1)} %get-tuple-element.86), channel_id=1, source_target_pairs={{0,1},{1,2},{2,3},{3,0},{4,5},{5,6},{6,7},{7,4},{8,9},{9,10},{10,1... | collective-permute-start | bytes 688136 | tf_op jit(solution)/shard_map/ppermute | solution.py:206
  186.7 5.6 %collective-permute-done.15.plus1 = bf16[2,448,256]{2,1,0:T(8,128)(2,1)S(1)} collective-permute-done((bf16[2,448,256]{2,1,0:T(8,128)(2,1)}, bf16[2,448,256]{2,1,0:T(8,128)(2,1)S(1)}, u32[]{:S(2)}, u32[]{:S(2)}) %collective-permute-start.15) | collective-permute-done | bytes 458784 | tf_op jit(solution)/shard_map/ppermute | solution.py:204
  192.7 3.1 %collective-permute-start.17 = (bf16[448,256]{1,0:T(8,128)(2,1)S(1)}, bf16[448,256]{1,0:T(8,128)(2,1)S(1)}, u32[]{:S(2)}, u32[]{:S(2)}) collective-permute-start(bf16[448,256]{1,0:T(8,128)(2,1)S(1)} %get-tuple-element.92), channel_id=1, source_target_pairs={{0,1},{1,2},{2,3},{3,0},{4,5},{5,6},{6,7},{7,4},{8,9},{9,10},{10,1... | collective-permute-start | bytes 688136 | tf_op jit(solution)/shard_map/ppermute | solution.py:206
  195.7 1.0 collective-permute-done.26.plus2
  196.7 2.8 %collective-permute-done.27.minus2 = bf16[448,256]{1,0:T(8,128)(2,1)S(1)} collective-permute-done((bf16[448,256]{1,0:T(8,128)(2,1)S(1)}, bf16[448,256]{1,0:T(8,128)(2,1)S(1)}, u32[]{:S(2)}, u32[]{:S(2)}) %collective-permute-start.27) | collective-permute-done | bytes 229408 | tf_op jit(solution)/shard_map/ppermute | solution.py:207
  199.5 0.7 copy-done.15
  200.2 3.3 %shard_map.70.refs_0_ = bf16[2,896,256]{2,1,0:T(8,128)(2,1)} custom-call(bf16[4,448,256]{2,1,0:T(8,128)(2,1)} %get-tuple-element.70.keep_ref, bf16[2,448,256]{2,1,0:T(8,128)(2,1)} %copy-done.5, bf16[2,448,256]{2,1,0:T(8,128)(2,1)} %copy-done.6, bf16[448,256]{1,0:T(8,128)(2,1)} %copy-done.13, bf16[448,256]{1,0:T(8,128)(2,1)} %copy-done.15, ...), custom_call_target="tpu_custom_call" | custom-call | flops 1835008 | bytes 3670016 | tf_op jit(solution)/shard_map/pallas_call | solution.py:238
  203.5 0.7 copy-done.11
  204.3 0.7 copy-done.14
  205.0 3.3 %shard_map.71 = bf16[2,896,256]{2,1,0:T(8,128)(2,1)} custom-call(bf16[4,448,256]{2,1,0:T(8,128)(2,1)} %get-tuple-element.61.keep_ref, bf16[2,448,256]{2,1,0:T(8,128)(2,1)} %copy-done.4, bf16[2,448,256]{2,1,0:T(8,128)(2,1)} %copy-done.7, bf16[448,256]{1,0:T(8,128)(2,1)} %copy-done.12, bf16[448,256]{1,0:T(8,128)(2,1)} %copy-done.14, ...), custom_call_target="tpu_custom_call", output_to_operand_aliasing={{}: (9, {})} | custom-call | flops 1835008 | bytes 3670016 | tf_op jit(solution)/shard_map/pallas_call | solution.py:238
  (84 shorter events, 4.6 us)
Async XLA Ops:
  6.5 113.8 %all-gather.7.cloned.1.call-start = ((), (), s32[]{:S(2)}) async-start(), calls=%async_computation.1 | async-start | bytes 4718592 | tf_op jit(solution)/shard_map/all_gather | solution.py:121
  7.8 14.6 %copy-start = (bf16[896,1024]{1,0:T(8,128)(2,1)S(1)}, bf16[896,1024]{1,0:T(8,128)(2,1)}, u32[]{:S(2)}) copy-start(bf16[896,1024]{1,0:T(8,128)(2,1)} %x_ref.7) | copy-start | bytes 5505028
  13.4 17.0 %collective-permute-start = (bf16[2,256,1024]{2,1,0:T(8,128)(2,1)}, bf16[2,256,1024]{2,1,0:T(8,128)(2,1)S(1)}, u32[]{:S(2)}, u32[]{:S(2)}) collective-permute-start(bf16[2,256,1024]{2,1,0:T(8,128)(2,1)} %get-tuple-element.43), channel_id=1, source_target_pairs={{0,16},{1,17},{2,18},{3,19},{4,20},{5,21},{6,22},{7,23}} | collective-permute-start | bytes 3145736 | tf_op jit(solution)/shard_map/ppermute | solution.py:102
  17.0 23.8 %collective-permute-start.1 = (bf16[2,256,1024]{2,1,0:T(8,128)(2,1)}, bf16[2,256,1024]{2,1,0:T(8,128)(2,1)}, u32[]{:S(2)}, u32[]{:S(2)}) collective-permute-start(bf16[2,256,1024]{2,1,0:T(8,128)(2,1)} %get-tuple-element.44), channel_id=1, source_target_pairs={{0,32},{1,33},{2,34},{3,35},{4,36},{5,37},{6,38},{7,39}} | collective-permute-start | bytes 3145736 | tf_op jit(solution)/shard_map/ppermute | solution.py:102
  20.2 20.5 %collective-permute-start.2 = (bf16[2,256,1024]{2,1,0:T(8,128)(2,1)}, bf16[2,256,1024]{2,1,0:T(8,128)(2,1)}, u32[]{:S(2)}, u32[]{:S(2)}) collective-permute-start(bf16[2,256,1024]{2,1,0:T(8,128)(2,1)} %get-tuple-element.45), channel_id=1, source_target_pairs={{0,48},{1,49},{2,50},{3,51},{4,52},{5,53},{6,54},{7,55}} | collective-permute-start | bytes 3145736 | tf_op jit(solution)/shard_map/ppermute | solution.py:102
  24.8 15.9 %copy-start.3 = (bf16[2,256,1024]{2,1,0:T(8,128)(2,1)S(1)}, bf16[2,256,1024]{2,1,0:T(8,128)(2,1)}, u32[]{:S(2)}) copy-start(bf16[2,256,1024]{2,1,0:T(8,128)(2,1)} %get-tuple-element.42) | copy-start | bytes 3145732
  42.2 13.6 %collective-permute-start.3 = (bf16[2,256,1024]{2,1,0:T(8,128)(2,1)S(1)}, bf16[2,256,1024]{2,1,0:T(8,128)(2,1)S(1)}, u32[]{:S(2)}, u32[]{:S(2)}) collective-permute-start(bf16[2,256,1024]{2,1,0:T(8,128)(2,1)S(1)} %select_select_fusion.1), channel_id=1, source_target_pairs={{0,128},{16,144},{32,160},{48,176},{1,129},{17,145},{33,161},{49,1... | collective-permute-start | bytes 3145736 | tf_op jit(solution)/shard_map/ppermute | solution.py:108
  43.5 14.7 %collective-permute-start.5 = (bf16[2,256,1024]{2,1,0:T(8,128)(2,1)}, bf16[2,256,1024]{2,1,0:T(8,128)(2,1)}, u32[]{:S(2)}, u32[]{:S(2)}) collective-permute-start(bf16[2,256,1024]{2,1,0:T(8,128)(2,1)} %get-tuple-element.52), channel_id=1, source_target_pairs={{0,16},{1,17},{2,18},{3,19},{4,20},{5,21},{6,22},{7,23}} | collective-permute-start | bytes 3145736 | tf_op jit(solution)/shard_map/ppermute | solution.py:102
  45.8 22.9 %collective-permute-start.6 = (bf16[2,256,1024]{2,1,0:T(8,128)(2,1)}, bf16[2,256,1024]{2,1,0:T(8,128)(2,1)}, u32[]{:S(2)}, u32[]{:S(2)}) collective-permute-start(bf16[2,256,1024]{2,1,0:T(8,128)(2,1)} %get-tuple-element.53), channel_id=1, source_target_pairs={{0,32},{1,33},{2,34},{3,35},{4,36},{5,37},{6,38},{7,39}} | collective-permute-start | bytes 3145736 | tf_op jit(solution)/shard_map/ppermute | solution.py:102
  52.1 16.6 %collective-permute-start.7 = (bf16[2,256,1024]{2,1,0:T(8,128)(2,1)}, bf16[2,256,1024]{2,1,0:T(8,128)(2,1)}, u32[]{:S(2)}, u32[]{:S(2)}) collective-permute-start(bf16[2,256,1024]{2,1,0:T(8,128)(2,1)} %get-tuple-element.54), channel_id=1, source_target_pairs={{0,48},{1,49},{2,50},{3,51},{4,52},{5,53},{6,54},{7,55}} | collective-permute-start | bytes 3145736 | tf_op jit(solution)/shard_map/ppermute | solution.py:102
  55.9 14.5 %collective-permute-start.4 = (bf16[2,256,1024]{2,1,0:T(8,128)(2,1)S(1)}, bf16[2,256,1024]{2,1,0:T(8,128)(2,1)}, u32[]{:S(2)}, u32[]{:S(2)}) collective-permute-start(bf16[2,256,1024]{2,1,0:T(8,128)(2,1)S(1)} %broadcast_select_fusion.1), channel_id=1, source_target_pairs={{0,64},{16,80},{32,96},{48,112},{128,192},{144,208},{160,224},{176... | collective-permute-start | bytes 3145736 | tf_op jit(solution)/shard_map/ppermute | solution.py:110
  70.5 27.2 %copy-start.16 = (s32[896]{0:T(1024)S(1)}, s32[896]{0:T(1024)}, u32[]{:S(2)}) copy-start(s32[896]{0:T(1024)} %param.11) | copy-start | bytes 10756
  70.6 2.8 %collective-permute-start.8 = (bf16[2,128,1024]{2,1,0:T(8,128)(2,1)S(1)}, bf16[2,128,1024]{2,1,0:T(8,128)(2,1)S(1)}, u32[]{:S(2)}, u32[]{:S(2)}) collective-permute-start(bf16[2,128,1024]{2,1,0:T(8,128)(2,1)S(1)} %slice.87), channel_id=1, source_target_pairs={{0,8},{16,24},{32,40},{48,56},{64,72},{80,88},{96,104},{112,120},{... | collective-permute-start | bytes 1572872 | tf_op jit(solution)/shard_map/ppermute | solution.py:116
  74.3 87.4 %all-gather.5.cloned.1.call-start = ((), (), s32[]{:S(2)}) async-start(), calls=%async_computation | async-start | bytes 4718592 | tf_op jit(solution)/shard_map/all_gather | solution.py:121
  74.3 16.8 %collective-permute-start.9 = (bf16[2,256,1024]{2,1,0:T(8,128)(2,1)S(1)}, bf16[2,256,1024]{2,1,0:T(8,128)(2,1)S(1)}, u32[]{:S(2)}, u32[]{:S(2)}) collective-permute-start(bf16[2,256,1024]{2,1,0:T(8,128)(2,1)S(1)} %select_select_fusion), channel_id=1, source_target_pairs={{0,128},{16,144},{32,160},{48,176},{1,129},{17,145},{33,161},{49,1... | collective-permute-start | bytes 3145736 | tf_op jit(solution)/shard_map/ppermute | solution.py:108
  91.3 23.3 %collective-permute-start.10 = (bf16[2,256,1024]{2,1,0:T(8,128)(2,1)S(1)}, bf16[2,256,1024]{2,1,0:T(8,128)(2,1)S(1)}, u32[]{:S(2)}, u32[]{:S(2)}) collective-permute-start(bf16[2,256,1024]{2,1,0:T(8,128)(2,1)S(1)} %broadcast_select_fusion), channel_id=1, source_target_pairs={{0,64},{16,80},{32,96},{48,112},{128,192},{144,208},{160,224},{176... | collective-permute-start | bytes 3145736 | tf_op jit(solution)/shard_map/ppermute | solution.py:110
  92.6 3.7 %collective-permute-start.11 = (f32[2,896]{1,0:T(2,128)S(1)}, f32[2,896]{1,0:T(2,128)S(1)}, u32[]{:S(2)}, u32[]{:S(2)}) collective-permute-start(f32[2,896]{1,0:T(2,128)S(1)} %pad_maximum_fusion.4), channel_id=1, source_target_pairs={{0,1},{1,0},{2,3},{3,2},{4,5},{5,4},{6,7},{7,6},{8,9},{9,8},{10,11... | collective-permute-start | bytes 21512 | tf_op jit(solution)/shard_map/ppermute | solution.py:284
  96.4 5.1 %collective-permute-start.12 = (f32[2,896]{1,0:T(2,128)S(1)}, f32[2,896]{1,0:T(2,128)S(1)}, u32[]{:S(2)}, u32[]{:S(2)}) collective-permute-start(f32[2,896]{1,0:T(2,128)S(1)} %add.156), channel_id=1, source_target_pairs={{0,2},{1,3},{2,0},{3,1},{4,6},{5,7},{6,4},{7,5},{8,10},{9,11},{10,... | collective-permute-start | bytes 21512 | tf_op jit(solution)/shard_map/ppermute | solution.py:284
  101.5 11.2 %collective-permute-start.13 = (f32[2,896]{1,0:T(2,128)S(1)}, f32[2,896]{1,0:T(2,128)S(1)}, u32[]{:S(2)}, u32[]{:S(2)}) collective-permute-start(f32[2,896]{1,0:T(2,128)S(1)} %add.157), channel_id=1, source_target_pairs={{0,4},{1,5},{2,6},{3,7},{4,0},{5,1},{6,2},{7,3},{8,12},{9,13},{10,... | collective-permute-start | bytes 21512 | tf_op jit(solution)/shard_map/ppermute | solution.py:284
  116.6 2.8 %collective-permute-start.14 = (bf16[2,128,1024]{2,1,0:T(8,128)(2,1)S(1)}, bf16[2,128,1024]{2,1,0:T(8,128)(2,1)S(1)}, u32[]{:S(2)}, u32[]{:S(2)}) collective-permute-start(bf16[2,128,1024]{2,1,0:T(8,128)(2,1)S(1)} %slice.89), channel_id=1, source_target_pairs={{0,8},{16,24},{32,40},{48,56},{64,72},{80,88},{96,104},{112,120},{... | collective-permute-start | bytes 1572872 | tf_op jit(solution)/shard_map/ppermute | solution.py:116
  127.8 13.6 %collective-permute-start.28 = (bf16[2,448,256]{2,1,0:T(8,128)(2,1)}, bf16[2,448,256]{2,1,0:T(8,128)(2,1)S(1)}, u32[]{:S(2)}, u32[]{:S(2)}) collective-permute-start(bf16[2,448,256]{2,1,0:T(8,128)(2,1)} %get-tuple-element.74), channel_id=1, source_target_pairs={{0,1},{1,2},{2,3},{3,0},{4,5},{5,6},{6,7},{7,4},{8,9},{9,10},{10,1... | collective-permute-start | bytes 1376264 | tf_op jit(solution)/shard_map/ppermute | solution.py:204
  128.3 13.9 %copy-start.9 = (bf16[4,448,256]{2,1,0:T(8,128)(2,1)S(1)}, bf16[4,448,256]{2,1,0:T(8,128)(2,1)}, u32[]{:S(2)}) copy-start(bf16[4,448,256]{2,1,0:T(8,128)(2,1)} %get-tuple-element.73) | copy-start | bytes 2752516
  128.3 13.9 %collective-permute-start.30 = (bf16[2,448,256]{2,1,0:T(8,128)(2,1)}, bf16[2,448,256]{2,1,0:T(8,128)(2,1)S(1)}, u32[]{:S(2)}, u32[]{:S(2)}) collective-permute-start(bf16[2,448,256]{2,1,0:T(8,128)(2,1)} %get-tuple-element.75), channel_id=1, source_target_pairs={{0,3},{1,0},{2,1},{3,2},{4,7},{5,4},{6,5},{7,6},{8,11},{9,8},{10,9... | collective-permute-start | bytes 1376264 | tf_op jit(solution)/shard_map/ppermute | solution.py:205
  137.2 13.9 %collective-permute-start.19 = (bf16[2,448,256]{2,1,0:T(8,128)(2,1)}, bf16[2,448,256]{2,1,0:T(8,128)(2,1)S(1)}, u32[]{:S(2)}, u32[]{:S(2)}) collective-permute-start(bf16[2,448,256]{2,1,0:T(8,128)(2,1)} %get-tuple-element.65), channel_id=1, source_target_pairs={{0,1},{1,2},{2,3},{3,0},{4,5},{5,6},{6,7},{7,4},{8,9},{9,10},{10,1... | collective-permute-start | bytes 1376264 | tf_op jit(solution)/shard_map/ppermute | solution.py:204
  139.0 14.9 %collective-permute-start.21 = (bf16[2,448,256]{2,1,0:T(8,128)(2,1)}, bf16[2,448,256]{2,1,0:T(8,128)(2,1)S(1)}, u32[]{:S(2)}, u32[]{:S(2)}) collective-permute-start(bf16[2,448,256]{2,1,0:T(8,128)(2,1)} %get-tuple-element.66), channel_id=1, source_target_pairs={{0,3},{1,0},{2,1},{3,2},{4,7},{5,4},{6,5},{7,6},{8,11},{9,8},{10,9... | collective-permute-start | bytes 1376264 | tf_op jit(solution)/shard_map/ppermute | solution.py:205
  142.3 14.9 %collective-permute-start.29 = (bf16[448,256]{1,0:T(8,128)(2,1)S(1)}, bf16[448,256]{1,0:T(8,128)(2,1)S(1)}, u32[]{:S(2)}, u32[]{:S(2)}) collective-permute-start(bf16[448,256]{1,0:T(8,128)(2,1)S(1)} %get-tuple-element.83), channel_id=1, source_target_pairs={{0,1},{1,2},{2,3},{3,0},{4,5},{5,6},{6,7},{7,4},{8,9},{9,10},{10,1... | collective-permute-start | bytes 688136 | tf_op jit(solution)/shard_map/ppermute | solution.py:206
  143.4 14.6 %collective-permute-start.31 = (bf16[448,256]{1,0:T(8,128)(2,1)S(1)}, bf16[448,256]{1,0:T(8,128)(2,1)S(1)}, u32[]{:S(2)}, u32[]{:S(2)}) collective-permute-start(bf16[448,256]{1,0:T(8,128)(2,1)S(1)} %get-tuple-element.84), channel_id=1, source_target_pairs={{0,3},{1,0},{2,1},{3,2},{4,7},{5,4},{6,5},{7,6},{8,11},{9,8},{10,9... | collective-permute-start | bytes 688136 | tf_op jit(solution)/shard_map/ppermute | solution.py:207
  155.1 23.4 %collective-permute-start.20 = (bf16[448,256]{1,0:T(8,128)(2,1)S(1)}, bf16[448,256]{1,0:T(8,128)(2,1)S(1)}, u32[]{:S(2)}, u32[]{:S(2)}) collective-permute-start(bf16[448,256]{1,0:T(8,128)(2,1)S(1)} %get-tuple-element.89), channel_id=1, source_target_pairs={{0,1},{1,2},{2,3},{3,0},{4,5},{5,6},{6,7},{7,4},{8,9},{9,10},{10,1... | collective-permute-start | bytes 688136 | tf_op jit(solution)/shard_map/ppermute | solution.py:206
  155.2 25.2 %collective-permute-start.22 = (bf16[448,256]{1,0:T(8,128)(2,1)S(1)}, bf16[448,256]{1,0:T(8,128)(2,1)S(1)}, u32[]{:S(2)}, u32[]{:S(2)}) collective-permute-start(bf16[448,256]{1,0:T(8,128)(2,1)S(1)} %get-tuple-element.90), channel_id=1, source_target_pairs={{0,3},{1,0},{2,1},{3,2},{4,7},{5,4},{6,5},{7,6},{8,11},{9,8},{10,9... | collective-permute-start | bytes 688136 | tf_op jit(solution)/shard_map/ppermute | solution.py:207
  158.2 37.5 %collective-permute-start.32 = (bf16[2,448,256]{2,1,0:T(8,128)(2,1)S(1)}, bf16[2,448,256]{2,1,0:T(8,128)(2,1)S(1)}, u32[]{:S(2)}, u32[]{:S(2)}) collective-permute-start(bf16[2,448,256]{2,1,0:T(8,128)(2,1)S(1)} %pad_maximum_fusion.3), channel_id=1, source_target_pairs={{0,4},{1,5},{2,6},{3,7},{4,0},{5,1},{6,2},{7,3},{8,12},{9,13},{10,... | collective-permute-start | bytes 1376264 | tf_op jit(solution)/shard_map/ppermute | solution.py:214
  169.1 11.8 %collective-permute-start.24 = (bf16[2,448,256]{2,1,0:T(8,128)(2,1)}, bf16[2,448,256]{2,1,0:T(8,128)(2,1)S(1)}, u32[]{:S(2)}, u32[]{:S(2)}) collective-permute-start(bf16[2,448,256]{2,1,0:T(8,128)(2,1)} %get-tuple-element.71), channel_id=1, source_target_pairs={{0,1},{1,2},{2,3},{3,0},{4,5},{5,6},{6,7},{7,4},{8,9},{9,10},{10,1... | collective-permute-start | bytes 1376264 | tf_op jit(solution)/shard_map/ppermute | solution.py:204
  169.7 11.0 %copy-start.8 = (bf16[4,448,256]{2,1,0:T(8,128)(2,1)S(1)}, bf16[4,448,256]{2,1,0:T(8,128)(2,1)}, u32[]{:S(2)}) copy-start(bf16[4,448,256]{2,1,0:T(8,128)(2,1)} %get-tuple-element.64) | copy-start | bytes 2752516
  169.7 13.9 %copy-start.1 = (bf16[4,448,256]{2,1,0:T(8,128)(2,1)S(1)}, bf16[4,448,256]{2,1,0:T(8,128)(2,1)}, u32[]{:S(2)}) copy-start(bf16[4,448,256]{2,1,0:T(8,128)(2,1)} %get-tuple-element.70.keep_ref) | copy-start | bytes 2752516
  169.7 13.9 %collective-permute-start.25 = (bf16[2,448,256]{2,1,0:T(8,128)(2,1)}, bf16[2,448,256]{2,1,0:T(8,128)(2,1)S(1)}, u32[]{:S(2)}, u32[]{:S(2)}) collective-permute-start(bf16[2,448,256]{2,1,0:T(8,128)(2,1)} %get-tuple-element.72), channel_id=1, source_target_pairs={{0,3},{1,0},{2,1},{3,2},{4,7},{5,4},{6,5},{7,6},{8,11},{9,8},{10,9... | collective-permute-start | bytes 1376264 | tf_op jit(solution)/shard_map/ppermute | solution.py:205
  178.5 14.0 %copy-start.2 = (bf16[4,448,256]{2,1,0:T(8,128)(2,1)S(1)}, bf16[4,448,256]{2,1,0:T(8,128)(2,1)}, u32[]{:S(2)}) copy-start(bf16[4,448,256]{2,1,0:T(8,128)(2,1)} %get-tuple-element.61.keep_ref) | copy-start | bytes 2752516
  178.5 13.7 %collective-permute-start.15 = (bf16[2,448,256]{2,1,0:T(8,128)(2,1)}, bf16[2,448,256]{2,1,0:T(8,128)(2,1)S(1)}, u32[]{:S(2)}, u32[]{:S(2)}) collective-permute-start(bf16[2,448,256]{2,1,0:T(8,128)(2,1)} %get-tuple-element.62), channel_id=1, source_target_pairs={{0,1},{1,2},{2,3},{3,0},{4,5},{5,6},{6,7},{7,4},{8,9},{9,10},{10,1... | collective-permute-start | bytes 1376264 | tf_op jit(solution)/shard_map/ppermute | solution.py:204
  180.4 12.2 %collective-permute-start.16 = (bf16[2,448,256]{2,1,0:T(8,128)(2,1)}, bf16[2,448,256]{2,1,0:T(8,128)(2,1)S(1)}, u32[]{:S(2)}, u32[]{:S(2)}) collective-permute-start(bf16[2,448,256]{2,1,0:T(8,128)(2,1)} %get-tuple-element.63), channel_id=1, source_target_pairs={{0,3},{1,0},{2,1},{3,2},{4,7},{5,4},{6,5},{7,6},{8,11},{9,8},{10,9... | collective-permute-start | bytes 1376264 | tf_op jit(solution)/shard_map/ppermute | solution.py:205
  180.9 18.6 %copy-start.5 = (bf16[2,448,256]{2,1,0:T(8,128)(2,1)}, bf16[2,448,256]{2,1,0:T(8,128)(2,1)S(1)}, u32[]{:S(2)}) copy-start(bf16[2,448,256]{2,1,0:T(8,128)(2,1)S(1)} %collective-permute-done.24.plus1) | copy-start | bytes 1376260
  180.9 22.6 %collective-permute-start.23 = (bf16[2,448,256]{2,1,0:T(8,128)(2,1)S(1)}, bf16[2,448,256]{2,1,0:T(8,128)(2,1)S(1)}, u32[]{:S(2)}, u32[]{:S(2)}) collective-permute-start(bf16[2,448,256]{2,1,0:T(8,128)(2,1)S(1)} %pad_maximum_fusion.2), channel_id=1, source_target_pairs={{0,4},{1,5},{2,6},{3,7},{4,0},{5,1},{6,2},{7,3},{8,12},{9,13},{10,... | collective-permute-start | bytes 1376264 | tf_op jit(solution)/shard_map/ppermute | solution.py:214
  183.6 16.0 %copy-start.6 = (bf16[2,448,256]{2,1,0:T(8,128)(2,1)}, bf16[2,448,256]{2,1,0:T(8,128)(2,1)S(1)}, u32[]{:S(2)}) copy-start(bf16[2,448,256]{2,1,0:T(8,128)(2,1)S(1)} %collective-permute-done.25.minus1) | copy-start | bytes 1376260
  183.7 13.1 %collective-permute-start.26 = (bf16[448,256]{1,0:T(8,128)(2,1)S(1)}, bf16[448,256]{1,0:T(8,128)(2,1)S(1)}, u32[]{:S(2)}, u32[]{:S(2)}) collective-permute-start(bf16[448,256]{1,0:T(8,128)(2,1)S(1)} %get-tuple-element.86), channel_id=1, source_target_pairs={{0,1},{1,2},{2,3},{3,0},{4,5},{5,6},{6,7},{7,4},{8,9},{9,10},{10,1... | collective-permute-start | bytes 688136 | tf_op jit(solution)/shard_map/ppermute | solution.py:206
  192.3 11.2 %copy-start.4 = (bf16[2,448,256]{2,1,0:T(8,128)(2,1)}, bf16[2,448,256]{2,1,0:T(8,128)(2,1)S(1)}, u32[]{:S(2)}) copy-start(bf16[2,448,256]{2,1,0:T(8,128)(2,1)S(1)} %collective-permute-done.15.plus1) | copy-start | bytes 1376260
  192.3 7.2 %collective-permute-start.27 = (bf16[448,256]{1,0:T(8,128)(2,1)S(1)}, bf16[448,256]{1,0:T(8,128)(2,1)S(1)}, u32[]{:S(2)}, u32[]{:S(2)}) collective-permute-start(bf16[448,256]{1,0:T(8,128)(2,1)S(1)} %get-tuple-element.85), channel_id=1, source_target_pairs={{0,3},{1,0},{2,1},{3,2},{4,7},{5,4},{6,5},{7,6},{8,11},{9,8},{10,9... | collective-permute-start | bytes 688136 | tf_op jit(solution)/shard_map/ppermute | solution.py:207
  192.5 11.0 %copy-start.7 = (bf16[2,448,256]{2,1,0:T(8,128)(2,1)}, bf16[2,448,256]{2,1,0:T(8,128)(2,1)S(1)}, u32[]{:S(2)}) copy-start(bf16[2,448,256]{2,1,0:T(8,128)(2,1)S(1)} %collective-permute-done.16.minus1) | copy-start | bytes 1376260
  192.7 10.8 %collective-permute-start.17 = (bf16[448,256]{1,0:T(8,128)(2,1)S(1)}, bf16[448,256]{1,0:T(8,128)(2,1)S(1)}, u32[]{:S(2)}, u32[]{:S(2)}) collective-permute-start(bf16[448,256]{1,0:T(8,128)(2,1)S(1)} %get-tuple-element.92), channel_id=1, source_target_pairs={{0,1},{1,2},{2,3},{3,0},{4,5},{5,6},{6,7},{7,4},{8,9},{9,10},{10,1... | collective-permute-start | bytes 688136 | tf_op jit(solution)/shard_map/ppermute | solution.py:206
  195.7 3.8 %copy-start.10 = (bf16[2,448,256]{2,1,0:T(8,128)(2,1)}, bf16[2,448,256]{2,1,0:T(8,128)(2,1)S(1)}, u32[]{:S(2)}) copy-start(bf16[2,448,256]{2,1,0:T(8,128)(2,1)S(1)} %collective-permute-done.32.came_ref) | copy-start | bytes 1376260
  195.7 7.8 %collective-permute-start.18 = (bf16[448,256]{1,0:T(8,128)(2,1)S(1)}, bf16[448,256]{1,0:T(8,128)(2,1)S(1)}, u32[]{:S(2)}, u32[]{:S(2)}) collective-permute-start(bf16[448,256]{1,0:T(8,128)(2,1)S(1)} %get-tuple-element.91), channel_id=1, source_target_pairs={{0,3},{1,0},{2,1},{3,2},{4,7},{5,4},{6,5},{7,6},{8,11},{9,8},{10,9... | collective-permute-start | bytes 688136 | tf_op jit(solution)/shard_map/ppermute | solution.py:207
  196.7 2.8 %copy-start.13 = (bf16[448,256]{1,0:T(8,128)(2,1)}, bf16[448,256]{1,0:T(8,128)(2,1)S(1)}, u32[]{:S(2)}) copy-start(bf16[448,256]{1,0:T(8,128)(2,1)S(1)} %collective-permute-done.26.plus2) | copy-start | bytes 688132
  199.5 0.7 copy-start.15
  203.5 0.8 copy-start.11
  203.5 0.9 copy-start.12
  204.3 0.7 copy-start.14
Sparse Core Ops, SparseCore 0:
  74.4 40.8 all-gather.6
  120.5 35.7 all-gather.4

commit v4 on v3

--- a/solution.py
+++ b/solution.py
@@ -11,7 +11,7 @@
 WIDE = 2 * HD
 LAYERS = 2
 NY, NX, NZ = 4, 4, 4
-VMEM = 56 << 20
+VMEM_LARGE, VMEM_SMALL = 52 << 20, 20 << 20
 LOW = jnp.bfloat16
 COLUMNS = LAYERS
 
@@ -65,36 +65,45 @@
     return jnp.dot(a, b, preferred_element_type=jnp.float32)
 
 
-def pieces_kernel(flags, w_ref, g_ref, *out_refs):
+def pieces_kernel(flags, w_ref, g_ref, *refs):
+    out_refs, raw, sems = refs[:NY], refs[NY], refs[NY + 1]
+    depth, wide = out_refs[0].shape[1:]
+    column = pl.multiple_of(flags[0] * wide, wide)
+
+    def read(y):
+        rows = pl.ds(y * depth, depth)
+        return pltpu.make_async_copy(w_ref.at[0, :, rows, pl.ds(column, wide)], raw.at[y], sems.at[y])
+
+    order = (2, 1, 3, 0)
+    for y in order:
+        read(y).start()
+    gains = []
     for layer in range(LAYERS):
-        row = g_ref[layer:layer + 1, :].astype(jnp.float32)
-        gain = jnp.broadcast_to(row, (HD, row.shape[1])).T
-        depth = row.shape[1] // NY
-        for y, out_ref in enumerate(out_refs):
-            rows = slice(y * depth, (y + 1) * depth)
-            for at in range(0, w_ref.shape[2], HD):
-                out_ref[layer, :, at:at + HD] = (w_ref[layer, rows, at:at + HD].astype(jnp.float32) * gain[rows]).astype(LOW)
-
-
-def pieces(flags, weights, gains, which):
-    depth, wide = weights.shape[2], weights.shape[3] // 2
+        row = g_ref[0, layer:layer + 1, :].astype(jnp.float32)
+        gains.append(jnp.broadcast_to(row, (HD, row.shape[1])).T)
+    for y in order:
+        read(y).wait()
+        for layer in range(LAYERS):
+            gain = gains[layer][y * depth:(y + 1) * depth]
+            for at in range(0, wide, HD):
+                out_refs[y][layer, :, at:at + HD] = (raw[y, layer, :, at:at + HD].astype(jnp.float32) * gain).astype(LOW)
+
+
+def pieces(weights, gains, row):
+    depth, wide = weights.shape[2] // NY, weights.shape[3] // 2
+    vmem = pl.BlockSpec(memory_space=pltpu.VMEM)
+    shape = (LAYERS, depth, wide)
     return pl.pallas_call(
         pieces_kernel,
-        out_shape=tuple(jax.ShapeDtypeStruct((LAYERS, depth // NY, wide), LOW) for _ in range(NY)),
-        grid_spec=pltpu.PrefetchScalarGridSpec(
-            num_scalar_prefetch=1,
-            grid=(1,),
-            in_specs=[
-                pl.BlockSpec((None, LAYERS, depth, wide), lambda i, f: (0, 0, 0, f[COLUMNS + which * NX] // NX)),
-                pl.BlockSpec((None, LAYERS, depth), lambda i, f: (0, 0, 0)),
-            ],
-            out_specs=tuple(pl.BlockSpec((LAYERS, depth // NY, wide), lambda i, f: (0, 0, 0)) for _ in range(NY)),
+        out_shape=tuple(jax.ShapeDtypeStruct(shape, LOW) for _ in range(NY)),
+        in_specs=[pl.BlockSpec(memory_space=pltpu.SMEM), pl.BlockSpec(memory_space=pltpu.HBM), vmem],
+        out_specs=tuple(vmem for _ in range(NY)),
+        scratch_shapes=[pltpu.VMEM((NY, *shape), LOW), pltpu.SemaphoreType.DMA((NY,))],
+        compiler_params=pltpu.CompilerParams(vmem_limit_bytes=VMEM_LARGE),
+        cost_estimate=pl.CostEstimate(
+            flops=LAYERS * NY * depth * wide, bytes_accessed=4 * LAYERS * NY * depth * wide, transcendentals=0
         ),
-        compiler_params=pltpu.CompilerParams(vmem_limit_bytes=VMEM),
-        cost_estimate=pl.CostEstimate(
-            flops=LAYERS * depth * wide, bytes_accessed=4 * LAYERS * depth * wide, transcendentals=0
-        ),
-    )(flags, weights, gains)
+    )(row.astype(jnp.int32).reshape(1), weights, gains)
 
 
 def scatter(parts):
@@ -121,79 +130,56 @@
     return lax.all_gather(half, "chain", axis_index_groups=ROWS, axis=0)
 
 
-def product_kernel(layer, flags, x_ref, g_ref, own_ref, src_ref, plus_ref, minus_ref, keep_ref, scaled):
-    j = pl.program_id(0)
+def product_kernel(layer, first, flags, x_ref, own_ref, src_ref, plus_ref, minus_ref, keep_ref, blocks, sems):
     held = flags[layer] > 0
     cut = x_ref.shape[0] // 2
-
-    @pl.when(j == 0)
-    def _():
-        gain = jnp.where(held, g_ref[layer:layer + 1, :].astype(jnp.float32), 1.0)
-        scaled[...] = (x_ref[...].astype(jnp.float32) * gain).astype(LOW)
-
-    def put(weights):
-        total = dot(scaled[...], weights).astype(LOW)
-        low, high = total[:cut], total[cut:]
-
-        @pl.when(j == 0)
+    for j in range(NX):
+        head = flags[first + j]
+
+        @pl.when(held)
         def _():
-            plus_ref[0] = low
-            minus_ref[0] = high
-
-        @pl.when(j == 1)
+            column = pl.ds(pl.multiple_of(head * WIDE, WIDE), WIDE)
+            pltpu.make_async_copy(own_ref.at[0, layer, :, :, column], blocks.at[j], sems.at[j]).start()
+
+        @pl.when(jnp.logical_not(held))
         def _():
-            plus_ref[1] = high
-            keep_ref[0] = low
-
-        @pl.when(j == 2)
-        def _():
-            minus_ref[1] = low
-            keep_ref[1] = high
-
-        @pl.when(j == 3)
-        def _():
-            keep_ref[2] = low
-            keep_ref[3] = high
-
-    @pl.when(held)
-    def _():
-        put(own_ref[...])
-
-    @pl.when(jnp.logical_not(held))
-    def _():
-        put(src_ref[...].reshape(own_ref.shape))
-
-
-def product(flags, x, gain, own, layer, src, which):
+            column = pl.ds(pl.multiple_of(head % NX * WIDE, WIDE), WIDE)
+            pltpu.make_async_copy(src_ref.at[:, layer, :, column], blocks.at[j], sems.at[j]).start()
+
+    low, high = slice(0, cut), slice(cut, 2 * cut)
+    goals = (
+        ((plus_ref, 0, low), (minus_ref, 0, high)),
+        ((plus_ref, 1, high), (keep_ref, 0, low)),
+        ((minus_ref, 1, low), (keep_ref, 1, high)),
+        ((keep_ref, 2, low), (keep_ref, 3, high)),
+    )
+    for j, goal in enumerate(goals):
+        pltpu.make_async_copy(src_ref.at[:, layer, :, pl.ds(0, WIDE)], blocks.at[j], sems.at[j]).wait()
+        block = blocks[j].reshape(-1, WIDE)
+        for ref, slot, rows in goal:
+            ref[slot] = dot(x_ref[rows, :], block).astype(LOW)
+
+
+def product(flags, x, own, layer, src, which):
     tokens, depth = x.shape
-    first = COLUMNS + which * NX
-
-    def whole(*shape):
-        return pl.BlockSpec(shape, lambda j, f: (0,) * len(shape))
-
     shapes = [(2, tokens // 2, WIDE), (2, tokens // 2, WIDE), (4, tokens // 2, WIDE)]
+    vmem, hbm = pl.BlockSpec(memory_space=pltpu.VMEM), pl.BlockSpec(memory_space=pltpu.HBM)
     return pl.pallas_call(
-        functools.partial(product_kernel, layer),
+        functools.partial(product_kernel, layer, COLUMNS + which * NX),
         out_shape=tuple(jax.ShapeDtypeStruct(shape, LOW) for shape in shapes),
-        grid_spec=pltpu.PrefetchScalarGridSpec(
-            num_scalar_prefetch=1,
-            grid=(NX,),
-            in_specs=[
-                whole(tokens, depth),
-                pl.BlockSpec((None, LAYERS, depth), lambda j, f: (0, 0, 0)),
-                pl.BlockSpec((None, None, depth, WIDE), lambda j, f: (0, layer, 0, f[first + j * f[layer]])),
-                pl.BlockSpec((2 * NY, None, depth // (2 * NY), WIDE), lambda j, f: (0, layer, 0, f[first + j * (1 - f[layer])] % NX)),
-            ],
-            out_specs=tuple(whole(*shape) for shape in shapes),
-            scratch_shapes=[pltpu.VMEM((tokens, depth), LOW)],
-        ),
-        compiler_params=pltpu.CompilerParams(vmem_limit_bytes=VMEM),
+        in_specs=[pl.BlockSpec(memory_space=pltpu.SMEM), vmem, hbm, hbm],
+        out_specs=(vmem, vmem, vmem),
+        scratch_shapes=[
+            pltpu.VMEM((NX, 2 * NY, depth // (2 * NY), WIDE), LOW),
+            pltpu.SemaphoreType.DMA((NX,)),
+        ],
+        compiler_params=pltpu.CompilerParams(vmem_limit_bytes=VMEM_LARGE),
         cost_estimate=pl.CostEstimate(
             flops=2 * tokens * depth * WIDE * NX,
             bytes_accessed=2 * (tokens * depth + NX * WIDE * (depth + tokens)),
             transcendentals=0,
         ),
-    )(flags, x, gain, own, src)
+    )(flags, x, own, src)
 
 
 def add(*terms):
@@ -229,7 +215,7 @@
 def close(layer, terms, came, turns, out):
     tokens = turns[0].shape[0]
     args = [*terms, came, *turns]
-    in_specs = [pl.BlockSpec(a.shape, lambda i, n=a.ndim: (0,) * n) for a in args]
+    in_specs = [pl.BlockSpec(memory_space=pltpu.VMEM) for _ in args]
     aliases = {}
     if out is not None:
         aliases = {len(args): 0}
@@ -242,7 +228,7 @@
         in_specs=in_specs,
         out_specs=pl.BlockSpec((None, tokens, WIDE), lambda i: (layer, 0, 0)),
         input_output_aliases=aliases,
-        compiler_params=pltpu.CompilerParams(vmem_limit_bytes=VMEM),
+        compiler_params=pltpu.CompilerParams(vmem_limit_bytes=VMEM_SMALL),
         cost_estimate=pl.CostEstimate(flops=8 * tokens * WIDE, bytes_accessed=16 * tokens * WIDE, transcendentals=0),
     )(*args)
 
@@ -268,18 +254,25 @@
     inputs = (hidden_first, hidden_second)
     width = hidden_first.shape[1] * lax.axis_size("tp")
     flags = flags_of(loaded_layers)
-    swap_parts = pieces(flags, weight_buffer, gain_buffer, 0)
-    swap = scatter(swap_parts)
-    keep_parts = pieces(flags, weight_buffer, gain_buffer, 1)
-    squares = jnp.stack([jnp.sum(jnp.square(v.astype(jnp.float32)), axis=1) for v in inputs])
-
-    swap, keep_parts, squares = lax.optimization_barrier((swap, keep_parts, squares))
+    h = place()[0]
+    own = weight_buffer.reshape(1, LAYERS, 2 * NY, -1, weight_buffer.shape[3])
+    swap = scatter(pieces(weight_buffer, gain_buffer, 1 - h))
+    keep_parts = pieces(weight_buffer, gain_buffer, h)
+    wide = [v.astype(jnp.float32) for v in inputs]
+    squares = jnp.stack([jnp.sum(jnp.square(v), axis=1) for v in wide])
+    scaled = [
+        jnp.where(loaded_layers[0] > layer, (v * gain_buffer[0, layer][None, :].astype(jnp.float32)).astype(LOW), inputs[layer])
+        for layer, v in enumerate(wide)
+    ]
+
+    swap, keep_parts, squares, scaled = lax.optimization_barrier((swap, keep_parts, squares, scaled))
     keep = scatter(keep_parts)
     swap = down(swap)
-    swap, keep, squares = lax.optimization_barrier((swap, keep, squares))
+    swap, keep = lax.optimization_barrier((swap, keep))
     swap_half = across(swap)
     swap_src = gather(swap_half)
     keep = down(after(keep, swap_half))
+    squares = after(squares, swap_half)
     for pairs in (X_ONE, X_TWO, H_SWAP):
         squares = squares + lax.ppermute(squares, "tp", pairs)
     turns = turns_of(squares, width, positions)
@@ -287,7 +280,7 @@
     keep_src = gather(across(keep))
 
     def sums(layer, src, which):
-        return product(flags, inputs[layer], gain_buffer, weight_buffer, layer, src, which)
+        return product(flags, scaled[layer], own, layer, src, which)
 
     came = [swapped(*round_x(*sums(layer, swap_src, 0))) for layer in range(LAYERS)]
     out = None

time: 219 us -> 210 us (0.959); the launches traced: 215 us -> 209 us
  Pallas kernels: 47.3 us -> 30.9 us
  waiting for transfers between devices: 69 us -> 79.3 us
  local copies, waits for them, and re-layouts: 4.91 us -> 1.29 us
    pallas_call x6, Pallas kernels: 40.8 us -> 28.7 us  [the longest x4 20.7 us: product(): pl.pallas_call(functools.partial(product_kernel, layer, COLUMNS + which *...]
    ppermute x2, waiting for transfers between devices: 0.01 us -> 7.55 us  [swapped(): return lax.ppermute(jnp.stack([low, high]).astype(LOW), 'tp', H_SWAP)]
    pallas_call x2, Pallas kernels: 6.53 us -> 2.22 us  [close(): pl.pallas_call(close_kernel, out_shape=jax.ShapeDtypeStruct((LAYERS, toke...]
    ppermute x4, waiting for transfers between devices: 14.4 us -> 18.4 us  [round_x(): plus1 = lax.ppermute(plus, 'tp', X_NEXT)]
    select_n x0 -> x1, other arithmetic: none -> 2.92 us  [shards(): jnp.where(loaded_layers[0] > layer, (v * gain_buffer[0, layer][None, :].a...]
  transfers between devices with their start and end apart: 35 -> 35, of which waited for: 17 -> 20; matrix products, arithmetic and copies ran while one was open for 6% -> 6% of each run, Pallas kernels for 18% -> 12%
where the time goes in v4:
time: 210 us; the launch traced here: 209 us
  waiting for transfers between devices  79.3 us (38%)
  starting transfers between devices  68 us (32%)
  Pallas kernels  30.9 us (15%)
  other arithmetic  14.7 us (7%)
  between operations  14.5 us (7%)
    ppermute x6, starting transfers between devices, scatter(): lax.ppermute(parts[k], 'chain', from_source(k))  20.9 us
    pallas_call x4, Pallas kernels, product(): pl.pallas_call(functools.partial(product_kernel, layer, COLUMNS + which *...  20.7 us
    ppermute x6, waiting for transfers between devices, scatter(): lax.ppermute(parts[k], 'chain', from_source(k))  20 us
    ppermute x4, waiting for transfers between devices, round_x(): plus1 = lax.ppermute(plus, 'tp', X_NEXT)  18.4 us
    ppermute x2, waiting for transfers between devices, down(): far = lax.ppermute(first, 'chain', Z_FAR)  12.9 us
    ppermute x3, starting transfers between devices, shards(): squares = squares + lax.ppermute(squares, 'tp', pairs)  9.51 us
    ppermute x3, waiting for transfers between devices, shards(): squares = squares + lax.ppermute(squares, 'tp', pairs)  8.84 us
    pallas_call x2, Pallas kernels, pieces(): pl.pallas_call(pieces_kernel, out_shape=tuple((jax.ShapeDtypeStruct(shape...  8.04 us
  transfers between devices with their start and end apart: 35, of which 20 were waited for; matrix products, arithmetic and copies ran while one was open for 6% of the time, Pallas kernels for 12%

profile of v4, /device:TPU:6, one launch (start us, length us, event | category | flops | bytes accessed | tf_op | source)
XLA Modules:
  0.0 208.7 jit_solution(17545523539125707455)
XLA Ops:
  6.5 0.7 copy-done.2
  7.2 4.0 %shard_map.64 = (bf16[2,256,1024]{2,1,0:T(8,128)(2,1)S(1)}, bf16[2,256,1024]{2,1,0:T(8,128)(2,1)}, bf16[2,256,1024]{2,1,0:T(8,128)(2,1)}, bf16[2,256,1024]{2,1,0:T(8,128)(2,1)}) custom-call(s32[1]{0:T(128)} %bitcast.8.flags, bf16[1,2,1024,2048]{3,2,1,0:T(8,128)(2,1)} %w_ref.3, bf16[1,2,1024]{2,1,0:T(2,128)(2,1)S(1)} %copy-done.2), custom_call_target="tpu_custom_call" | custom-call | flops 2097152 | bytes 8388608 | tf_op jit(solution)/shard_map/pallas_call | solution.py:96
  11.3 4.5 %collective-permute-start = (bf16[2,256,1024]{2,1,0:T(8,128)(2,1)}, bf16[2,256,1024]{2,1,0:T(8,128)(2,1)}, u32[]{:S(2)}, u32[]{:S(2)}) collective-permute-start(bf16[2,256,1024]{2,1,0:T(8,128)(2,1)} %get-tuple-element.45), channel_id=1, source_target_pairs={{0,16},{1,17},{2,18},{3,19},{4,20},{5,21},{6,22},{7,23}} | collective-permute-start | bytes 3145736 | tf_op jit(solution)/shard_map/ppermute | solution.py:111
  15.7 3.3 %collective-permute-start.1 = (bf16[2,256,1024]{2,1,0:T(8,128)(2,1)}, bf16[2,256,1024]{2,1,0:T(8,128)(2,1)}, u32[]{:S(2)}, u32[]{:S(2)}) collective-permute-start(bf16[2,256,1024]{2,1,0:T(8,128)(2,1)} %get-tuple-element.46), channel_id=1, source_target_pairs={{0,32},{1,33},{2,34},{3,35},{4,36},{5,37},{6,38},{7,39}} | collective-permute-start | bytes 3145736 | tf_op jit(solution)/shard_map/ppermute | solution.py:111
  19.1 2.3 %collective-permute-start.2 = (bf16[2,256,1024]{2,1,0:T(8,128)(2,1)}, bf16[2,256,1024]{2,1,0:T(8,128)(2,1)}, u32[]{:S(2)}, u32[]{:S(2)}) collective-permute-start(bf16[2,256,1024]{2,1,0:T(8,128)(2,1)} %get-tuple-element.47), channel_id=1, source_target_pairs={{0,48},{1,49},{2,50},{3,51},{4,52},{5,53},{6,54},{7,55}} | collective-permute-start | bytes 3145736 | tf_op jit(solution)/shard_map/ppermute | solution.py:111
  23.0 4.0 %shard_map.65 = (bf16[2,256,1024]{2,1,0:T(8,128)(2,1)S(1)}, bf16[2,256,1024]{2,1,0:T(8,128)(2,1)}, bf16[2,256,1024]{2,1,0:T(8,128)(2,1)}, bf16[2,256,1024]{2,1,0:T(8,128)(2,1)}) custom-call(s32[1]{0:T(128)} %bitcast.9.flags, bf16[1,2,1024,2048]{3,2,1,0:T(8,128)(2,1)} %w_ref.3, bf16[1,2,1024]{2,1,0:T(2,128)(2,1)S(1)} %copy-done.3), custom_call_target="tpu_custom_call" | custom-call | flops 2097152 | bytes 8388608 | tf_op jit(solution)/shard_map/pallas_call | solution.py:96
  27.1 2.9 %fusion.4 = (bf16[896,1024]{1,0:T(8,128)(2,1)}, bf16[896,1024]{1,0:T(8,128)(2,1)}) fusion(bf16[896,1024]{1,0:T(8,128)(2,1)S(1)} %copy-done.5, f32[1024]{0:T(1024)S(1)} %bitcast.81, pred[]{:T(512)} %bitcast.12, bf16[896,1024]{1,0:T(8,128)(2,1)S(1)} %copy-done.7, f32[1024]{0:T(1024)S(1)} %bitcast.82, pred[]{:T(512)} %bitcast.10), kind=kLoop, calls=%fused_computation.8 | loop fusion | flops 7340032 | bytes 7348226 | tf_op jit(solution)/shard_map/jit(_where)/select_n | solution.py:264
  30.0 8.6 %collective-permute-done.1 = bf16[2,256,1024]{2,1,0:T(8,128)(2,1)} collective-permute-done((bf16[2,256,1024]{2,1,0:T(8,128)(2,1)}, bf16[2,256,1024]{2,1,0:T(8,128)(2,1)}, u32[]{:S(2)}, u32[]{:S(2)}) %collective-permute-start.1) | collective-permute-done | bytes 1048608 | tf_op jit(solution)/shard_map/ppermute | solution.py:111
  38.6 1.4 select_select_fusion.1
  40.0 2.3 %collective-permute-start.3 = (bf16[2,256,1024]{2,1,0:T(8,128)(2,1)S(1)}, bf16[2,256,1024]{2,1,0:T(8,128)(2,1)}, u32[]{:S(2)}, u32[]{:S(2)}) collective-permute-start(bf16[2,256,1024]{2,1,0:T(8,128)(2,1)S(1)} %select_select_fusion.1), channel_id=1, source_target_pairs={{0,128},{16,144},{32,160},{48,176},{1,129},{17,145},{33,161},{49,1... | collective-permute-start | bytes 3145736 | tf_op jit(solution)/shard_map/ppermute | solution.py:117
  42.3 2.3 %collective-permute-start.5 = (bf16[2,256,1024]{2,1,0:T(8,128)(2,1)}, bf16[2,256,1024]{2,1,0:T(8,128)(2,1)}, u32[]{:S(2)}, u32[]{:S(2)}) collective-permute-start(bf16[2,256,1024]{2,1,0:T(8,128)(2,1)} %get-tuple-element.55), channel_id=1, source_target_pairs={{0,16},{1,17},{2,18},{3,19},{4,20},{5,21},{6,22},{7,23}} | collective-permute-start | bytes 3145736 | tf_op jit(solution)/shard_map/ppermute | solution.py:111
  44.6 6.2 %collective-permute-start.6 = (bf16[2,256,1024]{2,1,0:T(8,128)(2,1)}, bf16[2,256,1024]{2,1,0:T(8,128)(2,1)}, u32[]{:S(2)}, u32[]{:S(2)}) collective-permute-start(bf16[2,256,1024]{2,1,0:T(8,128)(2,1)} %get-tuple-element.56), channel_id=1, source_target_pairs={{0,32},{1,33},{2,34},{3,35},{4,36},{5,37},{6,38},{7,39}} | collective-permute-start | bytes 3145736 | tf_op jit(solution)/shard_map/ppermute | solution.py:111
  50.8 2.3 %collective-permute-start.7 = (bf16[2,256,1024]{2,1,0:T(8,128)(2,1)}, bf16[2,256,1024]{2,1,0:T(8,128)(2,1)}, u32[]{:S(2)}, u32[]{:S(2)}) collective-permute-start(bf16[2,256,1024]{2,1,0:T(8,128)(2,1)} %get-tuple-element.57), channel_id=1, source_target_pairs={{0,48},{1,49},{2,50},{3,51},{4,52},{5,53},{6,54},{7,55}} | collective-permute-start | bytes 3145736 | tf_op jit(solution)/shard_map/ppermute | solution.py:111
  53.1 0.5 collective-permute-done.3
  53.8 2.3 %collective-permute-start.4 = (bf16[2,256,1024]{2,1,0:T(8,128)(2,1)S(1)}, bf16[2,256,1024]{2,1,0:T(8,128)(2,1)}, u32[]{:S(2)}, u32[]{:S(2)}) collective-permute-start(bf16[2,256,1024]{2,1,0:T(8,128)(2,1)S(1)} %broadcast_select_fusion.1), channel_id=1, source_target_pairs={{0,64},{16,80},{32,96},{48,112},{128,192},{144,208},{160,224},{176... | collective-permute-start | bytes 3145736 | tf_op jit(solution)/shard_map/ppermute | solution.py:119
  56.2 11.2 %collective-permute-done.6 = bf16[2,256,1024]{2,1,0:T(8,128)(2,1)} collective-permute-done((bf16[2,256,1024]{2,1,0:T(8,128)(2,1)}, bf16[2,256,1024]{2,1,0:T(8,128)(2,1)}, u32[]{:S(2)}, u32[]{:S(2)}) %collective-permute-start.6) | collective-permute-done | bytes 1048608 | tf_op jit(solution)/shard_map/ppermute | solution.py:111
  67.5 1.5 select_select_fusion
  69.2 1.3 collective-permute-start.8
  70.5 1.5 collective-permute-done.8
  72.0 0.8 slice_select_fusion.1
  72.9 5.0 %collective-permute-start.9 = (bf16[2,256,1024]{2,1,0:T(8,128)(2,1)S(1)}, bf16[2,256,1024]{2,1,0:T(8,128)(2,1)S(1)}, u32[]{:S(2)}, u32[]{:S(2)}) collective-permute-start(bf16[2,256,1024]{2,1,0:T(8,128)(2,1)S(1)} %select_select_fusion), channel_id=1, source_target_pairs={{0,128},{16,144},{32,160},{48,176},{1,129},{17,145},{33,161},{49,1... | collective-permute-start | bytes 3145736 | tf_op jit(solution)/shard_map/ppermute | solution.py:117
  78.0 12.4 %collective-permute-done.9 = bf16[2,256,1024]{2,1,0:T(8,128)(2,1)S(1)} collective-permute-done((bf16[2,256,1024]{2,1,0:T(8,128)(2,1)S(1)}, bf16[2,256,1024]{2,1,0:T(8,128)(2,1)S(1)}, u32[]{:S(2)}, u32[]{:S(2)}) %collective-permute-start.9) | collective-permute-done | bytes 1048608 | tf_op jit(solution)/shard_map/ppermute | solution.py:117
  90.5 1.4 collective-permute-start.10
  91.9 0.9 collective-permute-start.11
  92.8 2.8 %collective-permute-done.11 = f32[2,896]{1,0:T(2,128)S(1)} collective-permute-done((f32[2,896]{1,0:T(2,128)S(1)}, f32[2,896]{1,0:T(2,128)S(1)}, u32[]{:S(2)}, u32[]{:S(2)}) %collective-permute-start.11) | collective-permute-done | bytes 7200 | tf_op jit(solution)/shard_map/ppermute | solution.py:277
  95.6 1.4 collective-permute-start.12
  97.0 3.7 %collective-permute-done.12 = f32[2,896]{1,0:T(2,128)S(1)} collective-permute-done((f32[2,896]{1,0:T(2,128)S(1)}, f32[2,896]{1,0:T(2,128)S(1)}, u32[]{:S(2)}, u32[]{:S(2)}) %collective-permute-start.12) | collective-permute-done | bytes 7200 | tf_op jit(solution)/shard_map/ppermute | solution.py:277
  100.8 7.2 %collective-permute-start.13 = (f32[2,896]{1,0:T(2,128)S(1)}, f32[2,896]{1,0:T(2,128)S(1)}, u32[]{:S(2)}, u32[]{:S(2)}) collective-permute-start(f32[2,896]{1,0:T(2,128)S(1)} %add.157), channel_id=1, source_target_pairs={{0,4},{1,5},{2,6},{3,7},{4,0},{5,1},{6,2},{7,3},{8,12},{9,13},{10,... | collective-permute-start | bytes 21512 | tf_op jit(solution)/shard_map/ppermute | solution.py:277
  107.9 1.7 fusion.24
  109.6 2.3 %collective-permute-done.13 = f32[2,896]{1,0:T(2,128)S(1)} collective-permute-done((f32[2,896]{1,0:T(2,128)S(1)}, f32[2,896]{1,0:T(2,128)S(1)}, u32[]{:S(2)}, u32[]{:S(2)}) %collective-permute-start.13) | collective-permute-done | bytes 7200 | tf_op jit(solution)/shard_map/ppermute | solution.py:277
  113.1 1.5 collective-permute-start.14
  114.6 1.3 collective-permute-done.14
  115.9 0.9 slice_select_fusion
  117.0 5.2 %shard_map.69 = (bf16[2,448,256]{2,1,0:T(8,128)(2,1)S(1)}, bf16[2,448,256]{2,1,0:T(8,128)(2,1)S(1)}, bf16[4,448,256]{2,1,0:T(8,128)(2,1)S(1)}) custom-call(s32[10]{0:T(128)S(1)} %stack.78.flags, bf16[896,1024]{1,0:T(8,128)(2,1)} %get-tuple-element.73.x_ref, bf16[1,2,8,128,2048]{4,3,2,1,0:T(8,128)(2,1)} %bitcast.73, bf16[8,2,128,1024]{3,2,1,0:T(8,128)(2,1)} %bitcast.77), custom_call_target="tpu_custom_call" | custom-call | flops 1879048192 | bytes 5767168 | tf_op jit(solution)/shard_map/pallas_call | solution.py:167
  122.2 0.6 collective-permute-start.28
  122.8 1.6 collective-permute-start.30
  124.3 5.2 %shard_map.67 = (bf16[2,448,256]{2,1,0:T(8,128)(2,1)S(1)}, bf16[2,448,256]{2,1,0:T(8,128)(2,1)S(1)}, bf16[4,448,256]{2,1,0:T(8,128)(2,1)S(1)}) custom-call(s32[10]{0:T(128)S(1)} %stack.78.flags, bf16[896,1024]{1,0:T(8,128)(2,1)} %get-tuple-element.52.x_ref, bf16[1,2,8,128,2048]{4,3,2,1,0:T(8,128)(2,1)} %bitcast.74, bf16[8,2,128,1024]{3,2,1,0:T(8,128)(2,1)} %bitcast.78), custom_call_target="tpu_custom_call" | custom-call | flops 1879048192 | bytes 5767168 | tf_op jit(solution)/shard_map/pallas_call | solution.py:167
  129.5 1.8 collective-permute-start.19
  131.6 4.0 %collective-permute-done.28 = bf16[2,448,256]{2,1,0:T(8,128)(2,1)S(1)} collective-permute-done((bf16[2,448,256]{2,1,0:T(8,128)(2,1)S(1)}, bf16[2,448,256]{2,1,0:T(8,128)(2,1)S(1)}, u32[]{:S(2)}, u32[]{:S(2)}) %collective-permute-start.28) | collective-permute-done | bytes 458784 | tf_op jit(solution)/shard_map/ppermute | solution.py:190
  135.6 1.7 collective-permute-done.30
  137.8 1.7 collective-permute-start.31
  139.6 5.9 %collective-permute-done.19 = bf16[2,448,256]{2,1,0:T(8,128)(2,1)S(1)} collective-permute-done((bf16[2,448,256]{2,1,0:T(8,128)(2,1)S(1)}, bf16[2,448,256]{2,1,0:T(8,128)(2,1)S(1)}, u32[]{:S(2)}, u32[]{:S(2)}) %collective-permute-start.19) | collective-permute-done | bytes 458784 | tf_op jit(solution)/shard_map/ppermute | solution.py:190
  145.5 1.7 collective-permute-done.21
  147.2 0.9 fusion.14
  148.4 1.7 collective-permute-start.22
  150.2 1.2 collective-permute-done.31
  151.6 0.8 pad_maximum_fusion.3
  152.4 3.7 %collective-permute-start.32 = (bf16[2,448,256]{2,1,0:T(8,128)(2,1)}, bf16[2,448,256]{2,1,0:T(8,128)(2,1)S(1)}, u32[]{:S(2)}, u32[]{:S(2)}) collective-permute-start(bf16[2,448,256]{2,1,0:T(8,128)(2,1)} %pad_maximum_fusion.3), channel_id=1, source_target_pairs={{0,4},{1,5},{2,6},{3,7},{4,0},{5,1},{6,2},{7,3},{8,12},{9,13},{10,... | collective-permute-start | bytes 1376264 | tf_op jit(solution)/shard_map/ppermute | solution.py:200
  156.1 5.2 %shard_map.68 = (bf16[2,448,256]{2,1,0:T(8,128)(2,1)S(1)}, bf16[2,448,256]{2,1,0:T(8,128)(2,1)S(1)}, bf16[4,448,256]{2,1,0:T(8,128)(2,1)S(1)}) custom-call(s32[10]{0:T(128)S(1)} %stack.78.flags, bf16[896,1024]{1,0:T(8,128)(2,1)} %get-tuple-element.73.x_ref, bf16[1,2,8,128,2048]{4,3,2,1,0:T(8,128)(2,1)} %bitcast.75, bf16[8,2,128,1024]{3,2,1,0:T(8,128)(2,1)} %bitcast.79), custom_call_target="tpu_custom_call" | custom-call | flops 1879048192 | bytes 5767168 | tf_op jit(solution)/shard_map/pallas_call | solution.py:167
  161.3 0.8 collective-permute-start.24
  162.1 1.3 collective-permute-start.25
  163.4 5.2 %shard_map.66 = (bf16[2,448,256]{2,1,0:T(8,128)(2,1)S(1)}, bf16[2,448,256]{2,1,0:T(8,128)(2,1)S(1)}, bf16[4,448,256]{2,1,0:T(8,128)(2,1)S(1)}) custom-call(s32[10]{0:T(128)S(1)} %stack.78.flags, bf16[896,1024]{1,0:T(8,128)(2,1)} %get-tuple-element.52.x_ref, bf16[1,2,8,128,2048]{4,3,2,1,0:T(8,128)(2,1)} %bitcast.76, bf16[8,2,128,1024]{3,2,1,0:T(8,128)(2,1)} %bitcast.80), custom_call_target="tpu_custom_call" | custom-call | flops 1879048192 | bytes 5767168 | tf_op jit(solution)/shard_map/pallas_call | solution.py:167
  168.6 2.0 collective-permute-start.15
  170.7 1.1 fusion.20
  171.9 2.9 %collective-permute-done.24.plus1 = bf16[2,448,256]{2,1,0:T(8,128)(2,1)S(1)} collective-permute-done((bf16[2,448,256]{2,1,0:T(8,128)(2,1)S(1)}, bf16[2,448,256]{2,1,0:T(8,128)(2,1)S(1)}, u32[]{:S(2)}, u32[]{:S(2)}) %collective-permute-start.24) | collective-permute-done | bytes 458784 | tf_op jit(solution)/shard_map/ppermute | solution.py:190
  174.8 2.3 %collective-permute-start.23 = (bf16[2,448,256]{2,1,0:T(8,128)(2,1)S(1)}, bf16[2,448,256]{2,1,0:T(8,128)(2,1)S(1)}, u32[]{:S(2)}, u32[]{:S(2)}) collective-permute-start(bf16[2,448,256]{2,1,0:T(8,128)(2,1)S(1)} %pad_maximum_fusion.2), channel_id=1, source_target_pairs={{0,4},{1,5},{2,6},{3,7},{4,0},{5,1},{6,2},{7,3},{8,12},{9,13},{10,... | collective-permute-start | bytes 1376264 | tf_op jit(solution)/shard_map/ppermute | solution.py:200
  177.3 1.8 collective-permute-start.26
  179.1 5.5 %collective-permute-done.15.plus1 = bf16[2,448,256]{2,1,0:T(8,128)(2,1)S(1)} collective-permute-done((bf16[2,448,256]{2,1,0:T(8,128)(2,1)S(1)}, bf16[2,448,256]{2,1,0:T(8,128)(2,1)S(1)}, u32[]{:S(2)}, u32[]{:S(2)}) %collective-permute-start.15) | collective-permute-done | bytes 458784 | tf_op jit(solution)/shard_map/ppermute | solution.py:190
  185.2 2.9 %collective-permute-start.17 = (bf16[448,256]{1,0:T(8,128)(2,1)S(1)}, bf16[448,256]{1,0:T(8,128)(2,1)S(1)}, u32[]{:S(2)}, u32[]{:S(2)}) collective-permute-start(bf16[448,256]{1,0:T(8,128)(2,1)S(1)} %get-tuple-element.96), channel_id=1, source_target_pairs={{0,1},{1,2},{2,3},{3,0},{4,5},{5,6},{6,7},{7,4},{8,9},{9,10},{10,1... | collective-permute-start | bytes 688136 | tf_op jit(solution)/shard_map/ppermute | solution.py:192
  188.1 1.5 collective-permute-done.26.plus2
  189.6 2.6 %collective-permute-done.27.minus2 = bf16[448,256]{1,0:T(8,128)(2,1)S(1)} collective-permute-done((bf16[448,256]{1,0:T(8,128)(2,1)S(1)}, bf16[448,256]{1,0:T(8,128)(2,1)S(1)}, u32[]{:S(2)}, u32[]{:S(2)}) %collective-permute-start.27) | collective-permute-done | bytes 229408 | tf_op jit(solution)/shard_map/ppermute | solution.py:193
  192.1 1.1 shard_map.70.refs_0_
  193.2 7.5 %collective-permute-done.23.came_ref = bf16[2,448,256]{2,1,0:T(8,128)(2,1)S(1)} collective-permute-done((bf16[2,448,256]{2,1,0:T(8,128)(2,1)S(1)}, bf16[2,448,256]{2,1,0:T(8,128)(2,1)S(1)}, u32[]{:S(2)}, u32[]{:S(2)}) %collective-permute-start.23) | collective-permute-done | bytes 458784 | tf_op jit(solution)/shard_map/ppermute | solution.py:200
  200.8 1.1 shard_map.71
  (78 shorter events, 5.0 us)
Async XLA Ops:
  6.5 110.5 %all-gather.7.cloned.1.call-start = ((), (), s32[]{:S(2)}) async-start(), calls=%async_computation.1 | async-start | bytes 4718592 | tf_op jit(solution)/shard_map/all_gather | solution.py:130
  6.5 0.7 copy-start.2
  7.2 14.2 %copy-start.6 = (bf16[896,1024]{1,0:T(8,128)(2,1)S(1)}, bf16[896,1024]{1,0:T(8,128)(2,1)}, u32[]{:S(2)}) copy-start(bf16[896,1024]{1,0:T(8,128)(2,1)} %param.6) | copy-start | bytes 5505028
  7.2 15.3 %copy-start.4 = (bf16[896,1024]{1,0:T(8,128)(2,1)S(1)}, bf16[896,1024]{1,0:T(8,128)(2,1)}, u32[]{:S(2)}) copy-start(bf16[896,1024]{1,0:T(8,128)(2,1)} %param.7) | copy-start | bytes 5505028
  11.3 11.7 %copy-start.3 = (bf16[1,2,1024]{2,1,0:T(2,128)(2,1)S(1)}, bf16[1,2,1024]{2,1,0:T(2,128)(2,1)}, u32[]{:S(2)}) copy-start(bf16[1,2,1024]{2,1,0:T(2,128)(2,1)} %g_ref.3) | copy-start | bytes 12292
  11.3 18.7 %collective-permute-start = (bf16[2,256,1024]{2,1,0:T(8,128)(2,1)}, bf16[2,256,1024]{2,1,0:T(8,128)(2,1)}, u32[]{:S(2)}, u32[]{:S(2)}) collective-permute-start(bf16[2,256,1024]{2,1,0:T(8,128)(2,1)} %get-tuple-element.45), channel_id=1, source_target_pairs={{0,16},{1,17},{2,18},{3,19},{4,20},{5,21},{6,22},{7,23}} | collective-permute-start | bytes 3145736 | tf_op jit(solution)/shard_map/ppermute | solution.py:111
  15.7 22.9 %collective-permute-start.1 = (bf16[2,256,1024]{2,1,0:T(8,128)(2,1)}, bf16[2,256,1024]{2,1,0:T(8,128)(2,1)}, u32[]{:S(2)}, u32[]{:S(2)}) collective-permute-start(bf16[2,256,1024]{2,1,0:T(8,128)(2,1)} %get-tuple-element.46), channel_id=1, source_target_pairs={{0,32},{1,33},{2,34},{3,35},{4,36},{5,37},{6,38},{7,39}} | collective-permute-start | bytes 3145736 | tf_op jit(solution)/shard_map/ppermute | solution.py:111
  19.1 19.6 %collective-permute-start.2 = (bf16[2,256,1024]{2,1,0:T(8,128)(2,1)}, bf16[2,256,1024]{2,1,0:T(8,128)(2,1)}, u32[]{:S(2)}, u32[]{:S(2)}) collective-permute-start(bf16[2,256,1024]{2,1,0:T(8,128)(2,1)} %get-tuple-element.47), channel_id=1, source_target_pairs={{0,48},{1,49},{2,50},{3,51},{4,52},{5,53},{6,54},{7,55}} | collective-permute-start | bytes 3145736 | tf_op jit(solution)/shard_map/ppermute | solution.py:111
  23.0 4.1 %copy-start.5 = (bf16[896,1024]{1,0:T(8,128)(2,1)S(1)}, bf16[896,1024]{1,0:T(8,128)(2,1)}, u32[]{:S(2)}) copy-start(bf16[896,1024]{1,0:T(8,128)(2,1)} %param.7) | copy-start | bytes 5505028
  23.0 4.1 %copy-start.7 = (bf16[896,1024]{1,0:T(8,128)(2,1)S(1)}, bf16[896,1024]{1,0:T(8,128)(2,1)}, u32[]{:S(2)}) copy-start(bf16[896,1024]{1,0:T(8,128)(2,1)} %param.6) | copy-start | bytes 5505028
  40.0 13.6 %collective-permute-start.3 = (bf16[2,256,1024]{2,1,0:T(8,128)(2,1)S(1)}, bf16[2,256,1024]{2,1,0:T(8,128)(2,1)}, u32[]{:S(2)}, u32[]{:S(2)}) collective-permute-start(bf16[2,256,1024]{2,1,0:T(8,128)(2,1)S(1)} %select_select_fusion.1), channel_id=1, source_target_pairs={{0,128},{16,144},{32,160},{48,176},{1,129},{17,145},{33,161},{49,1... | collective-permute-start | bytes 3145736 | tf_op jit(solution)/shard_map/ppermute | solution.py:117
  42.3 13.9 %collective-permute-start.5 = (bf16[2,256,1024]{2,1,0:T(8,128)(2,1)}, bf16[2,256,1024]{2,1,0:T(8,128)(2,1)}, u32[]{:S(2)}, u32[]{:S(2)}) collective-permute-start(bf16[2,256,1024]{2,1,0:T(8,128)(2,1)} %get-tuple-element.55), channel_id=1, source_target_pairs={{0,16},{1,17},{2,18},{3,19},{4,20},{5,21},{6,22},{7,23}} | collective-permute-start | bytes 3145736 | tf_op jit(solution)/shard_map/ppermute | solution.py:111
  44.6 22.9 %collective-permute-start.6 = (bf16[2,256,1024]{2,1,0:T(8,128)(2,1)}, bf16[2,256,1024]{2,1,0:T(8,128)(2,1)}, u32[]{:S(2)}, u32[]{:S(2)}) collective-permute-start(bf16[2,256,1024]{2,1,0:T(8,128)(2,1)} %get-tuple-element.56), channel_id=1, source_target_pairs={{0,32},{1,33},{2,34},{3,35},{4,36},{5,37},{6,38},{7,39}} | collective-permute-start | bytes 3145736 | tf_op jit(solution)/shard_map/ppermute | solution.py:111
  50.8 16.6 %collective-permute-start.7 = (bf16[2,256,1024]{2,1,0:T(8,128)(2,1)}, bf16[2,256,1024]{2,1,0:T(8,128)(2,1)}, u32[]{:S(2)}, u32[]{:S(2)}) collective-permute-start(bf16[2,256,1024]{2,1,0:T(8,128)(2,1)} %get-tuple-element.57), channel_id=1, source_target_pairs={{0,48},{1,49},{2,50},{3,51},{4,52},{5,53},{6,54},{7,55}} | collective-permute-start | bytes 3145736 | tf_op jit(solution)/shard_map/ppermute | solution.py:111
  53.8 15.2 %collective-permute-start.4 = (bf16[2,256,1024]{2,1,0:T(8,128)(2,1)S(1)}, bf16[2,256,1024]{2,1,0:T(8,128)(2,1)}, u32[]{:S(2)}, u32[]{:S(2)}) collective-permute-start(bf16[2,256,1024]{2,1,0:T(8,128)(2,1)S(1)} %broadcast_select_fusion.1), channel_id=1, source_target_pairs={{0,64},{16,80},{32,96},{48,112},{128,192},{144,208},{160,224},{176... | collective-permute-start | bytes 3145736 | tf_op jit(solution)/shard_map/ppermute | solution.py:119
  69.1 27.9 %copy-start.12 = (s32[896]{0:T(1024)S(1)}, s32[896]{0:T(1024)}, u32[]{:S(2)}) copy-start(s32[896]{0:T(1024)} %param.11) | copy-start | bytes 10756
  69.2 2.8 %collective-permute-start.8 = (bf16[2,128,1024]{2,1,0:T(8,128)(2,1)S(1)}, bf16[2,128,1024]{2,1,0:T(8,128)(2,1)S(1)}, u32[]{:S(2)}, u32[]{:S(2)}) collective-permute-start(bf16[2,128,1024]{2,1,0:T(8,128)(2,1)S(1)} %slice.95), channel_id=1, source_target_pairs={{0,8},{16,24},{32,40},{48,56},{64,72},{80,88},{96,104},{112,120},{... | collective-permute-start | bytes 1572872 | tf_op jit(solution)/shard_map/ppermute | solution.py:125
  72.9 83.2 %all-gather.5.cloned.1.call-start = ((), (), s32[]{:S(2)}) async-start(), calls=%async_computation | async-start | bytes 4718592 | tf_op jit(solution)/shard_map/all_gather | solution.py:130
  72.9 17.4 %collective-permute-start.9 = (bf16[2,256,1024]{2,1,0:T(8,128)(2,1)S(1)}, bf16[2,256,1024]{2,1,0:T(8,128)(2,1)S(1)}, u32[]{:S(2)}, u32[]{:S(2)}) collective-permute-start(bf16[2,256,1024]{2,1,0:T(8,128)(2,1)S(1)} %select_select_fusion), channel_id=1, source_target_pairs={{0,128},{16,144},{32,160},{48,176},{1,129},{17,145},{33,161},{49,1... | collective-permute-start | bytes 3145736 | tf_op jit(solution)/shard_map/ppermute | solution.py:117
  90.5 22.0 %collective-permute-start.10 = (bf16[2,256,1024]{2,1,0:T(8,128)(2,1)S(1)}, bf16[2,256,1024]{2,1,0:T(8,128)(2,1)S(1)}, u32[]{:S(2)}, u32[]{:S(2)}) collective-permute-start(bf16[2,256,1024]{2,1,0:T(8,128)(2,1)S(1)} %broadcast_select_fusion), channel_id=1, source_target_pairs={{0,64},{16,80},{32,96},{48,112},{128,192},{144,208},{160,224},{176... | collective-permute-start | bytes 3145736 | tf_op jit(solution)/shard_map/ppermute | solution.py:119
  91.9 3.7 %collective-permute-start.11 = (f32[2,896]{1,0:T(2,128)S(1)}, f32[2,896]{1,0:T(2,128)S(1)}, u32[]{:S(2)}, u32[]{:S(2)}) collective-permute-start(f32[2,896]{1,0:T(2,128)S(1)} %pad_maximum_fusion.4), channel_id=1, source_target_pairs={{0,1},{1,0},{2,3},{3,2},{4,5},{5,4},{6,7},{7,6},{8,9},{9,8},{10,11... | collective-permute-start | bytes 21512 | tf_op jit(solution)/shard_map/ppermute | solution.py:277
  95.6 5.1 %collective-permute-start.12 = (f32[2,896]{1,0:T(2,128)S(1)}, f32[2,896]{1,0:T(2,128)S(1)}, u32[]{:S(2)}, u32[]{:S(2)}) collective-permute-start(f32[2,896]{1,0:T(2,128)S(1)} %add.156), channel_id=1, source_target_pairs={{0,2},{1,3},{2,0},{3,1},{4,6},{5,7},{6,4},{7,5},{8,10},{9,11},{10,... | collective-permute-start | bytes 21512 | tf_op jit(solution)/shard_map/ppermute | solution.py:277
  100.8 11.2 %collective-permute-start.13 = (f32[2,896]{1,0:T(2,128)S(1)}, f32[2,896]{1,0:T(2,128)S(1)}, u32[]{:S(2)}, u32[]{:S(2)}) collective-permute-start(f32[2,896]{1,0:T(2,128)S(1)} %add.157), channel_id=1, source_target_pairs={{0,4},{1,5},{2,6},{3,7},{4,0},{5,1},{6,2},{7,3},{8,12},{9,13},{10,... | collective-permute-start | bytes 21512 | tf_op jit(solution)/shard_map/ppermute | solution.py:277
  113.1 2.8 %collective-permute-start.14 = (bf16[2,128,1024]{2,1,0:T(8,128)(2,1)S(1)}, bf16[2,128,1024]{2,1,0:T(8,128)(2,1)S(1)}, u32[]{:S(2)}, u32[]{:S(2)}) collective-permute-start(bf16[2,128,1024]{2,1,0:T(8,128)(2,1)S(1)} %slice.97), channel_id=1, source_target_pairs={{0,8},{16,24},{32,40},{48,56},{64,72},{80,88},{96,104},{112,120},{... | collective-permute-start | bytes 1572872 | tf_op jit(solution)/shard_map/ppermute | solution.py:125
  122.2 13.4 %collective-permute-start.28 = (bf16[2,448,256]{2,1,0:T(8,128)(2,1)S(1)}, bf16[2,448,256]{2,1,0:T(8,128)(2,1)S(1)}, u32[]{:S(2)}, u32[]{:S(2)}) collective-permute-start(bf16[2,448,256]{2,1,0:T(8,128)(2,1)S(1)} %get-tuple-element.78), channel_id=1, source_target_pairs={{0,1},{1,2},{2,3},{3,0},{4,5},{5,6},{6,7},{7,4},{8,9},{9,10},{10,1... | collective-permute-start | bytes 1376264 | tf_op jit(solution)/shard_map/ppermute | solution.py:190
  122.8 14.6 %collective-permute-start.30 = (bf16[2,448,256]{2,1,0:T(8,128)(2,1)S(1)}, bf16[2,448,256]{2,1,0:T(8,128)(2,1)S(1)}, u32[]{:S(2)}, u32[]{:S(2)}) collective-permute-start(bf16[2,448,256]{2,1,0:T(8,128)(2,1)S(1)} %get-tuple-element.79), channel_id=1, source_target_pairs={{0,3},{1,0},{2,1},{3,2},{4,7},{5,4},{6,5},{7,6},{8,11},{9,8},{10,9... | collective-permute-start | bytes 1376264 | tf_op jit(solution)/shard_map/ppermute | solution.py:191
  129.5 17.7 %copy-start = (bf16[4,448,256]{2,1,0:T(8,128)(2,1)}, bf16[4,448,256]{2,1,0:T(8,128)(2,1)S(1)}, u32[]{:S(2)}) copy-start(bf16[4,448,256]{2,1,0:T(8,128)(2,1)S(1)} %get-tuple-element.67) | copy-start | bytes 2752516
  129.5 16.0 %collective-permute-start.19 = (bf16[2,448,256]{2,1,0:T(8,128)(2,1)S(1)}, bf16[2,448,256]{2,1,0:T(8,128)(2,1)S(1)}, u32[]{:S(2)}, u32[]{:S(2)}) collective-permute-start(bf16[2,448,256]{2,1,0:T(8,128)(2,1)S(1)} %get-tuple-element.68), channel_id=1, source_target_pairs={{0,1},{1,2},{2,3},{3,0},{4,5},{5,6},{6,7},{7,4},{8,9},{9,10},{10,1... | collective-permute-start | bytes 1376264 | tf_op jit(solution)/shard_map/ppermute | solution.py:190
  131.3 15.9 %collective-permute-start.21 = (bf16[2,448,256]{2,1,0:T(8,128)(2,1)S(1)}, bf16[2,448,256]{2,1,0:T(8,128)(2,1)S(1)}, u32[]{:S(2)}, u32[]{:S(2)}) collective-permute-start(bf16[2,448,256]{2,1,0:T(8,128)(2,1)S(1)} %get-tuple-element.69), channel_id=1, source_target_pairs={{0,3},{1,0},{2,1},{3,2},{4,7},{5,4},{6,5},{7,6},{8,11},{9,8},{10,9... | collective-permute-start | bytes 1376264 | tf_op jit(solution)/shard_map/ppermute | solution.py:191
  137.5 12.7 %collective-permute-start.29 = (bf16[448,256]{1,0:T(8,128)(2,1)S(1)}, bf16[448,256]{1,0:T(8,128)(2,1)S(1)}, u32[]{:S(2)}, u32[]{:S(2)}) collective-permute-start(bf16[448,256]{1,0:T(8,128)(2,1)S(1)} %get-tuple-element.87), channel_id=1, source_target_pairs={{0,1},{1,2},{2,3},{3,0},{4,5},{5,6},{6,7},{7,4},{8,9},{9,10},{10,1... | collective-permute-start | bytes 688136 | tf_op jit(solution)/shard_map/ppermute | solution.py:192
  137.8 13.5 %collective-permute-start.31 = (bf16[448,256]{1,0:T(8,128)(2,1)S(1)}, bf16[448,256]{1,0:T(8,128)(2,1)S(1)}, u32[]{:S(2)}, u32[]{:S(2)}) collective-permute-start(bf16[448,256]{1,0:T(8,128)(2,1)S(1)} %get-tuple-element.88), channel_id=1, source_target_pairs={{0,3},{1,0},{2,1},{3,2},{4,7},{5,4},{6,5},{7,6},{8,11},{9,8},{10,9... | collective-permute-start | bytes 688136 | tf_op jit(solution)/shard_map/ppermute | solution.py:193
  145.5 6.9 %copy-start.8 = (bf16[2,448,256]{2,1,0:T(8,128)(2,1)}, bf16[2,448,256]{2,1,0:T(8,128)(2,1)S(1)}, u32[]{:S(2)}) copy-start(bf16[2,448,256]{2,1,0:T(8,128)(2,1)S(1)} %collective-permute-done.19) | copy-start | bytes 1376260
  147.2 5.2 %copy-start.10 = (bf16[2,448,256]{2,1,0:T(8,128)(2,1)}, bf16[2,448,256]{2,1,0:T(8,128)(2,1)S(1)}, u32[]{:S(2)}) copy-start(bf16[2,448,256]{2,1,0:T(8,128)(2,1)S(1)} %collective-permute-done.21) | copy-start | bytes 1376260
  148.1 20.5 %collective-permute-start.20 = (bf16[448,256]{1,0:T(8,128)(2,1)}, bf16[448,256]{1,0:T(8,128)(2,1)S(1)}, u32[]{:S(2)}, u32[]{:S(2)}) collective-permute-start(bf16[448,256]{1,0:T(8,128)(2,1)} %get-tuple-element.93), channel_id=1, source_target_pairs={{0,1},{1,2},{2,3},{3,0},{4,5},{5,6},{6,7},{7,4},{8,9},{9,10},{10,1... | collective-permute-start | bytes 688136 | tf_op jit(solution)/shard_map/ppermute | solution.py:192
  148.4 22.2 %collective-permute-start.22 = (bf16[448,256]{1,0:T(8,128)(2,1)}, bf16[448,256]{1,0:T(8,128)(2,1)}, u32[]{:S(2)}, u32[]{:S(2)}) collective-permute-start(bf16[448,256]{1,0:T(8,128)(2,1)} %get-tuple-element.94), channel_id=1, source_target_pairs={{0,3},{1,0},{2,1},{3,2},{4,7},{5,4},{6,5},{7,6},{8,11},{9,8},{10,9... | collective-permute-start | bytes 688136 | tf_op jit(solution)/shard_map/ppermute | solution.py:193
  152.4 35.7 %collective-permute-start.32 = (bf16[2,448,256]{2,1,0:T(8,128)(2,1)}, bf16[2,448,256]{2,1,0:T(8,128)(2,1)S(1)}, u32[]{:S(2)}, u32[]{:S(2)}) collective-permute-start(bf16[2,448,256]{2,1,0:T(8,128)(2,1)} %pad_maximum_fusion.3), channel_id=1, source_target_pairs={{0,4},{1,5},{2,6},{3,7},{4,0},{5,1},{6,2},{7,3},{8,12},{9,13},{10,... | collective-permute-start | bytes 1376264 | tf_op jit(solution)/shard_map/ppermute | solution.py:200
  161.3 13.5 %collective-permute-start.24 = (bf16[2,448,256]{2,1,0:T(8,128)(2,1)S(1)}, bf16[2,448,256]{2,1,0:T(8,128)(2,1)S(1)}, u32[]{:S(2)}, u32[]{:S(2)}) collective-permute-start(bf16[2,448,256]{2,1,0:T(8,128)(2,1)S(1)} %get-tuple-element.75), channel_id=1, source_target_pairs={{0,1},{1,2},{2,3},{3,0},{4,5},{5,6},{6,7},{7,4},{8,9},{9,10},{10,1... | collective-permute-start | bytes 1376264 | tf_op jit(solution)/shard_map/ppermute | solution.py:190
  162.1 8.6 %copy-start.1 = (bf16[4,448,256]{2,1,0:T(8,128)(2,1)S(1)}, bf16[4,448,256]{2,1,0:T(8,128)(2,1)}, u32[]{:S(2)}) copy-start(bf16[4,448,256]{2,1,0:T(8,128)(2,1)} %copy-done) | copy-start | bytes 2752516
  162.1 8.6 %copy-start.9 = (bf16[2,448,256]{2,1,0:T(8,128)(2,1)S(1)}, bf16[2,448,256]{2,1,0:T(8,128)(2,1)}, u32[]{:S(2)}) copy-start(bf16[2,448,256]{2,1,0:T(8,128)(2,1)} %copy-done.8) | copy-start | bytes 1376260
  162.1 8.6 %copy-start.11 = (bf16[2,448,256]{2,1,0:T(8,128)(2,1)S(1)}, bf16[2,448,256]{2,1,0:T(8,128)(2,1)}, u32[]{:S(2)}) copy-start(bf16[2,448,256]{2,1,0:T(8,128)(2,1)} %copy-done.10) | copy-start | bytes 1376260
  162.1 15.1 %collective-permute-start.25 = (bf16[2,448,256]{2,1,0:T(8,128)(2,1)S(1)}, bf16[2,448,256]{2,1,0:T(8,128)(2,1)S(1)}, u32[]{:S(2)}, u32[]{:S(2)}) collective-permute-start(bf16[2,448,256]{2,1,0:T(8,128)(2,1)S(1)} %get-tuple-element.76), channel_id=1, source_target_pairs={{0,3},{1,0},{2,1},{3,2},{4,7},{5,4},{6,5},{7,6},{8,11},{9,8},{10,9... | collective-permute-start | bytes 1376264 | tf_op jit(solution)/shard_map/ppermute | solution.py:191
  168.6 16.1 %collective-permute-start.15 = (bf16[2,448,256]{2,1,0:T(8,128)(2,1)S(1)}, bf16[2,448,256]{2,1,0:T(8,128)(2,1)S(1)}, u32[]{:S(2)}, u32[]{:S(2)}) collective-permute-start(bf16[2,448,256]{2,1,0:T(8,128)(2,1)S(1)} %get-tuple-element.65), channel_id=1, source_target_pairs={{0,1},{1,2},{2,3},{3,0},{4,5},{5,6},{6,7},{7,4},{8,9},{9,10},{10,1... | collective-permute-start | bytes 1376264 | tf_op jit(solution)/shard_map/ppermute | solution.py:190
  170.6 14.5 %collective-permute-start.16 = (bf16[2,448,256]{2,1,0:T(8,128)(2,1)S(1)}, bf16[2,448,256]{2,1,0:T(8,128)(2,1)S(1)}, u32[]{:S(2)}, u32[]{:S(2)}) collective-permute-start(bf16[2,448,256]{2,1,0:T(8,128)(2,1)S(1)} %get-tuple-element.66), channel_id=1, source_target_pairs={{0,3},{1,0},{2,1},{3,2},{4,7},{5,4},{6,5},{7,6},{8,11},{9,8},{10,9... | collective-permute-start | bytes 1376264 | tf_op jit(solution)/shard_map/ppermute | solution.py:191
  174.8 26.0 %collective-permute-start.23 = (bf16[2,448,256]{2,1,0:T(8,128)(2,1)S(1)}, bf16[2,448,256]{2,1,0:T(8,128)(2,1)S(1)}, u32[]{:S(2)}, u32[]{:S(2)}) collective-permute-start(bf16[2,448,256]{2,1,0:T(8,128)(2,1)S(1)} %pad_maximum_fusion.2), channel_id=1, source_target_pairs={{0,4},{1,5},{2,6},{3,7},{4,0},{5,1},{6,2},{7,3},{8,12},{9,13},{10,... | collective-permute-start | bytes 1376264 | tf_op jit(solution)/shard_map/ppermute | solution.py:200
  177.3 12.3 %collective-permute-start.26 = (bf16[448,256]{1,0:T(8,128)(2,1)S(1)}, bf16[448,256]{1,0:T(8,128)(2,1)S(1)}, u32[]{:S(2)}, u32[]{:S(2)}) collective-permute-start(bf16[448,256]{1,0:T(8,128)(2,1)S(1)} %get-tuple-element.90), channel_id=1, source_target_pairs={{0,1},{1,2},{2,3},{3,0},{4,5},{5,6},{6,7},{7,4},{8,9},{9,10},{10,1... | collective-permute-start | bytes 688136 | tf_op jit(solution)/shard_map/ppermute | solution.py:192
  184.7 7.5 %collective-permute-start.27 = (bf16[448,256]{1,0:T(8,128)(2,1)S(1)}, bf16[448,256]{1,0:T(8,128)(2,1)S(1)}, u32[]{:S(2)}, u32[]{:S(2)}) collective-permute-start(bf16[448,256]{1,0:T(8,128)(2,1)S(1)} %get-tuple-element.89), channel_id=1, source_target_pairs={{0,3},{1,0},{2,1},{3,2},{4,7},{5,4},{6,5},{7,6},{8,11},{9,8},{10,9... | collective-permute-start | bytes 688136 | tf_op jit(solution)/shard_map/ppermute | solution.py:193
  185.2 15.6 %collective-permute-start.17 = (bf16[448,256]{1,0:T(8,128)(2,1)S(1)}, bf16[448,256]{1,0:T(8,128)(2,1)S(1)}, u32[]{:S(2)}, u32[]{:S(2)}) collective-permute-start(bf16[448,256]{1,0:T(8,128)(2,1)S(1)} %get-tuple-element.96), channel_id=1, source_target_pairs={{0,1},{1,2},{2,3},{3,0},{4,5},{5,6},{6,7},{7,4},{8,9},{9,10},{10,1... | collective-permute-start | bytes 688136 | tf_op jit(solution)/shard_map/ppermute | solution.py:192
  188.1 12.7 %collective-permute-start.18 = (bf16[448,256]{1,0:T(8,128)(2,1)S(1)}, bf16[448,256]{1,0:T(8,128)(2,1)S(1)}, u32[]{:S(2)}, u32[]{:S(2)}) collective-permute-start(bf16[448,256]{1,0:T(8,128)(2,1)S(1)} %get-tuple-element.95), channel_id=1, source_target_pairs={{0,3},{1,0},{2,1},{3,2},{4,7},{5,4},{6,5},{7,6},{8,11},{9,8},{10,9... | collective-permute-start | bytes 688136 | tf_op jit(solution)/shard_map/ppermute | solution.py:193
Sparse Core Ops, SparseCore 0:
  73.0 41.4 all-gather.6
  117.0 35.7 all-gather.4

commit v5 on v4

--- a/solution.py
+++ b/solution.py
@@ -66,7 +66,7 @@
 
 
 def pieces_kernel(flags, w_ref, g_ref, *refs):
-    out_refs, raw, sems = refs[:NY], refs[NY], refs[NY + 1]
+    out_refs, (raw, near, sems) = refs[:NY], refs[NY:]
     depth, wide = out_refs[0].shape[1:]
     column = pl.multiple_of(flags[0] * wide, wide)
 
@@ -75,11 +75,14 @@
         return pltpu.make_async_copy(w_ref.at[0, :, rows, pl.ds(column, wide)], raw.at[y], sems.at[y])
 
     order = (2, 1, 3, 0)
+    gain_copy = pltpu.make_async_copy(g_ref, near, sems.at[NY])
+    gain_copy.start()
     for y in order:
         read(y).start()
+    gain_copy.wait()
     gains = []
     for layer in range(LAYERS):
-        row = g_ref[0, layer:layer + 1, :].astype(jnp.float32)
+        row = near[0, layer:layer + 1, :].astype(jnp.float32)
         gains.append(jnp.broadcast_to(row, (HD, row.shape[1])).T)
     for y in order:
         read(y).wait()
@@ -96,9 +99,9 @@
     return pl.pallas_call(
         pieces_kernel,
         out_shape=tuple(jax.ShapeDtypeStruct(shape, LOW) for _ in range(NY)),
-        in_specs=[pl.BlockSpec(memory_space=pltpu.SMEM), pl.BlockSpec(memory_space=pltpu.HBM), vmem],
+        in_specs=[pl.BlockSpec(memory_space=pltpu.SMEM), pl.BlockSpec(memory_space=pltpu.HBM), pl.BlockSpec(memory_space=pltpu.HBM)],
         out_specs=tuple(vmem for _ in range(NY)),
-        scratch_shapes=[pltpu.VMEM((NY, *shape), LOW), pltpu.SemaphoreType.DMA((NY,))],
+        scratch_shapes=[pltpu.VMEM((NY, *shape), LOW), pltpu.VMEM(gains.shape, LOW), pltpu.SemaphoreType.DMA((NY + 1,))],
         compiler_params=pltpu.CompilerParams(vmem_limit_bytes=VMEM_LARGE),
         cost_estimate=pl.CostEstimate(
             flops=LAYERS * NY * depth * wide, bytes_accessed=4 * LAYERS * NY * depth * wide, transcendentals=0
@@ -133,18 +136,22 @@
 def product_kernel(layer, first, flags, x_ref, own_ref, src_ref, plus_ref, minus_ref, keep_ref, blocks, sems):
     held = flags[layer] > 0
     cut = x_ref.shape[0] // 2
+
+    def goal_of(j):
+        return blocks.at[j // 2, :, :, pl.ds(j % 2 * WIDE, WIDE)]
+
     for j in range(NX):
         head = flags[first + j]
 
         @pl.when(held)
         def _():
             column = pl.ds(pl.multiple_of(head * WIDE, WIDE), WIDE)
-            pltpu.make_async_copy(own_ref.at[0, layer, :, :, column], blocks.at[j], sems.at[j]).start()
+            pltpu.make_async_copy(own_ref.at[0, layer, :, :, column], goal_of(j), sems.at[j]).start()
 
         @pl.when(jnp.logical_not(held))
         def _():
             column = pl.ds(pl.multiple_of(head % NX * WIDE, WIDE), WIDE)
-            pltpu.make_async_copy(src_ref.at[:, layer, :, column], blocks.at[j], sems.at[j]).start()
+            pltpu.make_async_copy(src_ref.at[:, layer, :, column], goal_of(j), sems.at[j]).start()
 
     low, high = slice(0, cut), slice(cut, 2 * cut)
     goals = (
@@ -153,11 +160,16 @@
         ((minus_ref, 1, low), (keep_ref, 1, high)),
         ((keep_ref, 2, low), (keep_ref, 3, high)),
     )
-    for j, goal in enumerate(goals):
-        pltpu.make_async_copy(src_ref.at[:, layer, :, pl.ds(0, WIDE)], blocks.at[j], sems.at[j]).wait()
-        block = blocks[j].reshape(-1, WIDE)
-        for ref, slot, rows in goal:
-            ref[slot] = dot(x_ref[rows, :], block).astype(LOW)
+    for pair in range(NX // 2):
+        for j in (2 * pair, 2 * pair + 1):
+            pltpu.make_async_copy(src_ref.at[:, layer, :, pl.ds(0, WIDE)], goal_of(j), sems.at[j]).wait()
+        block = blocks[pair].reshape(-1, 2 * WIDE)
+        for rows in (low, high):
+            total = dot(x_ref[rows, :], block).astype(LOW)
+            for k in range(2):
+                for ref, slot, where in goals[2 * pair + k]:
+                    if where == rows:
+                        ref[slot] = total[:, k * WIDE:(k + 1) * WIDE]
 
 
 def product(flags, x, own, layer, src, which):
@@ -170,7 +182,7 @@
         in_specs=[pl.BlockSpec(memory_space=pltpu.SMEM), vmem, hbm, hbm],
         out_specs=(vmem, vmem, vmem),
         scratch_shapes=[
-            pltpu.VMEM((NX, 2 * NY, depth // (2 * NY), WIDE), LOW),
+            pltpu.VMEM((NX // 2, 2 * NY, depth // (2 * NY), 2 * WIDE), LOW),
             pltpu.SemaphoreType.DMA((NX,)),
         ],
         compiler_params=pltpu.CompilerParams(vmem_limit_bytes=VMEM_LARGE),
@@ -271,13 +283,18 @@
     swap, keep = lax.optimization_barrier((swap, keep))
     swap_half = across(swap)
     swap_src = gather(swap_half)
-    keep = down(after(keep, swap_half))
+    z = place()[2]
+    far = lax.ppermute(after(keep, swap_half), "chain", Z_FAR)
     squares = after(squares, swap_half)
-    for pairs in (X_ONE, X_TWO, H_SWAP):
+    squares = squares + lax.ppermute(squares, "tp", H_SWAP)
+    far, squares = lax.optimization_barrier((far, squares))
+    second = jnp.where(z == 2, far, keep)
+    near = lax.ppermute(second, "chain", Z_NEAR)
+    for pairs in (X_ONE, X_TWO):
         squares = squares + lax.ppermute(squares, "tp", pairs)
     turns = turns_of(squares, width, positions)
-    keep, turns = lax.optimization_barrier((keep, turns))
-    keep_src = gather(across(keep))
+    near, turns = lax.optimization_barrier((near, turns))
+    keep_src = gather(across(jnp.where((z == 1) | (z == 3), near, second)))
 
     def sums(layer, src, which):
         return product(flags, scaled[layer], own, layer, src, which)

time: 210 us -> 206 us (0.981); the launches traced: 209 us -> 202 us
  waiting for transfers between devices: 79.3 us -> 73.6 us
    ppermute x0 -> x3, waiting for transfers between devices: none -> 15.6 us  [the longest x1 12.8 us: shards(): squares = squares + lax.ppermute(squares, 'tp', H_SWAP)]
    ppermute x0 -> x3, starting transfers between devices: none -> 13.7 us  [the longest x1 7.28 us: shards(): squares = squares + lax.ppermute(squares, 'tp', H_SWAP)]
    ppermute x2 -> x1, waiting for transfers between devices: 12.9 us -> 0.54 us  [down(): far = lax.ppermute(first, 'chain', Z_FAR)]
    ppermute x2, waiting for transfers between devices: 7.55 us -> 0.01 us  [swapped(): return lax.ppermute(jnp.stack([low, high]).astype(LOW), 'tp', H_SWAP)]
    ppermute x3 -> x2, starting transfers between devices: 9.51 us -> 2.32 us  [shards(): squares = squares + lax.ppermute(squares, 'tp', pairs)]
    ppermute x2 -> x1, starting transfers between devices: 7.31 us -> 2.27 us  [down(): far = lax.ppermute(first, 'chain', Z_FAR)]
    ppermute x3 -> x2, waiting for transfers between devices: 8.84 us -> 4.85 us  [shards(): squares = squares + lax.ppermute(squares, 'tp', pairs)]
  transfers between devices with their start and end apart: 35 -> 35, of which waited for: 20 -> 21; matrix products, arithmetic and copies ran while one was open for 6% -> 6% of each run, Pallas kernels for 12% -> 12%
where the time goes in v5:
time: 206 us; the launch traced here: 202 us
  waiting for transfers between devices  73.6 us (36%)
  starting transfers between devices  68.1 us (33%)
  Pallas kernels  30.2 us (15%)
  other arithmetic  14.7 us (7%)
  between operations  14.5 us (7%)
    ppermute x6, starting transfers between devices, scatter(): lax.ppermute(parts[k], 'chain', from_source(k))  20.9 us
    ppermute x6, waiting for transfers between devices, scatter(): lax.ppermute(parts[k], 'chain', from_source(k))  20 us
    pallas_call x4, Pallas kernels, product(): pl.pallas_call(functools.partial(product_kernel, layer, COLUMNS + which *...  20 us
    ppermute x4, waiting for transfers between devices, round_x(): plus1 = lax.ppermute(plus, 'tp', X_NEXT)  19 us
    ppermute x1, waiting for transfers between devices, shards(): squares = squares + lax.ppermute(squares, 'tp', H_SWAP)  12.8 us
    pallas_call x2, Pallas kernels, pieces(): pl.pallas_call(pieces_kernel, out_shape=tuple((jax.ShapeDtypeStruct(shape...  8.06 us
    ppermute x1, starting transfers between devices, shards(): squares = squares + lax.ppermute(squares, 'tp', H_SWAP)  7.28 us
    ppermute x2, starting transfers between devices, swapped(): return lax.ppermute(jnp.stack([low, high]).astype(LOW), 'tp', H_SWAP)  5.91 us
  transfers between devices with their start and end apart: 35, of which 21 were waited for; matrix products, arithmetic and copies ran while one was open for 6% of the time, Pallas kernels for 12%

profile of v5, /device:TPU:6, one launch (start us, length us, event | category | flops | bytes accessed | tf_op | source)
XLA Modules:
  0.0 202.5 jit_solution(8105902308371842243)
XLA Ops:
  6.5 0.7 copy-done.2
  7.2 4.0 %shard_map.64 = (bf16[2,256,1024]{2,1,0:T(8,128)(2,1)S(1)}, bf16[2,256,1024]{2,1,0:T(8,128)(2,1)}, bf16[2,256,1024]{2,1,0:T(8,128)(2,1)}, bf16[2,256,1024]{2,1,0:T(8,128)(2,1)}) custom-call(s32[1]{0:T(128)} %bitcast.8.flags, bf16[1,2,1024,2048]{3,2,1,0:T(8,128)(2,1)} %w_ref.3, bf16[1,2,1024]{2,1,0:T(2,128)(2,1)S(1)} %copy-done.2), custom_call_target="tpu_custom_call" | custom-call | flops 2097152 | bytes 8388608 | tf_op jit(solution)/shard_map/pallas_call | solution.py:99
  11.3 4.5 %collective-permute-start = (bf16[2,256,1024]{2,1,0:T(8,128)(2,1)}, bf16[2,256,1024]{2,1,0:T(8,128)(2,1)}, u32[]{:S(2)}, u32[]{:S(2)}) collective-permute-start(bf16[2,256,1024]{2,1,0:T(8,128)(2,1)} %get-tuple-element.47), channel_id=1, source_target_pairs={{0,16},{1,17},{2,18},{3,19},{4,20},{5,21},{6,22},{7,23}} | collective-permute-start | bytes 3145736 | tf_op jit(solution)/shard_map/ppermute | solution.py:114
  15.8 3.3 %collective-permute-start.1 = (bf16[2,256,1024]{2,1,0:T(8,128)(2,1)}, bf16[2,256,1024]{2,1,0:T(8,128)(2,1)}, u32[]{:S(2)}, u32[]{:S(2)}) collective-permute-start(bf16[2,256,1024]{2,1,0:T(8,128)(2,1)} %get-tuple-element.48), channel_id=1, source_target_pairs={{0,32},{1,33},{2,34},{3,35},{4,36},{5,37},{6,38},{7,39}} | collective-permute-start | bytes 3145736 | tf_op jit(solution)/shard_map/ppermute | solution.py:114
  19.1 2.3 %collective-permute-start.2 = (bf16[2,256,1024]{2,1,0:T(8,128)(2,1)}, bf16[2,256,1024]{2,1,0:T(8,128)(2,1)}, u32[]{:S(2)}, u32[]{:S(2)}) collective-permute-start(bf16[2,256,1024]{2,1,0:T(8,128)(2,1)} %get-tuple-element.49), channel_id=1, source_target_pairs={{0,48},{1,49},{2,50},{3,51},{4,52},{5,53},{6,54},{7,55}} | collective-permute-start | bytes 3145736 | tf_op jit(solution)/shard_map/ppermute | solution.py:114
  23.0 4.0 %shard_map.65 = (bf16[2,256,1024]{2,1,0:T(8,128)(2,1)S(1)}, bf16[2,256,1024]{2,1,0:T(8,128)(2,1)}, bf16[2,256,1024]{2,1,0:T(8,128)(2,1)}, bf16[2,256,1024]{2,1,0:T(8,128)(2,1)}) custom-call(s32[1]{0:T(128)} %bitcast.9.flags, bf16[1,2,1024,2048]{3,2,1,0:T(8,128)(2,1)} %w_ref.3, bf16[1,2,1024]{2,1,0:T(2,128)(2,1)S(1)} %copy-done.3), custom_call_target="tpu_custom_call" | custom-call | flops 2097152 | bytes 8388608 | tf_op jit(solution)/shard_map/pallas_call | solution.py:99
  27.1 2.9 %fusion.4 = (bf16[896,1024]{1,0:T(8,128)(2,1)}, bf16[896,1024]{1,0:T(8,128)(2,1)}) fusion(bf16[896,1024]{1,0:T(8,128)(2,1)S(1)} %copy-done.5, f32[1024]{0:T(1024)S(1)} %bitcast.81, pred[]{:T(512)} %bitcast.12, bf16[896,1024]{1,0:T(8,128)(2,1)S(1)} %copy-done.7, f32[1024]{0:T(1024)S(1)} %bitcast.82, pred[]{:T(512)} %bitcast.10), kind=kLoop, calls=%fused_computation.8 | loop fusion | flops 7340032 | bytes 7348226 | tf_op jit(solution)/shard_map/jit(_where)/select_n | solution.py:276
  30.0 8.6 %collective-permute-done.1 = bf16[2,256,1024]{2,1,0:T(8,128)(2,1)} collective-permute-done((bf16[2,256,1024]{2,1,0:T(8,128)(2,1)}, bf16[2,256,1024]{2,1,0:T(8,128)(2,1)}, u32[]{:S(2)}, u32[]{:S(2)}) %collective-permute-start.1) | collective-permute-done | bytes 1048608 | tf_op jit(solution)/shard_map/ppermute | solution.py:114
  38.6 1.4 select_select_fusion.1
  40.0 2.3 %collective-permute-start.3 = (bf16[2,256,1024]{2,1,0:T(8,128)(2,1)S(1)}, bf16[2,256,1024]{2,1,0:T(8,128)(2,1)}, u32[]{:S(2)}, u32[]{:S(2)}) collective-permute-start(bf16[2,256,1024]{2,1,0:T(8,128)(2,1)S(1)} %select_select_fusion.1), channel_id=1, source_target_pairs={{0,128},{16,144},{32,160},{48,176},{1,129},{17,145},{33,161},{49,1... | collective-permute-start | bytes 3145736 | tf_op jit(solution)/shard_map/ppermute | solution.py:120
  42.3 2.3 %collective-permute-start.5 = (bf16[2,256,1024]{2,1,0:T(8,128)(2,1)}, bf16[2,256,1024]{2,1,0:T(8,128)(2,1)}, u32[]{:S(2)}, u32[]{:S(2)}) collective-permute-start(bf16[2,256,1024]{2,1,0:T(8,128)(2,1)} %get-tuple-element.57), channel_id=1, source_target_pairs={{0,16},{1,17},{2,18},{3,19},{4,20},{5,21},{6,22},{7,23}} | collective-permute-start | bytes 3145736 | tf_op jit(solution)/shard_map/ppermute | solution.py:114
  44.6 6.2 %collective-permute-start.6 = (bf16[2,256,1024]{2,1,0:T(8,128)(2,1)}, bf16[2,256,1024]{2,1,0:T(8,128)(2,1)}, u32[]{:S(2)}, u32[]{:S(2)}) collective-permute-start(bf16[2,256,1024]{2,1,0:T(8,128)(2,1)} %get-tuple-element.58), channel_id=1, source_target_pairs={{0,32},{1,33},{2,34},{3,35},{4,36},{5,37},{6,38},{7,39}} | collective-permute-start | bytes 3145736 | tf_op jit(solution)/shard_map/ppermute | solution.py:114
  50.8 2.3 %collective-permute-start.7 = (bf16[2,256,1024]{2,1,0:T(8,128)(2,1)}, bf16[2,256,1024]{2,1,0:T(8,128)(2,1)}, u32[]{:S(2)}, u32[]{:S(2)}) collective-permute-start(bf16[2,256,1024]{2,1,0:T(8,128)(2,1)} %get-tuple-element.59), channel_id=1, source_target_pairs={{0,48},{1,49},{2,50},{3,51},{4,52},{5,53},{6,54},{7,55}} | collective-permute-start | bytes 3145736 | tf_op jit(solution)/shard_map/ppermute | solution.py:114
  53.1 0.5 collective-permute-done.3
  53.8 2.3 %collective-permute-start.4 = (bf16[2,256,1024]{2,1,0:T(8,128)(2,1)S(1)}, bf16[2,256,1024]{2,1,0:T(8,128)(2,1)}, u32[]{:S(2)}, u32[]{:S(2)}) collective-permute-start(bf16[2,256,1024]{2,1,0:T(8,128)(2,1)S(1)} %broadcast_select_fusion.1), channel_id=1, source_target_pairs={{0,64},{16,80},{32,96},{48,112},{128,192},{144,208},{160,224},{176... | collective-permute-start | bytes 3145736 | tf_op jit(solution)/shard_map/ppermute | solution.py:122
  56.2 11.2 %collective-permute-done.6 = bf16[2,256,1024]{2,1,0:T(8,128)(2,1)} collective-permute-done((bf16[2,256,1024]{2,1,0:T(8,128)(2,1)}, bf16[2,256,1024]{2,1,0:T(8,128)(2,1)}, u32[]{:S(2)}, u32[]{:S(2)}) %collective-permute-start.6) | collective-permute-done | bytes 1048608 | tf_op jit(solution)/shard_map/ppermute | solution.py:114
  67.5 1.5 select_select_fusion
  69.2 1.3 collective-permute-start.8
  70.5 1.5 collective-permute-done.8
  72.0 0.8 slice_select_fusion.1
  72.9 5.0 %collective-permute-start.9 = (bf16[2,256,1024]{2,1,0:T(8,128)(2,1)S(1)}, bf16[2,256,1024]{2,1,0:T(8,128)(2,1)S(1)}, u32[]{:S(2)}, u32[]{:S(2)}) collective-permute-start(bf16[2,256,1024]{2,1,0:T(8,128)(2,1)S(1)} %select_select_fusion), channel_id=1, source_target_pairs={{0,128},{16,144},{32,160},{48,176},{1,129},{17,145},{33,161},{49,1... | collective-permute-start | bytes 3145736 | tf_op jit(solution)/shard_map/ppermute | solution.py:287
  78.0 7.3 %collective-permute-start.10 = (f32[2,896]{1,0:T(2,128)S(1)}, f32[2,896]{1,0:T(2,128)S(1)}, u32[]{:S(2)}, u32[]{:S(2)}) collective-permute-start(f32[2,896]{1,0:T(2,128)S(1)} %pad_maximum_fusion.4), channel_id=1, source_target_pairs={{0,4},{1,5},{2,6},{3,7},{4,0},{5,1},{6,2},{7,3},{8,12},{9,13},{10,... | collective-permute-start | bytes 21512 | tf_op jit(solution)/shard_map/ppermute | solution.py:289
  85.3 12.8 %collective-permute-done.10 = f32[2,896]{1,0:T(2,128)S(1)} collective-permute-done((f32[2,896]{1,0:T(2,128)S(1)}, f32[2,896]{1,0:T(2,128)S(1)}, u32[]{:S(2)}, u32[]{:S(2)}) %collective-permute-start.10) | collective-permute-done | bytes 7200 | tf_op jit(solution)/shard_map/ppermute | solution.py:289
  98.3 1.4 collective-permute-start.11
  99.6 0.9 collective-permute-start.12
  100.6 2.8 %collective-permute-done.12 = f32[2,896]{1,0:T(2,128)S(1)} collective-permute-done((f32[2,896]{1,0:T(2,128)S(1)}, f32[2,896]{1,0:T(2,128)S(1)}, u32[]{:S(2)}, u32[]{:S(2)}) %collective-permute-start.12) | collective-permute-done | bytes 7200 | tf_op jit(solution)/shard_map/ppermute | solution.py:294
  103.3 1.4 collective-permute-start.13
  104.8 1.7 fusion.24
  106.4 2.1 %collective-permute-done.13 = f32[2,896]{1,0:T(2,128)S(1)} collective-permute-done((f32[2,896]{1,0:T(2,128)S(1)}, f32[2,896]{1,0:T(2,128)S(1)}, u32[]{:S(2)}, u32[]{:S(2)}) %collective-permute-start.13) | collective-permute-done | bytes 7200 | tf_op jit(solution)/shard_map/ppermute | solution.py:294
  109.1 2.8 %collective-permute-done.11 = bf16[2,256,1024]{2,1,0:T(8,128)(2,1)S(1)} collective-permute-done((bf16[2,256,1024]{2,1,0:T(8,128)(2,1)S(1)}, bf16[2,256,1024]{2,1,0:T(8,128)(2,1)S(1)}, u32[]{:S(2)}, u32[]{:S(2)}) %collective-permute-start.11) | collective-permute-done | bytes 1048608 | tf_op jit(solution)/shard_map/ppermute | solution.py:292
  112.4 1.5 collective-permute-start.14
  113.9 1.3 collective-permute-done.14
  115.2 0.9 slice_select_fusion
  116.3 5.0 %shard_map.69 = (bf16[2,448,256]{2,1,0:T(8,128)(2,1)S(1)}, bf16[2,448,256]{2,1,0:T(8,128)(2,1)S(1)}, bf16[4,448,256]{2,1,0:T(8,128)(2,1)S(1)}) custom-call(s32[10]{0:T(128)S(1)} %stack.78.flags, bf16[896,1024]{1,0:T(8,128)(2,1)} %get-tuple-element.77.x_ref, bf16[1,2,8,128,2048]{4,3,2,1,0:T(8,128)(2,1)} %bitcast.73, bf16[8,2,128,1024]{3,2,1,0:T(8,128)(2,1)} %bitcast.77), custom_call_target="tpu_custom_call" | custom-call | flops 1879048192 | bytes 5767168 | tf_op jit(solution)/shard_map/pallas_call | solution.py:179
  121.3 0.6 collective-permute-start.28
  121.9 1.5 collective-permute-start.30
  123.4 5.0 %shard_map.67 = (bf16[2,448,256]{2,1,0:T(8,128)(2,1)S(1)}, bf16[2,448,256]{2,1,0:T(8,128)(2,1)S(1)}, bf16[4,448,256]{2,1,0:T(8,128)(2,1)S(1)}) custom-call(s32[10]{0:T(128)S(1)} %stack.78.flags, bf16[896,1024]{1,0:T(8,128)(2,1)} %get-tuple-element.54.x_ref, bf16[1,2,8,128,2048]{4,3,2,1,0:T(8,128)(2,1)} %bitcast.74, bf16[8,2,128,1024]{3,2,1,0:T(8,128)(2,1)} %bitcast.78), custom_call_target="tpu_custom_call" | custom-call | flops 1879048192 | bytes 5767168 | tf_op jit(solution)/shard_map/pallas_call | solution.py:179
  128.5 1.8 collective-permute-start.19
  130.6 4.2 %collective-permute-done.28 = bf16[2,448,256]{2,1,0:T(8,128)(2,1)S(1)} collective-permute-done((bf16[2,448,256]{2,1,0:T(8,128)(2,1)S(1)}, bf16[2,448,256]{2,1,0:T(8,128)(2,1)S(1)}, u32[]{:S(2)}, u32[]{:S(2)}) %collective-permute-start.28) | collective-permute-done | bytes 458784 | tf_op jit(solution)/shard_map/ppermute | solution.py:202
  134.7 1.7 collective-permute-done.30
  136.9 1.7 collective-permute-start.31
  138.7 5.9 %collective-permute-done.19 = bf16[2,448,256]{2,1,0:T(8,128)(2,1)S(1)} collective-permute-done((bf16[2,448,256]{2,1,0:T(8,128)(2,1)S(1)}, bf16[2,448,256]{2,1,0:T(8,128)(2,1)S(1)}, u32[]{:S(2)}, u32[]{:S(2)}) %collective-permute-start.19) | collective-permute-done | bytes 458784 | tf_op jit(solution)/shard_map/ppermute | solution.py:202
  144.6 1.7 collective-permute-done.21
  146.3 0.9 fusion.14
  147.5 1.7 collective-permute-start.22
  149.3 1.2 collective-permute-done.31
  150.7 0.8 pad_maximum_fusion.3
  151.5 4.0 %collective-permute-start.32 = (bf16[2,448,256]{2,1,0:T(8,128)(2,1)}, bf16[2,448,256]{2,1,0:T(8,128)(2,1)S(1)}, u32[]{:S(2)}, u32[]{:S(2)}) collective-permute-start(bf16[2,448,256]{2,1,0:T(8,128)(2,1)} %pad_maximum_fusion.3), channel_id=1, source_target_pairs={{0,4},{1,5},{2,6},{3,7},{4,0},{5,1},{6,2},{7,3},{8,12},{9,13},{10,... | collective-permute-start | bytes 1376264 | tf_op jit(solution)/shard_map/ppermute | solution.py:212
  155.5 5.0 %shard_map.68 = (bf16[2,448,256]{2,1,0:T(8,128)(2,1)S(1)}, bf16[2,448,256]{2,1,0:T(8,128)(2,1)S(1)}, bf16[4,448,256]{2,1,0:T(8,128)(2,1)S(1)}) custom-call(s32[10]{0:T(128)S(1)} %stack.78.flags, bf16[896,1024]{1,0:T(8,128)(2,1)} %get-tuple-element.77.x_ref, bf16[1,2,8,128,2048]{4,3,2,1,0:T(8,128)(2,1)} %bitcast.75, bf16[8,2,128,1024]{3,2,1,0:T(8,128)(2,1)} %bitcast.79), custom_call_target="tpu_custom_call" | custom-call | flops 1879048192 | bytes 5767168 | tf_op jit(solution)/shard_map/pallas_call | solution.py:179
  160.5 0.8 collective-permute-start.24
  161.3 1.3 collective-permute-start.25
  162.6 5.0 %shard_map.66 = (bf16[2,448,256]{2,1,0:T(8,128)(2,1)S(1)}, bf16[2,448,256]{2,1,0:T(8,128)(2,1)S(1)}, bf16[4,448,256]{2,1,0:T(8,128)(2,1)S(1)}) custom-call(s32[10]{0:T(128)S(1)} %stack.78.flags, bf16[896,1024]{1,0:T(8,128)(2,1)} %get-tuple-element.54.x_ref, bf16[1,2,8,128,2048]{4,3,2,1,0:T(8,128)(2,1)} %bitcast.76, bf16[8,2,128,1024]{3,2,1,0:T(8,128)(2,1)} %bitcast.80), custom_call_target="tpu_custom_call" | custom-call | flops 1879048192 | bytes 5767168 | tf_op jit(solution)/shard_map/pallas_call | solution.py:179
  167.6 2.0 collective-permute-start.15
  169.7 1.1 fusion.20
  170.9 3.1 %collective-permute-done.24.plus1 = bf16[2,448,256]{2,1,0:T(8,128)(2,1)S(1)} collective-permute-done((bf16[2,448,256]{2,1,0:T(8,128)(2,1)S(1)}, bf16[2,448,256]{2,1,0:T(8,128)(2,1)S(1)}, u32[]{:S(2)}, u32[]{:S(2)}) %collective-permute-start.24) | collective-permute-done | bytes 458784 | tf_op jit(solution)/shard_map/ppermute | solution.py:202
  174.0 1.9 collective-permute-start.23
  176.1 2.0 collective-permute-start.26
  178.1 5.8 %collective-permute-done.15.plus1 = bf16[2,448,256]{2,1,0:T(8,128)(2,1)S(1)} collective-permute-done((bf16[2,448,256]{2,1,0:T(8,128)(2,1)S(1)}, bf16[2,448,256]{2,1,0:T(8,128)(2,1)S(1)}, u32[]{:S(2)}, u32[]{:S(2)}) %collective-permute-start.15) | collective-permute-done | bytes 458784 | tf_op jit(solution)/shard_map/ppermute | solution.py:202
  184.4 2.9 %collective-permute-start.17 = (bf16[448,256]{1,0:T(8,128)(2,1)S(1)}, bf16[448,256]{1,0:T(8,128)(2,1)S(1)}, u32[]{:S(2)}, u32[]{:S(2)}) collective-permute-start(bf16[448,256]{1,0:T(8,128)(2,1)S(1)} %get-tuple-element.100), channel_id=1, source_target_pairs={{0,1},{1,2},{2,3},{3,0},{4,5},{5,6},{6,7},{7,4},{8,9},{9,10},{10,1... | collective-permute-start | bytes 688136 | tf_op jit(solution)/shard_map/ppermute | solution.py:204
  187.3 1.5 collective-permute-done.26.plus2
  188.8 2.3 %collective-permute-done.27.minus2 = bf16[448,256]{1,0:T(8,128)(2,1)S(1)} collective-permute-done((bf16[448,256]{1,0:T(8,128)(2,1)S(1)}, bf16[448,256]{1,0:T(8,128)(2,1)S(1)}, u32[]{:S(2)}, u32[]{:S(2)}) %collective-permute-start.27) | collective-permute-done | bytes 229408 | tf_op jit(solution)/shard_map/ppermute | solution.py:205
  191.1 1.1 shard_map.70.refs_0_
  192.2 2.3 %collective-permute-done.18.minus2 = bf16[448,256]{1,0:T(8,128)(2,1)S(1)} collective-permute-done((bf16[448,256]{1,0:T(8,128)(2,1)S(1)}, bf16[448,256]{1,0:T(8,128)(2,1)S(1)}, u32[]{:S(2)}, u32[]{:S(2)}) %collective-permute-start.18) | collective-permute-done | bytes 229408 | tf_op jit(solution)/shard_map/ppermute | solution.py:205
  194.5 1.1 shard_map.71
  (78 shorter events, 4.9 us)
Async XLA Ops:
  6.5 109.8 %all-gather.7.cloned.1.call-start = ((), (), s32[]{:S(2)}) async-start(), calls=%async_computation.1 | async-start | bytes 4718592 | tf_op jit(solution)/shard_map/all_gather | solution.py:133
  6.5 0.7 copy-start.2
  7.2 14.2 %copy-start.6 = (bf16[896,1024]{1,0:T(8,128)(2,1)S(1)}, bf16[896,1024]{1,0:T(8,128)(2,1)}, u32[]{:S(2)}) copy-start(bf16[896,1024]{1,0:T(8,128)(2,1)} %param.6) | copy-start | bytes 5505028
  7.2 15.3 %copy-start.4 = (bf16[896,1024]{1,0:T(8,128)(2,1)S(1)}, bf16[896,1024]{1,0:T(8,128)(2,1)}, u32[]{:S(2)}) copy-start(bf16[896,1024]{1,0:T(8,128)(2,1)} %param.7) | copy-start | bytes 5505028
  11.3 11.7 %copy-start.3 = (bf16[1,2,1024]{2,1,0:T(2,128)(2,1)S(1)}, bf16[1,2,1024]{2,1,0:T(2,128)(2,1)}, u32[]{:S(2)}) copy-start(bf16[1,2,1024]{2,1,0:T(2,128)(2,1)} %g_ref.3) | copy-start | bytes 12292
  11.3 18.7 %collective-permute-start = (bf16[2,256,1024]{2,1,0:T(8,128)(2,1)}, bf16[2,256,1024]{2,1,0:T(8,128)(2,1)}, u32[]{:S(2)}, u32[]{:S(2)}) collective-permute-start(bf16[2,256,1024]{2,1,0:T(8,128)(2,1)} %get-tuple-element.47), channel_id=1, source_target_pairs={{0,16},{1,17},{2,18},{3,19},{4,20},{5,21},{6,22},{7,23}} | collective-permute-start | bytes 3145736 | tf_op jit(solution)/shard_map/ppermute | solution.py:114
  15.8 22.9 %collective-permute-start.1 = (bf16[2,256,1024]{2,1,0:T(8,128)(2,1)}, bf16[2,256,1024]{2,1,0:T(8,128)(2,1)}, u32[]{:S(2)}, u32[]{:S(2)}) collective-permute-start(bf16[2,256,1024]{2,1,0:T(8,128)(2,1)} %get-tuple-element.48), channel_id=1, source_target_pairs={{0,32},{1,33},{2,34},{3,35},{4,36},{5,37},{6,38},{7,39}} | collective-permute-start | bytes 3145736 | tf_op jit(solution)/shard_map/ppermute | solution.py:114
  19.1 19.6 %collective-permute-start.2 = (bf16[2,256,1024]{2,1,0:T(8,128)(2,1)}, bf16[2,256,1024]{2,1,0:T(8,128)(2,1)}, u32[]{:S(2)}, u32[]{:S(2)}) collective-permute-start(bf16[2,256,1024]{2,1,0:T(8,128)(2,1)} %get-tuple-element.49), channel_id=1, source_target_pairs={{0,48},{1,49},{2,50},{3,51},{4,52},{5,53},{6,54},{7,55}} | collective-permute-start | bytes 3145736 | tf_op jit(solution)/shard_map/ppermute | solution.py:114
  23.0 4.1 %copy-start.5 = (bf16[896,1024]{1,0:T(8,128)(2,1)S(1)}, bf16[896,1024]{1,0:T(8,128)(2,1)}, u32[]{:S(2)}) copy-start(bf16[896,1024]{1,0:T(8,128)(2,1)} %param.7) | copy-start | bytes 5505028
  23.0 4.1 %copy-start.7 = (bf16[896,1024]{1,0:T(8,128)(2,1)S(1)}, bf16[896,1024]{1,0:T(8,128)(2,1)}, u32[]{:S(2)}) copy-start(bf16[896,1024]{1,0:T(8,128)(2,1)} %param.6) | copy-start | bytes 5505028
  40.0 13.6 %collective-permute-start.3 = (bf16[2,256,1024]{2,1,0:T(8,128)(2,1)S(1)}, bf16[2,256,1024]{2,1,0:T(8,128)(2,1)}, u32[]{:S(2)}, u32[]{:S(2)}) collective-permute-start(bf16[2,256,1024]{2,1,0:T(8,128)(2,1)S(1)} %select_select_fusion.1), channel_id=1, source_target_pairs={{0,128},{16,144},{32,160},{48,176},{1,129},{17,145},{33,161},{49,1... | collective-permute-start | bytes 3145736 | tf_op jit(solution)/shard_map/ppermute | solution.py:120
  42.3 13.9 %collective-permute-start.5 = (bf16[2,256,1024]{2,1,0:T(8,128)(2,1)}, bf16[2,256,1024]{2,1,0:T(8,128)(2,1)}, u32[]{:S(2)}, u32[]{:S(2)}) collective-permute-start(bf16[2,256,1024]{2,1,0:T(8,128)(2,1)} %get-tuple-element.57), channel_id=1, source_target_pairs={{0,16},{1,17},{2,18},{3,19},{4,20},{5,21},{6,22},{7,23}} | collective-permute-start | bytes 3145736 | tf_op jit(solution)/shard_map/ppermute | solution.py:114
  44.6 22.9 %collective-permute-start.6 = (bf16[2,256,1024]{2,1,0:T(8,128)(2,1)}, bf16[2,256,1024]{2,1,0:T(8,128)(2,1)}, u32[]{:S(2)}, u32[]{:S(2)}) collective-permute-start(bf16[2,256,1024]{2,1,0:T(8,128)(2,1)} %get-tuple-element.58), channel_id=1, source_target_pairs={{0,32},{1,33},{2,34},{3,35},{4,36},{5,37},{6,38},{7,39}} | collective-permute-start | bytes 3145736 | tf_op jit(solution)/shard_map/ppermute | solution.py:114
  50.8 16.6 %collective-permute-start.7 = (bf16[2,256,1024]{2,1,0:T(8,128)(2,1)}, bf16[2,256,1024]{2,1,0:T(8,128)(2,1)}, u32[]{:S(2)}, u32[]{:S(2)}) collective-permute-start(bf16[2,256,1024]{2,1,0:T(8,128)(2,1)} %get-tuple-element.59), channel_id=1, source_target_pairs={{0,48},{1,49},{2,50},{3,51},{4,52},{5,53},{6,54},{7,55}} | collective-permute-start | bytes 3145736 | tf_op jit(solution)/shard_map/ppermute | solution.py:114
  53.8 15.2 %collective-permute-start.4 = (bf16[2,256,1024]{2,1,0:T(8,128)(2,1)S(1)}, bf16[2,256,1024]{2,1,0:T(8,128)(2,1)}, u32[]{:S(2)}, u32[]{:S(2)}) collective-permute-start(bf16[2,256,1024]{2,1,0:T(8,128)(2,1)S(1)} %broadcast_select_fusion.1), channel_id=1, source_target_pairs={{0,64},{16,80},{32,96},{48,112},{128,192},{144,208},{160,224},{176... | collective-permute-start | bytes 3145736 | tf_op jit(solution)/shard_map/ppermute | solution.py:122
  69.1 31.4 %copy-start.12 = (s32[896]{0:T(1024)S(1)}, s32[896]{0:T(1024)}, u32[]{:S(2)}) copy-start(s32[896]{0:T(1024)} %param.11) | copy-start | bytes 10756
  69.2 2.8 %collective-permute-start.8 = (bf16[2,128,1024]{2,1,0:T(8,128)(2,1)S(1)}, bf16[2,128,1024]{2,1,0:T(8,128)(2,1)S(1)}, u32[]{:S(2)}, u32[]{:S(2)}) collective-permute-start(bf16[2,128,1024]{2,1,0:T(8,128)(2,1)S(1)} %slice.95), channel_id=1, source_target_pairs={{0,8},{16,24},{32,40},{48,56},{64,72},{80,88},{96,104},{112,120},{... | collective-permute-start | bytes 1572872 | tf_op jit(solution)/shard_map/ppermute | solution.py:128
  72.9 82.6 %all-gather.5.cloned.1.call-start = ((), (), s32[]{:S(2)}) async-start(), calls=%async_computation | async-start | bytes 4718592 | tf_op jit(solution)/shard_map/all_gather | solution.py:133
  72.9 25.2 %collective-permute-start.9 = (bf16[2,256,1024]{2,1,0:T(8,128)(2,1)S(1)}, bf16[2,256,1024]{2,1,0:T(8,128)(2,1)S(1)}, u32[]{:S(2)}, u32[]{:S(2)}) collective-permute-start(bf16[2,256,1024]{2,1,0:T(8,128)(2,1)S(1)} %select_select_fusion), channel_id=1, source_target_pairs={{0,128},{16,144},{32,160},{48,176},{1,129},{17,145},{33,161},{49,1... | collective-permute-start | bytes 3145736 | tf_op jit(solution)/shard_map/ppermute | solution.py:287
  78.0 20.1 %collective-permute-start.10 = (f32[2,896]{1,0:T(2,128)S(1)}, f32[2,896]{1,0:T(2,128)S(1)}, u32[]{:S(2)}, u32[]{:S(2)}) collective-permute-start(f32[2,896]{1,0:T(2,128)S(1)} %pad_maximum_fusion.4), channel_id=1, source_target_pairs={{0,4},{1,5},{2,6},{3,7},{4,0},{5,1},{6,2},{7,3},{8,12},{9,13},{10,... | collective-permute-start | bytes 21512 | tf_op jit(solution)/shard_map/ppermute | solution.py:289
  98.3 13.6 %collective-permute-start.11 = (bf16[2,256,1024]{2,1,0:T(8,128)(2,1)S(1)}, bf16[2,256,1024]{2,1,0:T(8,128)(2,1)S(1)}, u32[]{:S(2)}, u32[]{:S(2)}) collective-permute-start(bf16[2,256,1024]{2,1,0:T(8,128)(2,1)S(1)} %broadcast_select_fusion), channel_id=1, source_target_pairs={{0,64},{16,80},{32,96},{48,112},{128,192},{144,208},{160,224},{176... | collective-permute-start | bytes 3145736 | tf_op jit(solution)/shard_map/ppermute | solution.py:292
  99.6 3.7 %collective-permute-start.12 = (f32[2,896]{1,0:T(2,128)S(1)}, f32[2,896]{1,0:T(2,128)S(1)}, u32[]{:S(2)}, u32[]{:S(2)}) collective-permute-start(f32[2,896]{1,0:T(2,128)S(1)} %add.156), channel_id=1, source_target_pairs={{0,1},{1,0},{2,3},{3,2},{4,5},{5,4},{6,7},{7,6},{8,9},{9,8},{10,11... | collective-permute-start | bytes 21512 | tf_op jit(solution)/shard_map/ppermute | solution.py:294
  103.3 5.1 %collective-permute-start.13 = (f32[2,896]{1,0:T(2,128)S(1)}, f32[2,896]{1,0:T(2,128)S(1)}, u32[]{:S(2)}, u32[]{:S(2)}) collective-permute-start(f32[2,896]{1,0:T(2,128)S(1)} %add.157), channel_id=1, source_target_pairs={{0,2},{1,3},{2,0},{3,1},{4,6},{5,7},{6,4},{7,5},{8,10},{9,11},{10,... | collective-permute-start | bytes 21512 | tf_op jit(solution)/shard_map/ppermute | solution.py:294
  112.4 2.8 %collective-permute-start.14 = (bf16[2,128,1024]{2,1,0:T(8,128)(2,1)S(1)}, bf16[2,128,1024]{2,1,0:T(8,128)(2,1)S(1)}, u32[]{:S(2)}, u32[]{:S(2)}) collective-permute-start(bf16[2,128,1024]{2,1,0:T(8,128)(2,1)S(1)} %slice.123), channel_id=1, source_target_pairs={{0,8},{16,24},{32,40},{48,56},{64,72},{80,88},{96,104},{112,120},{... | collective-permute-start | bytes 1572872 | tf_op jit(solution)/shard_map/ppermute | solution.py:128
  121.3 13.4 %collective-permute-start.28 = (bf16[2,448,256]{2,1,0:T(8,128)(2,1)S(1)}, bf16[2,448,256]{2,1,0:T(8,128)(2,1)S(1)}, u32[]{:S(2)}, u32[]{:S(2)}) collective-permute-start(bf16[2,448,256]{2,1,0:T(8,128)(2,1)S(1)} %get-tuple-element.82), channel_id=1, source_target_pairs={{0,1},{1,2},{2,3},{3,0},{4,5},{5,6},{6,7},{7,4},{8,9},{9,10},{10,1... | collective-permute-start | bytes 1376264 | tf_op jit(solution)/shard_map/ppermute | solution.py:202
  121.9 14.6 %collective-permute-start.30 = (bf16[2,448,256]{2,1,0:T(8,128)(2,1)S(1)}, bf16[2,448,256]{2,1,0:T(8,128)(2,1)S(1)}, u32[]{:S(2)}, u32[]{:S(2)}) collective-permute-start(bf16[2,448,256]{2,1,0:T(8,128)(2,1)S(1)} %get-tuple-element.83), channel_id=1, source_target_pairs={{0,3},{1,0},{2,1},{3,2},{4,7},{5,4},{6,5},{7,6},{8,11},{9,8},{10,9... | collective-permute-start | bytes 1376264 | tf_op jit(solution)/shard_map/ppermute | solution.py:203
  128.4 17.9 %copy-start = (bf16[4,448,256]{2,1,0:T(8,128)(2,1)}, bf16[4,448,256]{2,1,0:T(8,128)(2,1)S(1)}, u32[]{:S(2)}) copy-start(bf16[4,448,256]{2,1,0:T(8,128)(2,1)S(1)} %get-tuple-element.71) | copy-start | bytes 2752516
  128.5 16.1 %collective-permute-start.19 = (bf16[2,448,256]{2,1,0:T(8,128)(2,1)S(1)}, bf16[2,448,256]{2,1,0:T(8,128)(2,1)S(1)}, u32[]{:S(2)}, u32[]{:S(2)}) collective-permute-start(bf16[2,448,256]{2,1,0:T(8,128)(2,1)S(1)} %get-tuple-element.72), channel_id=1, source_target_pairs={{0,1},{1,2},{2,3},{3,0},{4,5},{5,6},{6,7},{7,4},{8,9},{9,10},{10,1... | collective-permute-start | bytes 1376264 | tf_op jit(solution)/shard_map/ppermute | solution.py:202
  130.2 16.1 %collective-permute-start.21 = (bf16[2,448,256]{2,1,0:T(8,128)(2,1)S(1)}, bf16[2,448,256]{2,1,0:T(8,128)(2,1)S(1)}, u32[]{:S(2)}, u32[]{:S(2)}) collective-permute-start(bf16[2,448,256]{2,1,0:T(8,128)(2,1)S(1)} %get-tuple-element.73), channel_id=1, source_target_pairs={{0,3},{1,0},{2,1},{3,2},{4,7},{5,4},{6,5},{7,6},{8,11},{9,8},{10,9... | collective-permute-start | bytes 1376264 | tf_op jit(solution)/shard_map/ppermute | solution.py:203
  136.6 12.7 %collective-permute-start.29 = (bf16[448,256]{1,0:T(8,128)(2,1)S(1)}, bf16[448,256]{1,0:T(8,128)(2,1)S(1)}, u32[]{:S(2)}, u32[]{:S(2)}) collective-permute-start(bf16[448,256]{1,0:T(8,128)(2,1)S(1)} %get-tuple-element.91), channel_id=1, source_target_pairs={{0,1},{1,2},{2,3},{3,0},{4,5},{5,6},{6,7},{7,4},{8,9},{9,10},{10,1... | collective-permute-start | bytes 688136 | tf_op jit(solution)/shard_map/ppermute | solution.py:204
  136.9 13.6 %collective-permute-start.31 = (bf16[448,256]{1,0:T(8,128)(2,1)S(1)}, bf16[448,256]{1,0:T(8,128)(2,1)S(1)}, u32[]{:S(2)}, u32[]{:S(2)}) collective-permute-start(bf16[448,256]{1,0:T(8,128)(2,1)S(1)} %get-tuple-element.92), channel_id=1, source_target_pairs={{0,3},{1,0},{2,1},{3,2},{4,7},{5,4},{6,5},{7,6},{8,11},{9,8},{10,9... | collective-permute-start | bytes 688136 | tf_op jit(solution)/shard_map/ppermute | solution.py:205
  144.6 6.9 %copy-start.8 = (bf16[2,448,256]{2,1,0:T(8,128)(2,1)}, bf16[2,448,256]{2,1,0:T(8,128)(2,1)S(1)}, u32[]{:S(2)}) copy-start(bf16[2,448,256]{2,1,0:T(8,128)(2,1)S(1)} %collective-permute-done.19) | copy-start | bytes 1376260
  146.3 5.2 %copy-start.10 = (bf16[2,448,256]{2,1,0:T(8,128)(2,1)}, bf16[2,448,256]{2,1,0:T(8,128)(2,1)S(1)}, u32[]{:S(2)}) copy-start(bf16[2,448,256]{2,1,0:T(8,128)(2,1)S(1)} %collective-permute-done.21) | copy-start | bytes 1376260
  147.2 20.4 %collective-permute-start.20 = (bf16[448,256]{1,0:T(8,128)(2,1)}, bf16[448,256]{1,0:T(8,128)(2,1)S(1)}, u32[]{:S(2)}, u32[]{:S(2)}) collective-permute-start(bf16[448,256]{1,0:T(8,128)(2,1)} %get-tuple-element.97), channel_id=1, source_target_pairs={{0,1},{1,2},{2,3},{3,0},{4,5},{5,6},{6,7},{7,4},{8,9},{9,10},{10,1... | collective-permute-start | bytes 688136 | tf_op jit(solution)/shard_map/ppermute | solution.py:204
  147.5 22.1 %collective-permute-start.22 = (bf16[448,256]{1,0:T(8,128)(2,1)}, bf16[448,256]{1,0:T(8,128)(2,1)}, u32[]{:S(2)}, u32[]{:S(2)}) collective-permute-start(bf16[448,256]{1,0:T(8,128)(2,1)} %get-tuple-element.98), channel_id=1, source_target_pairs={{0,3},{1,0},{2,1},{3,2},{4,7},{5,4},{6,5},{7,6},{8,11},{9,8},{10,9... | collective-permute-start | bytes 688136 | tf_op jit(solution)/shard_map/ppermute | solution.py:205
  151.5 35.8 %collective-permute-start.32 = (bf16[2,448,256]{2,1,0:T(8,128)(2,1)}, bf16[2,448,256]{2,1,0:T(8,128)(2,1)S(1)}, u32[]{:S(2)}, u32[]{:S(2)}) collective-permute-start(bf16[2,448,256]{2,1,0:T(8,128)(2,1)} %pad_maximum_fusion.3), channel_id=1, source_target_pairs={{0,4},{1,5},{2,6},{3,7},{4,0},{5,1},{6,2},{7,3},{8,12},{9,13},{10,... | collective-permute-start | bytes 1376264 | tf_op jit(solution)/shard_map/ppermute | solution.py:212
  160.5 13.5 %collective-permute-start.24 = (bf16[2,448,256]{2,1,0:T(8,128)(2,1)S(1)}, bf16[2,448,256]{2,1,0:T(8,128)(2,1)S(1)}, u32[]{:S(2)}, u32[]{:S(2)}) collective-permute-start(bf16[2,448,256]{2,1,0:T(8,128)(2,1)S(1)} %get-tuple-element.79), channel_id=1, source_target_pairs={{0,1},{1,2},{2,3},{3,0},{4,5},{5,6},{6,7},{7,4},{8,9},{9,10},{10,1... | collective-permute-start | bytes 1376264 | tf_op jit(solution)/shard_map/ppermute | solution.py:202
  161.3 8.4 %copy-start.1 = (bf16[4,448,256]{2,1,0:T(8,128)(2,1)S(1)}, bf16[4,448,256]{2,1,0:T(8,128)(2,1)}, u32[]{:S(2)}) copy-start(bf16[4,448,256]{2,1,0:T(8,128)(2,1)} %copy-done) | copy-start | bytes 2752516
  161.3 8.4 %copy-start.9 = (bf16[2,448,256]{2,1,0:T(8,128)(2,1)S(1)}, bf16[2,448,256]{2,1,0:T(8,128)(2,1)}, u32[]{:S(2)}) copy-start(bf16[2,448,256]{2,1,0:T(8,128)(2,1)} %copy-done.8) | copy-start | bytes 1376260
  161.3 8.4 %copy-start.11 = (bf16[2,448,256]{2,1,0:T(8,128)(2,1)S(1)}, bf16[2,448,256]{2,1,0:T(8,128)(2,1)}, u32[]{:S(2)}) copy-start(bf16[2,448,256]{2,1,0:T(8,128)(2,1)} %copy-done.10) | copy-start | bytes 1376260
  161.3 14.7 %collective-permute-start.25 = (bf16[2,448,256]{2,1,0:T(8,128)(2,1)S(1)}, bf16[2,448,256]{2,1,0:T(8,128)(2,1)S(1)}, u32[]{:S(2)}, u32[]{:S(2)}) collective-permute-start(bf16[2,448,256]{2,1,0:T(8,128)(2,1)S(1)} %get-tuple-element.80), channel_id=1, source_target_pairs={{0,3},{1,0},{2,1},{3,2},{4,7},{5,4},{6,5},{7,6},{8,11},{9,8},{10,9... | collective-permute-start | bytes 1376264 | tf_op jit(solution)/shard_map/ppermute | solution.py:203
  167.6 16.2 %collective-permute-start.15 = (bf16[2,448,256]{2,1,0:T(8,128)(2,1)S(1)}, bf16[2,448,256]{2,1,0:T(8,128)(2,1)S(1)}, u32[]{:S(2)}, u32[]{:S(2)}) collective-permute-start(bf16[2,448,256]{2,1,0:T(8,128)(2,1)S(1)} %get-tuple-element.69), channel_id=1, source_target_pairs={{0,1},{1,2},{2,3},{3,0},{4,5},{5,6},{6,7},{7,4},{8,9},{9,10},{10,1... | collective-permute-start | bytes 1376264 | tf_op jit(solution)/shard_map/ppermute | solution.py:202
  169.6 14.7 %collective-permute-start.16 = (bf16[2,448,256]{2,1,0:T(8,128)(2,1)S(1)}, bf16[2,448,256]{2,1,0:T(8,128)(2,1)S(1)}, u32[]{:S(2)}, u32[]{:S(2)}) collective-permute-start(bf16[2,448,256]{2,1,0:T(8,128)(2,1)S(1)} %get-tuple-element.70), channel_id=1, source_target_pairs={{0,3},{1,0},{2,1},{3,2},{4,7},{5,4},{6,5},{7,6},{8,11},{9,8},{10,9... | collective-permute-start | bytes 1376264 | tf_op jit(solution)/shard_map/ppermute | solution.py:203
  174.0 18.2 %collective-permute-start.23 = (bf16[2,448,256]{2,1,0:T(8,128)(2,1)S(1)}, bf16[2,448,256]{2,1,0:T(8,128)(2,1)S(1)}, u32[]{:S(2)}, u32[]{:S(2)}) collective-permute-start(bf16[2,448,256]{2,1,0:T(8,128)(2,1)S(1)} %pad_maximum_fusion.2), channel_id=1, source_target_pairs={{0,4},{1,5},{2,6},{3,7},{4,0},{5,1},{6,2},{7,3},{8,12},{9,13},{10,... | collective-permute-start | bytes 1376264 | tf_op jit(solution)/shard_map/ppermute | solution.py:212
  176.1 12.7 %collective-permute-start.26 = (bf16[448,256]{1,0:T(8,128)(2,1)S(1)}, bf16[448,256]{1,0:T(8,128)(2,1)S(1)}, u32[]{:S(2)}, u32[]{:S(2)}) collective-permute-start(bf16[448,256]{1,0:T(8,128)(2,1)S(1)} %get-tuple-element.94), channel_id=1, source_target_pairs={{0,1},{1,2},{2,3},{3,0},{4,5},{5,6},{6,7},{7,4},{8,9},{9,10},{10,1... | collective-permute-start | bytes 688136 | tf_op jit(solution)/shard_map/ppermute | solution.py:204
  183.9 7.2 %collective-permute-start.27 = (bf16[448,256]{1,0:T(8,128)(2,1)S(1)}, bf16[448,256]{1,0:T(8,128)(2,1)S(1)}, u32[]{:S(2)}, u32[]{:S(2)}) collective-permute-start(bf16[448,256]{1,0:T(8,128)(2,1)S(1)} %get-tuple-element.93), channel_id=1, source_target_pairs={{0,3},{1,0},{2,1},{3,2},{4,7},{5,4},{6,5},{7,6},{8,11},{9,8},{10,9... | collective-permute-start | bytes 688136 | tf_op jit(solution)/shard_map/ppermute | solution.py:205
  184.4 7.8 %collective-permute-start.17 = (bf16[448,256]{1,0:T(8,128)(2,1)S(1)}, bf16[448,256]{1,0:T(8,128)(2,1)S(1)}, u32[]{:S(2)}, u32[]{:S(2)}) collective-permute-start(bf16[448,256]{1,0:T(8,128)(2,1)S(1)} %get-tuple-element.100), channel_id=1, source_target_pairs={{0,1},{1,2},{2,3},{3,0},{4,5},{5,6},{6,7},{7,4},{8,9},{9,10},{10,1... | collective-permute-start | bytes 688136 | tf_op jit(solution)/shard_map/ppermute | solution.py:204
  187.3 7.2 %collective-permute-start.18 = (bf16[448,256]{1,0:T(8,128)(2,1)S(1)}, bf16[448,256]{1,0:T(8,128)(2,1)S(1)}, u32[]{:S(2)}, u32[]{:S(2)}) collective-permute-start(bf16[448,256]{1,0:T(8,128)(2,1)S(1)} %get-tuple-element.99), channel_id=1, source_target_pairs={{0,3},{1,0},{2,1},{3,2},{4,7},{5,4},{6,5},{7,6},{8,11},{9,8},{10,9... | collective-permute-start | bytes 688136 | tf_op jit(solution)/shard_map/ppermute | solution.py:205
Sparse Core Ops, SparseCore 0:
  73.0 41.4 all-gather.6
  116.4 34.6 all-gather.4

commit v6 on v5

--- a/solution.py
+++ b/solution.py
@@ -65,17 +65,17 @@
     return jnp.dot(a, b, preferred_element_type=jnp.float32)
 
 
-def pieces_kernel(flags, w_ref, g_ref, *refs):
-    out_refs, (raw, near, sems) = refs[:NY], refs[NY:]
+def pieces_kernel(order, flags, w_ref, g_ref, *refs):
+    *out_refs, raw, near, sems = refs
     depth, wide = out_refs[0].shape[1:]
     column = pl.multiple_of(flags[0] * wide, wide)
 
     def read(y):
         rows = pl.ds(y * depth, depth)
-        return pltpu.make_async_copy(w_ref.at[0, :, rows, pl.ds(column, wide)], raw.at[y], sems.at[y])
-
-    order = (2, 1, 3, 0)
-    gain_copy = pltpu.make_async_copy(g_ref, near, sems.at[NY])
+        k = order.index(y)
+        return pltpu.make_async_copy(w_ref.at[0, :, rows, pl.ds(column, wide)], raw.at[k], sems.at[k])
+
+    gain_copy = pltpu.make_async_copy(g_ref, near, sems.at[len(order)])
     gain_copy.start()
     for y in order:
         read(y).start()
@@ -84,29 +84,30 @@
     for layer in range(LAYERS):
         row = near[0, layer:layer + 1, :].astype(jnp.float32)
         gains.append(jnp.broadcast_to(row, (HD, row.shape[1])).T)
-    for y in order:
+    for k, y in enumerate(order):
         read(y).wait()
         for layer in range(LAYERS):
             gain = gains[layer][y * depth:(y + 1) * depth]
             for at in range(0, wide, HD):
-                out_refs[y][layer, :, at:at + HD] = (raw[y, layer, :, at:at + HD].astype(jnp.float32) * gain).astype(LOW)
-
-
-def pieces(weights, gains, row):
+                out_refs[k][layer, :, at:at + HD] = (raw[k, layer, :, at:at + HD].astype(jnp.float32) * gain).astype(LOW)
+
+
+def pieces(weights, gains, row, order):
     depth, wide = weights.shape[2] // NY, weights.shape[3] // 2
     vmem = pl.BlockSpec(memory_space=pltpu.VMEM)
     shape = (LAYERS, depth, wide)
-    return pl.pallas_call(
-        pieces_kernel,
-        out_shape=tuple(jax.ShapeDtypeStruct(shape, LOW) for _ in range(NY)),
+    parts = pl.pallas_call(
+        functools.partial(pieces_kernel, order),
+        out_shape=tuple(jax.ShapeDtypeStruct(shape, LOW) for _ in order),
         in_specs=[pl.BlockSpec(memory_space=pltpu.SMEM), pl.BlockSpec(memory_space=pltpu.HBM), pl.BlockSpec(memory_space=pltpu.HBM)],
-        out_specs=tuple(vmem for _ in range(NY)),
-        scratch_shapes=[pltpu.VMEM((NY, *shape), LOW), pltpu.VMEM(gains.shape, LOW), pltpu.SemaphoreType.DMA((NY + 1,))],
+        out_specs=tuple(vmem for _ in order),
+        scratch_shapes=[pltpu.VMEM((len(order), *shape), LOW), pltpu.VMEM(gains.shape, LOW), pltpu.SemaphoreType.DMA((len(order) + 1,))],
         compiler_params=pltpu.CompilerParams(vmem_limit_bytes=VMEM_LARGE),
         cost_estimate=pl.CostEstimate(
-            flops=LAYERS * NY * depth * wide, bytes_accessed=4 * LAYERS * NY * depth * wide, transcendentals=0
+            flops=LAYERS * len(order) * depth * wide, bytes_accessed=4 * LAYERS * len(order) * depth * wide, transcendentals=0
         ),
     )(row.astype(jnp.int32).reshape(1), weights, gains)
+    return dict(zip(order, parts))
 
 
 def scatter(parts):
@@ -268,8 +269,9 @@
     flags = flags_of(loaded_layers)
     h = place()[0]
     own = weight_buffer.reshape(1, LAYERS, 2 * NY, -1, weight_buffer.shape[3])
-    swap = scatter(pieces(weight_buffer, gain_buffer, 1 - h))
-    keep_parts = pieces(weight_buffer, gain_buffer, h)
+    soon = pieces(weight_buffer, gain_buffer, 1 - h, (2,))
+    swap = scatter(soon | pieces(weight_buffer, gain_buffer, 1 - h, (1, 3, 0)))
+    keep_parts = pieces(weight_buffer, gain_buffer, h, (2, 1, 3, 0))
     wide = [v.astype(jnp.float32) for v in inputs]
     squares = jnp.stack([jnp.sum(jnp.square(v), axis=1) for v in wide])
     scaled = [

time: 206 us -> 205 us (level)
  waiting for transfers between devices: 73.6 us -> 70.2 us
    ppermute x6, waiting for transfers between devices: 20 us -> 16.6 us  [scatter(): lax.ppermute(parts[k], 'chain', from_source(k))]
    pallas_call x2 -> x3, Pallas kernels: 8.06 us -> 8.82 us  [pieces(): pl.pallas_call(functools.partial(pieces_kernel, order), out_shape=tuple((...]
  transfers between devices with their start and end apart: 35 -> 35, of which waited for: 21 -> 21; matrix products, arithmetic and copies ran while one was open for 6% -> 7% of each run, Pallas kernels for 12% -> 13%
where the time goes in v6:
time: 205 us; the launch traced here: 201 us
  waiting for transfers between devices  70.2 us (34%)
  starting transfers between devices  68 us (33%)
  Pallas kernels  31 us (15%)
  other arithmetic  16.4 us (8%)
  between operations  14.6 us (7%)
    ppermute x6, starting transfers between devices, scatter(): lax.ppermute(parts[k], 'chain', from_source(k))  20.9 us
    pallas_call x4, Pallas kernels, product(): pl.pallas_call(functools.partial(product_kernel, layer, COLUMNS + which *...  20 us
    ppermute x4, waiting for transfers between devices, round_x(): plus1 = lax.ppermute(plus, 'tp', X_NEXT)  19.1 us
    ppermute x6, waiting for transfers between devices, scatter(): lax.ppermute(parts[k], 'chain', from_source(k))  16.6 us
    ppermute x1, waiting for transfers between devices, shards(): squares = squares + lax.ppermute(squares, 'tp', H_SWAP)  12.8 us
    pallas_call x3, Pallas kernels, pieces(): pl.pallas_call(functools.partial(pieces_kernel, order), out_shape=tuple((...  8.82 us
    ppermute x1, starting transfers between devices, shards(): squares = squares + lax.ppermute(squares, 'tp', H_SWAP)  7.28 us
    ppermute x2, starting transfers between devices, swapped(): return lax.ppermute(jnp.stack([low, high]).astype(LOW), 'tp', H_SWAP)  5.91 us
  transfers between devices with their start and end apart: 35, of which 21 were waited for; matrix products, arithmetic and copies ran while one was open for 7% of the time, Pallas kernels for 13%

profile of v6, /device:TPU:6, one launch (start us, length us, event | category | flops | bytes accessed | tf_op | source)
XLA Modules:
  0.0 201.4 jit_solution(11725420046047203336)
XLA Ops:
  6.5 0.7 copy-done.2
  7.2 3.2 %shard_map.64 = (bf16[2,256,1024]{2,1,0:T(8,128)(2,1)S(1)}, bf16[2,256,1024]{2,1,0:T(8,128)(2,1)}, bf16[2,256,1024]{2,1,0:T(8,128)(2,1)}) custom-call(s32[1]{0:T(128)} %bitcast.8.flags, bf16[1,2,1024,2048]{3,2,1,0:T(8,128)(2,1)} %w_ref.5, bf16[1,2,1024]{2,1,0:T(2,128)(2,1)S(1)} %copy-done.2), custom_call_target="tpu_custom_call" | custom-call | flops 1572864 | bytes 6291456 | tf_op jit(solution)/shard_map/pallas_call | solution.py:99
  10.5 4.5 %collective-permute-start = (bf16[2,256,1024]{2,1,0:T(8,128)(2,1)S(1)}, bf16[2,256,1024]{2,1,0:T(8,128)(2,1)}, u32[]{:S(2)}, u32[]{:S(2)}) collective-permute-start(bf16[2,256,1024]{2,1,0:T(8,128)(2,1)S(1)} %get-tuple-element.46), channel_id=1, source_target_pairs={{0,16},{1,17},{2,18},{3,19},{4,20},{5,21},{6,22},{7,23}} | collective-permute-start | bytes 3145736 | tf_op jit(solution)/shard_map/ppermute | solution.py:115
  15.0 3.3 %collective-permute-start.2 = (bf16[2,256,1024]{2,1,0:T(8,128)(2,1)}, bf16[2,256,1024]{2,1,0:T(8,128)(2,1)}, u32[]{:S(2)}, u32[]{:S(2)}) collective-permute-start(bf16[2,256,1024]{2,1,0:T(8,128)(2,1)} %get-tuple-element.47), channel_id=1, source_target_pairs={{0,48},{1,49},{2,50},{3,51},{4,52},{5,53},{6,54},{7,55}} | collective-permute-start | bytes 3145736 | tf_op jit(solution)/shard_map/ppermute | solution.py:115
  18.2 1.6 shard_map.65
  19.8 2.3 %collective-permute-start.1 = (bf16[2,256,1024]{2,1,0:T(8,128)(2,1)S(1)}, bf16[2,256,1024]{2,1,0:T(8,128)(2,1)}, u32[]{:S(2)}, u32[]{:S(2)}) collective-permute-start(bf16[2,256,1024]{2,1,0:T(8,128)(2,1)S(1)} %shard_map.65), channel_id=1, source_target_pairs={{0,32},{1,33},{2,34},{3,35},{4,36},{5,37},{6,38},{7,39}} | collective-permute-start | bytes 3145736 | tf_op jit(solution)/shard_map/ppermute | solution.py:115
  23.2 1.9 fusion.2
  25.2 4.0 %shard_map.66 = (bf16[2,256,1024]{2,1,0:T(8,128)(2,1)S(1)}, bf16[2,256,1024]{2,1,0:T(8,128)(2,1)}, bf16[2,256,1024]{2,1,0:T(8,128)(2,1)}, bf16[2,256,1024]{2,1,0:T(8,128)(2,1)}) custom-call(s32[1]{0:T(128)} %bitcast.9.flags, bf16[1,2,1024,2048]{3,2,1,0:T(8,128)(2,1)} %w_ref.5, bf16[1,2,1024]{2,1,0:T(2,128)(2,1)S(1)} %copy-done.3), custom_call_target="tpu_custom_call" | custom-call | flops 2097152 | bytes 8388608 | tf_op jit(solution)/shard_map/pallas_call | solution.py:99
  29.3 3.0 %fusion.4 = (bf16[896,1024]{1,0:T(8,128)(2,1)}, bf16[896,1024]{1,0:T(8,128)(2,1)}) fusion(bf16[896,1024]{1,0:T(8,128)(2,1)S(1)} %copy-done.4, f32[1024]{0:T(1024)S(1)} %bitcast.81, pred[]{:T(512)} %bitcast.12, bf16[896,1024]{1,0:T(8,128)(2,1)S(1)} %copy-done.6, f32[1024]{0:T(1024)S(1)} %bitcast.82, pred[]{:T(512)} %bitcast.10), kind=kLoop, calls=%fused_computation.8 | loop fusion | flops 7340032 | bytes 7348226 | tf_op jit(solution)/shard_map/jit(_where)/select_n | solution.py:278
  32.2 5.3 %collective-permute-done.1 = bf16[2,256,1024]{2,1,0:T(8,128)(2,1)} collective-permute-done((bf16[2,256,1024]{2,1,0:T(8,128)(2,1)S(1)}, bf16[2,256,1024]{2,1,0:T(8,128)(2,1)}, u32[]{:S(2)}, u32[]{:S(2)}) %collective-permute-start.1) | collective-permute-done | bytes 1048608 | tf_op jit(solution)/shard_map/ppermute | solution.py:115
  37.5 1.4 select_select_fusion.1
  38.9 2.3 %collective-permute-start.3 = (bf16[2,256,1024]{2,1,0:T(8,128)(2,1)S(1)}, bf16[2,256,1024]{2,1,0:T(8,128)(2,1)}, u32[]{:S(2)}, u32[]{:S(2)}) collective-permute-start(bf16[2,256,1024]{2,1,0:T(8,128)(2,1)S(1)} %select_select_fusion.1), channel_id=1, source_target_pairs={{0,128},{16,144},{32,160},{48,176},{1,129},{17,145},{33,161},{49,1... | collective-permute-start | bytes 3145736 | tf_op jit(solution)/shard_map/ppermute | solution.py:121
  41.2 2.3 %collective-permute-start.5 = (bf16[2,256,1024]{2,1,0:T(8,128)(2,1)}, bf16[2,256,1024]{2,1,0:T(8,128)(2,1)}, u32[]{:S(2)}, u32[]{:S(2)}) collective-permute-start(bf16[2,256,1024]{2,1,0:T(8,128)(2,1)} %get-tuple-element.55), channel_id=1, source_target_pairs={{0,16},{1,17},{2,18},{3,19},{4,20},{5,21},{6,22},{7,23}} | collective-permute-start | bytes 3145736 | tf_op jit(solution)/shard_map/ppermute | solution.py:115
  43.4 6.4 %collective-permute-start.6 = (bf16[2,256,1024]{2,1,0:T(8,128)(2,1)S(1)}, bf16[2,256,1024]{2,1,0:T(8,128)(2,1)}, u32[]{:S(2)}, u32[]{:S(2)}) collective-permute-start(bf16[2,256,1024]{2,1,0:T(8,128)(2,1)S(1)} %get-tuple-element.56), channel_id=1, source_target_pairs={{0,32},{1,33},{2,34},{3,35},{4,36},{5,37},{6,38},{7,39}} | collective-permute-start | bytes 3145736 | tf_op jit(solution)/shard_map/ppermute | solution.py:115
  49.8 2.3 %collective-permute-start.7 = (bf16[2,256,1024]{2,1,0:T(8,128)(2,1)}, bf16[2,256,1024]{2,1,0:T(8,128)(2,1)}, u32[]{:S(2)}, u32[]{:S(2)}) collective-permute-start(bf16[2,256,1024]{2,1,0:T(8,128)(2,1)} %get-tuple-element.57), channel_id=1, source_target_pairs={{0,48},{1,49},{2,50},{3,51},{4,52},{5,53},{6,54},{7,55}} | collective-permute-start | bytes 3145736 | tf_op jit(solution)/shard_map/ppermute | solution.py:115
  52.6 2.3 %collective-permute-start.4 = (bf16[2,256,1024]{2,1,0:T(8,128)(2,1)S(1)}, bf16[2,256,1024]{2,1,0:T(8,128)(2,1)}, u32[]{:S(2)}, u32[]{:S(2)}) collective-permute-start(bf16[2,256,1024]{2,1,0:T(8,128)(2,1)S(1)} %broadcast_select_fusion.1), channel_id=1, source_target_pairs={{0,64},{16,80},{32,96},{48,112},{128,192},{144,208},{160,224},{176... | collective-permute-start | bytes 3145736 | tf_op jit(solution)/shard_map/ppermute | solution.py:123
  55.1 11.1 %collective-permute-done.6 = bf16[2,256,1024]{2,1,0:T(8,128)(2,1)} collective-permute-done((bf16[2,256,1024]{2,1,0:T(8,128)(2,1)S(1)}, bf16[2,256,1024]{2,1,0:T(8,128)(2,1)}, u32[]{:S(2)}, u32[]{:S(2)}) %collective-permute-start.6) | collective-permute-done | bytes 1048608 | tf_op jit(solution)/shard_map/ppermute | solution.py:115
  66.2 1.7 select_select_fusion
  68.2 1.3 collective-permute-start.8
  69.5 1.5 collective-permute-done.8
  71.0 0.8 slice_select_fusion.1
  71.9 4.9 %collective-permute-start.9 = (bf16[2,256,1024]{2,1,0:T(8,128)(2,1)S(1)}, bf16[2,256,1024]{2,1,0:T(8,128)(2,1)S(1)}, u32[]{:S(2)}, u32[]{:S(2)}) collective-permute-start(bf16[2,256,1024]{2,1,0:T(8,128)(2,1)S(1)} %select_select_fusion), channel_id=1, source_target_pairs={{0,128},{16,144},{32,160},{48,176},{1,129},{17,145},{33,161},{49,1... | collective-permute-start | bytes 3145736 | tf_op jit(solution)/shard_map/ppermute | solution.py:289
  76.8 7.3 %collective-permute-start.10 = (f32[2,896]{1,0:T(2,128)S(1)}, f32[2,896]{1,0:T(2,128)S(1)}, u32[]{:S(2)}, u32[]{:S(2)}) collective-permute-start(f32[2,896]{1,0:T(2,128)S(1)} %pad_maximum_fusion.4), channel_id=1, source_target_pairs={{0,4},{1,5},{2,6},{3,7},{4,0},{5,1},{6,2},{7,3},{8,12},{9,13},{10,... | collective-permute-start | bytes 21512 | tf_op jit(solution)/shard_map/ppermute | solution.py:291
  84.1 12.8 %collective-permute-done.10 = f32[2,896]{1,0:T(2,128)S(1)} collective-permute-done((f32[2,896]{1,0:T(2,128)S(1)}, f32[2,896]{1,0:T(2,128)S(1)}, u32[]{:S(2)}, u32[]{:S(2)}) %collective-permute-start.10) | collective-permute-done | bytes 7200 | tf_op jit(solution)/shard_map/ppermute | solution.py:291
  97.1 1.4 collective-permute-start.11
  98.5 0.9 collective-permute-start.12
  99.4 2.8 %collective-permute-done.12 = f32[2,896]{1,0:T(2,128)S(1)} collective-permute-done((f32[2,896]{1,0:T(2,128)S(1)}, f32[2,896]{1,0:T(2,128)S(1)}, u32[]{:S(2)}, u32[]{:S(2)}) %collective-permute-start.12) | collective-permute-done | bytes 7200 | tf_op jit(solution)/shard_map/ppermute | solution.py:296
  102.2 1.4 collective-permute-start.13
  103.6 1.7 fusion.24
  105.3 2.1 %collective-permute-done.13 = f32[2,896]{1,0:T(2,128)S(1)} collective-permute-done((f32[2,896]{1,0:T(2,128)S(1)}, f32[2,896]{1,0:T(2,128)S(1)}, u32[]{:S(2)}, u32[]{:S(2)}) %collective-permute-start.13) | collective-permute-done | bytes 7200 | tf_op jit(solution)/shard_map/ppermute | solution.py:296
  107.9 2.8 %collective-permute-done.11 = bf16[2,256,1024]{2,1,0:T(8,128)(2,1)S(1)} collective-permute-done((bf16[2,256,1024]{2,1,0:T(8,128)(2,1)S(1)}, bf16[2,256,1024]{2,1,0:T(8,128)(2,1)S(1)}, u32[]{:S(2)}, u32[]{:S(2)}) %collective-permute-start.11) | collective-permute-done | bytes 1048608 | tf_op jit(solution)/shard_map/ppermute | solution.py:294
  111.2 1.5 collective-permute-start.14
  112.7 1.3 collective-permute-done.14
  114.0 0.9 slice_select_fusion
  115.2 5.0 %shard_map.70 = (bf16[2,448,256]{2,1,0:T(8,128)(2,1)S(1)}, bf16[2,448,256]{2,1,0:T(8,128)(2,1)S(1)}, bf16[4,448,256]{2,1,0:T(8,128)(2,1)S(1)}) custom-call(s32[10]{0:T(128)S(1)} %stack.78.flags, bf16[896,1024]{1,0:T(8,128)(2,1)} %get-tuple-element.75.x_ref, bf16[1,2,8,128,2048]{4,3,2,1,0:T(8,128)(2,1)} %bitcast.73, bf16[8,2,128,1024]{3,2,1,0:T(8,128)(2,1)} %bitcast.77), custom_call_target="tpu_custom_call" | custom-call | flops 1879048192 | bytes 5767168 | tf_op jit(solution)/shard_map/pallas_call | solution.py:180
  120.8 1.5 collective-permute-start.30
  122.3 5.0 %shard_map.68 = (bf16[2,448,256]{2,1,0:T(8,128)(2,1)S(1)}, bf16[2,448,256]{2,1,0:T(8,128)(2,1)S(1)}, bf16[4,448,256]{2,1,0:T(8,128)(2,1)S(1)}) custom-call(s32[10]{0:T(128)S(1)} %stack.78.flags, bf16[896,1024]{1,0:T(8,128)(2,1)} %get-tuple-element.52.x_ref, bf16[1,2,8,128,2048]{4,3,2,1,0:T(8,128)(2,1)} %bitcast.74, bf16[8,2,128,1024]{3,2,1,0:T(8,128)(2,1)} %bitcast.78), custom_call_target="tpu_custom_call" | custom-call | flops 1879048192 | bytes 5767168 | tf_op jit(solution)/shard_map/pallas_call | solution.py:180
  127.3 1.8 collective-permute-start.19
  129.4 4.2 %collective-permute-done.28 = bf16[2,448,256]{2,1,0:T(8,128)(2,1)S(1)} collective-permute-done((bf16[2,448,256]{2,1,0:T(8,128)(2,1)S(1)}, bf16[2,448,256]{2,1,0:T(8,128)(2,1)S(1)}, u32[]{:S(2)}, u32[]{:S(2)}) %collective-permute-start.28) | collective-permute-done | bytes 458784 | tf_op jit(solution)/shard_map/ppermute | solution.py:203
  133.6 1.7 collective-permute-done.30
  135.8 1.7 collective-permute-start.31
  137.6 5.9 %collective-permute-done.19 = bf16[2,448,256]{2,1,0:T(8,128)(2,1)S(1)} collective-permute-done((bf16[2,448,256]{2,1,0:T(8,128)(2,1)S(1)}, bf16[2,448,256]{2,1,0:T(8,128)(2,1)S(1)}, u32[]{:S(2)}, u32[]{:S(2)}) %collective-permute-start.19) | collective-permute-done | bytes 458784 | tf_op jit(solution)/shard_map/ppermute | solution.py:203
  143.4 1.7 collective-permute-done.21
  145.2 0.9 fusion.14
  146.4 1.7 collective-permute-start.22
  148.2 1.2 collective-permute-done.31
  149.5 0.8 pad_maximum_fusion.3
  150.4 4.1 %collective-permute-start.32 = (bf16[2,448,256]{2,1,0:T(8,128)(2,1)}, bf16[2,448,256]{2,1,0:T(8,128)(2,1)S(1)}, u32[]{:S(2)}, u32[]{:S(2)}) collective-permute-start(bf16[2,448,256]{2,1,0:T(8,128)(2,1)} %pad_maximum_fusion.3), channel_id=1, source_target_pairs={{0,4},{1,5},{2,6},{3,7},{4,0},{5,1},{6,2},{7,3},{8,12},{9,13},{10,... | collective-permute-start | bytes 1376264 | tf_op jit(solution)/shard_map/ppermute | solution.py:213
  154.4 5.0 %shard_map.69 = (bf16[2,448,256]{2,1,0:T(8,128)(2,1)S(1)}, bf16[2,448,256]{2,1,0:T(8,128)(2,1)S(1)}, bf16[4,448,256]{2,1,0:T(8,128)(2,1)S(1)}) custom-call(s32[10]{0:T(128)S(1)} %stack.78.flags, bf16[896,1024]{1,0:T(8,128)(2,1)} %get-tuple-element.75.x_ref, bf16[1,2,8,128,2048]{4,3,2,1,0:T(8,128)(2,1)} %bitcast.75, bf16[8,2,128,1024]{3,2,1,0:T(8,128)(2,1)} %bitcast.79), custom_call_target="tpu_custom_call" | custom-call | flops 1879048192 | bytes 5767168 | tf_op jit(solution)/shard_map/pallas_call | solution.py:180
  159.4 0.8 collective-permute-start.24
  160.2 1.3 collective-permute-start.25
  161.6 5.0 %shard_map.67 = (bf16[2,448,256]{2,1,0:T(8,128)(2,1)S(1)}, bf16[2,448,256]{2,1,0:T(8,128)(2,1)S(1)}, bf16[4,448,256]{2,1,0:T(8,128)(2,1)S(1)}) custom-call(s32[10]{0:T(128)S(1)} %stack.78.flags, bf16[896,1024]{1,0:T(8,128)(2,1)} %get-tuple-element.52.x_ref, bf16[1,2,8,128,2048]{4,3,2,1,0:T(8,128)(2,1)} %bitcast.76, bf16[8,2,128,1024]{3,2,1,0:T(8,128)(2,1)} %bitcast.80), custom_call_target="tpu_custom_call" | custom-call | flops 1879048192 | bytes 5767168 | tf_op jit(solution)/shard_map/pallas_call | solution.py:180
  166.6 2.0 collective-permute-start.15
  168.7 1.1 fusion.20
  169.9 3.1 %collective-permute-done.24.plus1 = bf16[2,448,256]{2,1,0:T(8,128)(2,1)S(1)} collective-permute-done((bf16[2,448,256]{2,1,0:T(8,128)(2,1)S(1)}, bf16[2,448,256]{2,1,0:T(8,128)(2,1)S(1)}, u32[]{:S(2)}, u32[]{:S(2)}) %collective-permute-start.24) | collective-permute-done | bytes 458784 | tf_op jit(solution)/shard_map/ppermute | solution.py:203
  173.0 1.8 collective-permute-start.23
  174.9 2.0 collective-permute-start.26
  176.9 5.9 %collective-permute-done.15.plus1 = bf16[2,448,256]{2,1,0:T(8,128)(2,1)S(1)} collective-permute-done((bf16[2,448,256]{2,1,0:T(8,128)(2,1)S(1)}, bf16[2,448,256]{2,1,0:T(8,128)(2,1)S(1)}, u32[]{:S(2)}, u32[]{:S(2)}) %collective-permute-start.15) | collective-permute-done | bytes 458784 | tf_op jit(solution)/shard_map/ppermute | solution.py:203
  183.3 2.9 %collective-permute-start.17 = (bf16[448,256]{1,0:T(8,128)(2,1)S(1)}, bf16[448,256]{1,0:T(8,128)(2,1)S(1)}, u32[]{:S(2)}, u32[]{:S(2)}) collective-permute-start(bf16[448,256]{1,0:T(8,128)(2,1)S(1)} %get-tuple-element.98), channel_id=1, source_target_pairs={{0,1},{1,2},{2,3},{3,0},{4,5},{5,6},{6,7},{7,4},{8,9},{9,10},{10,1... | collective-permute-start | bytes 688136 | tf_op jit(solution)/shard_map/ppermute | solution.py:205
  186.2 1.5 collective-permute-done.26.plus2
  187.7 2.3 %collective-permute-done.27.minus2 = bf16[448,256]{1,0:T(8,128)(2,1)S(1)} collective-permute-done((bf16[448,256]{1,0:T(8,128)(2,1)S(1)}, bf16[448,256]{1,0:T(8,128)(2,1)S(1)}, u32[]{:S(2)}, u32[]{:S(2)}) %collective-permute-start.27) | collective-permute-done | bytes 229408 | tf_op jit(solution)/shard_map/ppermute | solution.py:206
  190.0 1.1 shard_map.71.refs_0_
  191.2 2.3 %collective-permute-done.18.minus2 = bf16[448,256]{1,0:T(8,128)(2,1)S(1)} collective-permute-done((bf16[448,256]{1,0:T(8,128)(2,1)S(1)}, bf16[448,256]{1,0:T(8,128)(2,1)S(1)}, u32[]{:S(2)}, u32[]{:S(2)}) %collective-permute-start.18) | collective-permute-done | bytes 229408 | tf_op jit(solution)/shard_map/ppermute | solution.py:206
  193.5 1.1 shard_map.72
  (79 shorter events, 5.5 us)
Async XLA Ops:
  6.5 108.6 %all-gather.7.cloned.1.call-start = ((), (), s32[]{:S(2)}) async-start(), calls=%async_computation.1 | async-start | bytes 4718592 | tf_op jit(solution)/shard_map/all_gather | solution.py:134
  6.5 0.7 copy-start.2
  10.5 21.8 %collective-permute-start = (bf16[2,256,1024]{2,1,0:T(8,128)(2,1)S(1)}, bf16[2,256,1024]{2,1,0:T(8,128)(2,1)}, u32[]{:S(2)}, u32[]{:S(2)}) collective-permute-start(bf16[2,256,1024]{2,1,0:T(8,128)(2,1)S(1)} %get-tuple-element.46), channel_id=1, source_target_pairs={{0,16},{1,17},{2,18},{3,19},{4,20},{5,21},{6,22},{7,23}} | collective-permute-start | bytes 3145736 | tf_op jit(solution)/shard_map/ppermute | solution.py:115
  15.0 7.1 %copy-start.5 = (bf16[896,1024]{1,0:T(8,128)(2,1)S(1)}, bf16[896,1024]{1,0:T(8,128)(2,1)}, u32[]{:S(2)}) copy-start(bf16[896,1024]{1,0:T(8,128)(2,1)} %param.6) | copy-start | bytes 5505028
  15.0 17.3 %collective-permute-start.2 = (bf16[2,256,1024]{2,1,0:T(8,128)(2,1)}, bf16[2,256,1024]{2,1,0:T(8,128)(2,1)}, u32[]{:S(2)}, u32[]{:S(2)}) collective-permute-start(bf16[2,256,1024]{2,1,0:T(8,128)(2,1)} %get-tuple-element.47), channel_id=1, source_target_pairs={{0,48},{1,49},{2,50},{3,51},{4,52},{5,53},{6,54},{7,55}} | collective-permute-start | bytes 3145736 | tf_op jit(solution)/shard_map/ppermute | solution.py:115
  19.8 5.4 %copy-start.3 = (bf16[1,2,1024]{2,1,0:T(2,128)(2,1)S(1)}, bf16[1,2,1024]{2,1,0:T(2,128)(2,1)}, u32[]{:S(2)}) copy-start(bf16[1,2,1024]{2,1,0:T(2,128)(2,1)} %g_ref.5) | copy-start | bytes 12292
  19.8 17.7 %collective-permute-start.1 = (bf16[2,256,1024]{2,1,0:T(8,128)(2,1)S(1)}, bf16[2,256,1024]{2,1,0:T(8,128)(2,1)}, u32[]{:S(2)}, u32[]{:S(2)}) collective-permute-start(bf16[2,256,1024]{2,1,0:T(8,128)(2,1)S(1)} %shard_map.65), channel_id=1, source_target_pairs={{0,32},{1,33},{2,34},{3,35},{4,36},{5,37},{6,38},{7,39}} | collective-permute-start | bytes 3145736 | tf_op jit(solution)/shard_map/ppermute | solution.py:115
  25.2 4.1 %copy-start.4 = (bf16[896,1024]{1,0:T(8,128)(2,1)S(1)}, bf16[896,1024]{1,0:T(8,128)(2,1)}, u32[]{:S(2)}) copy-start(bf16[896,1024]{1,0:T(8,128)(2,1)} %param.7) | copy-start | bytes 5505028
  25.2 4.1 %copy-start.6 = (bf16[896,1024]{1,0:T(8,128)(2,1)S(1)}, bf16[896,1024]{1,0:T(8,128)(2,1)}, u32[]{:S(2)}) copy-start(bf16[896,1024]{1,0:T(8,128)(2,1)} %param.6) | copy-start | bytes 5505028
  29.3 8.2 %copy-start.7 = (bf16[2,256,1024]{2,1,0:T(8,128)(2,1)S(1)}, bf16[2,256,1024]{2,1,0:T(8,128)(2,1)}, u32[]{:S(2)}) copy-start(bf16[2,256,1024]{2,1,0:T(8,128)(2,1)} %get-tuple-element.45) | copy-start | bytes 3145732
  38.9 13.6 %collective-permute-start.3 = (bf16[2,256,1024]{2,1,0:T(8,128)(2,1)S(1)}, bf16[2,256,1024]{2,1,0:T(8,128)(2,1)}, u32[]{:S(2)}, u32[]{:S(2)}) collective-permute-start(bf16[2,256,1024]{2,1,0:T(8,128)(2,1)S(1)} %select_select_fusion.1), channel_id=1, source_target_pairs={{0,128},{16,144},{32,160},{48,176},{1,129},{17,145},{33,161},{49,1... | collective-permute-start | bytes 3145736 | tf_op jit(solution)/shard_map/ppermute | solution.py:121
  41.2 13.9 %collective-permute-start.5 = (bf16[2,256,1024]{2,1,0:T(8,128)(2,1)}, bf16[2,256,1024]{2,1,0:T(8,128)(2,1)}, u32[]{:S(2)}, u32[]{:S(2)}) collective-permute-start(bf16[2,256,1024]{2,1,0:T(8,128)(2,1)} %get-tuple-element.55), channel_id=1, source_target_pairs={{0,16},{1,17},{2,18},{3,19},{4,20},{5,21},{6,22},{7,23}} | collective-permute-start | bytes 3145736 | tf_op jit(solution)/shard_map/ppermute | solution.py:115
  43.4 22.8 %collective-permute-start.6 = (bf16[2,256,1024]{2,1,0:T(8,128)(2,1)S(1)}, bf16[2,256,1024]{2,1,0:T(8,128)(2,1)}, u32[]{:S(2)}, u32[]{:S(2)}) collective-permute-start(bf16[2,256,1024]{2,1,0:T(8,128)(2,1)S(1)} %get-tuple-element.56), channel_id=1, source_target_pairs={{0,32},{1,33},{2,34},{3,35},{4,36},{5,37},{6,38},{7,39}} | collective-permute-start | bytes 3145736 | tf_op jit(solution)/shard_map/ppermute | solution.py:115
  49.8 16.4 %collective-permute-start.7 = (bf16[2,256,1024]{2,1,0:T(8,128)(2,1)}, bf16[2,256,1024]{2,1,0:T(8,128)(2,1)}, u32[]{:S(2)}, u32[]{:S(2)}) collective-permute-start(bf16[2,256,1024]{2,1,0:T(8,128)(2,1)} %get-tuple-element.57), channel_id=1, source_target_pairs={{0,48},{1,49},{2,50},{3,51},{4,52},{5,53},{6,54},{7,55}} | collective-permute-start | bytes 3145736 | tf_op jit(solution)/shard_map/ppermute | solution.py:115
  52.6 15.3 %collective-permute-start.4 = (bf16[2,256,1024]{2,1,0:T(8,128)(2,1)S(1)}, bf16[2,256,1024]{2,1,0:T(8,128)(2,1)}, u32[]{:S(2)}, u32[]{:S(2)}) collective-permute-start(bf16[2,256,1024]{2,1,0:T(8,128)(2,1)S(1)} %broadcast_select_fusion.1), channel_id=1, source_target_pairs={{0,64},{16,80},{32,96},{48,112},{128,192},{144,208},{160,224},{176... | collective-permute-start | bytes 3145736 | tf_op jit(solution)/shard_map/ppermute | solution.py:123
  68.1 31.3 %copy-start.12 = (s32[896]{0:T(1024)S(1)}, s32[896]{0:T(1024)}, u32[]{:S(2)}) copy-start(s32[896]{0:T(1024)} %param.11) | copy-start | bytes 10756
  68.2 2.8 %collective-permute-start.8 = (bf16[2,128,1024]{2,1,0:T(8,128)(2,1)S(1)}, bf16[2,128,1024]{2,1,0:T(8,128)(2,1)S(1)}, u32[]{:S(2)}, u32[]{:S(2)}) collective-permute-start(bf16[2,128,1024]{2,1,0:T(8,128)(2,1)S(1)} %slice.95), channel_id=1, source_target_pairs={{0,8},{16,24},{32,40},{48,56},{64,72},{80,88},{96,104},{112,120},{... | collective-permute-start | bytes 1572872 | tf_op jit(solution)/shard_map/ppermute | solution.py:129
  71.8 82.6 %all-gather.5.cloned.1.call-start = ((), (), s32[]{:S(2)}) async-start(), calls=%async_computation | async-start | bytes 4718592 | tf_op jit(solution)/shard_map/all_gather | solution.py:134
  71.9 25.1 %collective-permute-start.9 = (bf16[2,256,1024]{2,1,0:T(8,128)(2,1)S(1)}, bf16[2,256,1024]{2,1,0:T(8,128)(2,1)S(1)}, u32[]{:S(2)}, u32[]{:S(2)}) collective-permute-start(bf16[2,256,1024]{2,1,0:T(8,128)(2,1)S(1)} %select_select_fusion), channel_id=1, source_target_pairs={{0,128},{16,144},{32,160},{48,176},{1,129},{17,145},{33,161},{49,1... | collective-permute-start | bytes 3145736 | tf_op jit(solution)/shard_map/ppermute | solution.py:289
  76.8 20.1 %collective-permute-start.10 = (f32[2,896]{1,0:T(2,128)S(1)}, f32[2,896]{1,0:T(2,128)S(1)}, u32[]{:S(2)}, u32[]{:S(2)}) collective-permute-start(f32[2,896]{1,0:T(2,128)S(1)} %pad_maximum_fusion.4), channel_id=1, source_target_pairs={{0,4},{1,5},{2,6},{3,7},{4,0},{5,1},{6,2},{7,3},{8,12},{9,13},{10,... | collective-permute-start | bytes 21512 | tf_op jit(solution)/shard_map/ppermute | solution.py:291
  97.1 13.6 %collective-permute-start.11 = (bf16[2,256,1024]{2,1,0:T(8,128)(2,1)S(1)}, bf16[2,256,1024]{2,1,0:T(8,128)(2,1)S(1)}, u32[]{:S(2)}, u32[]{:S(2)}) collective-permute-start(bf16[2,256,1024]{2,1,0:T(8,128)(2,1)S(1)} %broadcast_select_fusion), channel_id=1, source_target_pairs={{0,64},{16,80},{32,96},{48,112},{128,192},{144,208},{160,224},{176... | collective-permute-start | bytes 3145736 | tf_op jit(solution)/shard_map/ppermute | solution.py:294
  98.5 3.7 %collective-permute-start.12 = (f32[2,896]{1,0:T(2,128)S(1)}, f32[2,896]{1,0:T(2,128)S(1)}, u32[]{:S(2)}, u32[]{:S(2)}) collective-permute-start(f32[2,896]{1,0:T(2,128)S(1)} %add.156), channel_id=1, source_target_pairs={{0,1},{1,0},{2,3},{3,2},{4,5},{5,4},{6,7},{7,6},{8,9},{9,8},{10,11... | collective-permute-start | bytes 21512 | tf_op jit(solution)/shard_map/ppermute | solution.py:296
  102.2 5.1 %collective-permute-start.13 = (f32[2,896]{1,0:T(2,128)S(1)}, f32[2,896]{1,0:T(2,128)S(1)}, u32[]{:S(2)}, u32[]{:S(2)}) collective-permute-start(f32[2,896]{1,0:T(2,128)S(1)} %add.157), channel_id=1, source_target_pairs={{0,2},{1,3},{2,0},{3,1},{4,6},{5,7},{6,4},{7,5},{8,10},{9,11},{10,... | collective-permute-start | bytes 21512 | tf_op jit(solution)/shard_map/ppermute | solution.py:296
  111.2 2.8 %collective-permute-start.14 = (bf16[2,128,1024]{2,1,0:T(8,128)(2,1)S(1)}, bf16[2,128,1024]{2,1,0:T(8,128)(2,1)S(1)}, u32[]{:S(2)}, u32[]{:S(2)}) collective-permute-start(bf16[2,128,1024]{2,1,0:T(8,128)(2,1)S(1)} %slice.123), channel_id=1, source_target_pairs={{0,8},{16,24},{32,40},{48,56},{64,72},{80,88},{96,104},{112,120},{... | collective-permute-start | bytes 1572872 | tf_op jit(solution)/shard_map/ppermute | solution.py:129
  120.2 13.4 %collective-permute-start.28 = (bf16[2,448,256]{2,1,0:T(8,128)(2,1)S(1)}, bf16[2,448,256]{2,1,0:T(8,128)(2,1)S(1)}, u32[]{:S(2)}, u32[]{:S(2)}) collective-permute-start(bf16[2,448,256]{2,1,0:T(8,128)(2,1)S(1)} %get-tuple-element.80), channel_id=1, source_target_pairs={{0,1},{1,2},{2,3},{3,0},{4,5},{5,6},{6,7},{7,4},{8,9},{9,10},{10,1... | collective-permute-start | bytes 1376264 | tf_op jit(solution)/shard_map/ppermute | solution.py:203
  120.8 14.6 %collective-permute-start.30 = (bf16[2,448,256]{2,1,0:T(8,128)(2,1)S(1)}, bf16[2,448,256]{2,1,0:T(8,128)(2,1)S(1)}, u32[]{:S(2)}, u32[]{:S(2)}) collective-permute-start(bf16[2,448,256]{2,1,0:T(8,128)(2,1)S(1)} %get-tuple-element.81), channel_id=1, source_target_pairs={{0,3},{1,0},{2,1},{3,2},{4,7},{5,4},{6,5},{7,6},{8,11},{9,8},{10,9... | collective-permute-start | bytes 1376264 | tf_op jit(solution)/shard_map/ppermute | solution.py:204
  127.3 17.9 %copy-start = (bf16[4,448,256]{2,1,0:T(8,128)(2,1)}, bf16[4,448,256]{2,1,0:T(8,128)(2,1)S(1)}, u32[]{:S(2)}) copy-start(bf16[4,448,256]{2,1,0:T(8,128)(2,1)S(1)} %get-tuple-element.69) | copy-start | bytes 2752516
  127.3 16.1 %collective-permute-start.19 = (bf16[2,448,256]{2,1,0:T(8,128)(2,1)S(1)}, bf16[2,448,256]{2,1,0:T(8,128)(2,1)S(1)}, u32[]{:S(2)}, u32[]{:S(2)}) collective-permute-start(bf16[2,448,256]{2,1,0:T(8,128)(2,1)S(1)} %get-tuple-element.70), channel_id=1, source_target_pairs={{0,1},{1,2},{2,3},{3,0},{4,5},{5,6},{6,7},{7,4},{8,9},{9,10},{10,1... | collective-permute-start | bytes 1376264 | tf_op jit(solution)/shard_map/ppermute | solution.py:203
  129.1 16.1 %collective-permute-start.21 = (bf16[2,448,256]{2,1,0:T(8,128)(2,1)S(1)}, bf16[2,448,256]{2,1,0:T(8,128)(2,1)S(1)}, u32[]{:S(2)}, u32[]{:S(2)}) collective-permute-start(bf16[2,448,256]{2,1,0:T(8,128)(2,1)S(1)} %get-tuple-element.71), channel_id=1, source_target_pairs={{0,3},{1,0},{2,1},{3,2},{4,7},{5,4},{6,5},{7,6},{8,11},{9,8},{10,9... | collective-permute-start | bytes 1376264 | tf_op jit(solution)/shard_map/ppermute | solution.py:204
  135.5 12.7 %collective-permute-start.29 = (bf16[448,256]{1,0:T(8,128)(2,1)S(1)}, bf16[448,256]{1,0:T(8,128)(2,1)S(1)}, u32[]{:S(2)}, u32[]{:S(2)}) collective-permute-start(bf16[448,256]{1,0:T(8,128)(2,1)S(1)} %get-tuple-element.89), channel_id=1, source_target_pairs={{0,1},{1,2},{2,3},{3,0},{4,5},{5,6},{6,7},{7,4},{8,9},{9,10},{10,1... | collective-permute-start | bytes 688136 | tf_op jit(solution)/shard_map/ppermute | solution.py:205
  135.8 13.6 %collective-permute-start.31 = (bf16[448,256]{1,0:T(8,128)(2,1)S(1)}, bf16[448,256]{1,0:T(8,128)(2,1)S(1)}, u32[]{:S(2)}, u32[]{:S(2)}) collective-permute-start(bf16[448,256]{1,0:T(8,128)(2,1)S(1)} %get-tuple-element.90), channel_id=1, source_target_pairs={{0,3},{1,0},{2,1},{3,2},{4,7},{5,4},{6,5},{7,6},{8,11},{9,8},{10,9... | collective-permute-start | bytes 688136 | tf_op jit(solution)/shard_map/ppermute | solution.py:206
  143.4 6.9 %copy-start.8 = (bf16[2,448,256]{2,1,0:T(8,128)(2,1)}, bf16[2,448,256]{2,1,0:T(8,128)(2,1)S(1)}, u32[]{:S(2)}) copy-start(bf16[2,448,256]{2,1,0:T(8,128)(2,1)S(1)} %collective-permute-done.19) | copy-start | bytes 1376260
  145.2 5.2 %copy-start.10 = (bf16[2,448,256]{2,1,0:T(8,128)(2,1)}, bf16[2,448,256]{2,1,0:T(8,128)(2,1)S(1)}, u32[]{:S(2)}) copy-start(bf16[2,448,256]{2,1,0:T(8,128)(2,1)S(1)} %collective-permute-done.21) | copy-start | bytes 1376260
  146.1 20.5 %collective-permute-start.20 = (bf16[448,256]{1,0:T(8,128)(2,1)}, bf16[448,256]{1,0:T(8,128)(2,1)S(1)}, u32[]{:S(2)}, u32[]{:S(2)}) collective-permute-start(bf16[448,256]{1,0:T(8,128)(2,1)} %get-tuple-element.95), channel_id=1, source_target_pairs={{0,1},{1,2},{2,3},{3,0},{4,5},{5,6},{6,7},{7,4},{8,9},{9,10},{10,1... | collective-permute-start | bytes 688136 | tf_op jit(solution)/shard_map/ppermute | solution.py:205
  146.4 22.2 %collective-permute-start.22 = (bf16[448,256]{1,0:T(8,128)(2,1)}, bf16[448,256]{1,0:T(8,128)(2,1)}, u32[]{:S(2)}, u32[]{:S(2)}) collective-permute-start(bf16[448,256]{1,0:T(8,128)(2,1)} %get-tuple-element.96), channel_id=1, source_target_pairs={{0,3},{1,0},{2,1},{3,2},{4,7},{5,4},{6,5},{7,6},{8,11},{9,8},{10,9... | collective-permute-start | bytes 688136 | tf_op jit(solution)/shard_map/ppermute | solution.py:206
  150.4 35.9 %collective-permute-start.32 = (bf16[2,448,256]{2,1,0:T(8,128)(2,1)}, bf16[2,448,256]{2,1,0:T(8,128)(2,1)S(1)}, u32[]{:S(2)}, u32[]{:S(2)}) collective-permute-start(bf16[2,448,256]{2,1,0:T(8,128)(2,1)} %pad_maximum_fusion.3), channel_id=1, source_target_pairs={{0,4},{1,5},{2,6},{3,7},{4,0},{5,1},{6,2},{7,3},{8,12},{9,13},{10,... | collective-permute-start | bytes 1376264 | tf_op jit(solution)/shard_map/ppermute | solution.py:213
  159.4 13.5 %collective-permute-start.24 = (bf16[2,448,256]{2,1,0:T(8,128)(2,1)S(1)}, bf16[2,448,256]{2,1,0:T(8,128)(2,1)S(1)}, u32[]{:S(2)}, u32[]{:S(2)}) collective-permute-start(bf16[2,448,256]{2,1,0:T(8,128)(2,1)S(1)} %get-tuple-element.77), channel_id=1, source_target_pairs={{0,1},{1,2},{2,3},{3,0},{4,5},{5,6},{6,7},{7,4},{8,9},{9,10},{10,1... | collective-permute-start | bytes 1376264 | tf_op jit(solution)/shard_map/ppermute | solution.py:203
  160.2 8.5 %copy-start.1 = (bf16[4,448,256]{2,1,0:T(8,128)(2,1)S(1)}, bf16[4,448,256]{2,1,0:T(8,128)(2,1)}, u32[]{:S(2)}) copy-start(bf16[4,448,256]{2,1,0:T(8,128)(2,1)} %copy-done) | copy-start | bytes 2752516
  160.2 8.5 %copy-start.9 = (bf16[2,448,256]{2,1,0:T(8,128)(2,1)S(1)}, bf16[2,448,256]{2,1,0:T(8,128)(2,1)}, u32[]{:S(2)}) copy-start(bf16[2,448,256]{2,1,0:T(8,128)(2,1)} %copy-done.8) | copy-start | bytes 1376260
  160.2 8.5 %copy-start.11 = (bf16[2,448,256]{2,1,0:T(8,128)(2,1)S(1)}, bf16[2,448,256]{2,1,0:T(8,128)(2,1)}, u32[]{:S(2)}) copy-start(bf16[2,448,256]{2,1,0:T(8,128)(2,1)} %copy-done.10) | copy-start | bytes 1376260
  160.2 14.6 %collective-permute-start.25 = (bf16[2,448,256]{2,1,0:T(8,128)(2,1)S(1)}, bf16[2,448,256]{2,1,0:T(8,128)(2,1)S(1)}, u32[]{:S(2)}, u32[]{:S(2)}) collective-permute-start(bf16[2,448,256]{2,1,0:T(8,128)(2,1)S(1)} %get-tuple-element.78), channel_id=1, source_target_pairs={{0,3},{1,0},{2,1},{3,2},{4,7},{5,4},{6,5},{7,6},{8,11},{9,8},{10,9... | collective-permute-start | bytes 1376264 | tf_op jit(solution)/shard_map/ppermute | solution.py:204
  166.6 16.2 %collective-permute-start.15 = (bf16[2,448,256]{2,1,0:T(8,128)(2,1)S(1)}, bf16[2,448,256]{2,1,0:T(8,128)(2,1)S(1)}, u32[]{:S(2)}, u32[]{:S(2)}) collective-permute-start(bf16[2,448,256]{2,1,0:T(8,128)(2,1)S(1)} %get-tuple-element.67), channel_id=1, source_target_pairs={{0,1},{1,2},{2,3},{3,0},{4,5},{5,6},{6,7},{7,4},{8,9},{9,10},{10,1... | collective-permute-start | bytes 1376264 | tf_op jit(solution)/shard_map/ppermute | solution.py:203
  168.6 14.7 %collective-permute-start.16 = (bf16[2,448,256]{2,1,0:T(8,128)(2,1)S(1)}, bf16[2,448,256]{2,1,0:T(8,128)(2,1)S(1)}, u32[]{:S(2)}, u32[]{:S(2)}) collective-permute-start(bf16[2,448,256]{2,1,0:T(8,128)(2,1)S(1)} %get-tuple-element.68), channel_id=1, source_target_pairs={{0,3},{1,0},{2,1},{3,2},{4,7},{5,4},{6,5},{7,6},{8,11},{9,8},{10,9... | collective-permute-start | bytes 1376264 | tf_op jit(solution)/shard_map/ppermute | solution.py:204
  173.0 18.2 %collective-permute-start.23 = (bf16[2,448,256]{2,1,0:T(8,128)(2,1)S(1)}, bf16[2,448,256]{2,1,0:T(8,128)(2,1)S(1)}, u32[]{:S(2)}, u32[]{:S(2)}) collective-permute-start(bf16[2,448,256]{2,1,0:T(8,128)(2,1)S(1)} %pad_maximum_fusion.2), channel_id=1, source_target_pairs={{0,4},{1,5},{2,6},{3,7},{4,0},{5,1},{6,2},{7,3},{8,12},{9,13},{10,... | collective-permute-start | bytes 1376264 | tf_op jit(solution)/shard_map/ppermute | solution.py:213
  174.9 12.8 %collective-permute-start.26 = (bf16[448,256]{1,0:T(8,128)(2,1)S(1)}, bf16[448,256]{1,0:T(8,128)(2,1)S(1)}, u32[]{:S(2)}, u32[]{:S(2)}) collective-permute-start(bf16[448,256]{1,0:T(8,128)(2,1)S(1)} %get-tuple-element.92), channel_id=1, source_target_pairs={{0,1},{1,2},{2,3},{3,0},{4,5},{5,6},{6,7},{7,4},{8,9},{9,10},{10,1... | collective-permute-start | bytes 688136 | tf_op jit(solution)/shard_map/ppermute | solution.py:205
  182.8 7.2 %collective-permute-start.27 = (bf16[448,256]{1,0:T(8,128)(2,1)S(1)}, bf16[448,256]{1,0:T(8,128)(2,1)S(1)}, u32[]{:S(2)}, u32[]{:S(2)}) collective-permute-start(bf16[448,256]{1,0:T(8,128)(2,1)S(1)} %get-tuple-element.91), channel_id=1, source_target_pairs={{0,3},{1,0},{2,1},{3,2},{4,7},{5,4},{6,5},{7,6},{8,11},{9,8},{10,9... | collective-permute-start | bytes 688136 | tf_op jit(solution)/shard_map/ppermute | solution.py:206
  183.3 7.8 %collective-permute-start.17 = (bf16[448,256]{1,0:T(8,128)(2,1)S(1)}, bf16[448,256]{1,0:T(8,128)(2,1)S(1)}, u32[]{:S(2)}, u32[]{:S(2)}) collective-permute-start(bf16[448,256]{1,0:T(8,128)(2,1)S(1)} %get-tuple-element.98), channel_id=1, source_target_pairs={{0,1},{1,2},{2,3},{3,0},{4,5},{5,6},{6,7},{7,4},{8,9},{9,10},{10,1... | collective-permute-start | bytes 688136 | tf_op jit(solution)/shard_map/ppermute | solution.py:205
  186.2 7.2 %collective-permute-start.18 = (bf16[448,256]{1,0:T(8,128)(2,1)S(1)}, bf16[448,256]{1,0:T(8,128)(2,1)S(1)}, u32[]{:S(2)}, u32[]{:S(2)}) collective-permute-start(bf16[448,256]{1,0:T(8,128)(2,1)S(1)} %get-tuple-element.97), channel_id=1, source_target_pairs={{0,3},{1,0},{2,1},{3,2},{4,7},{5,4},{6,5},{7,6},{8,11},{9,8},{10,9... | collective-permute-start | bytes 688136 | tf_op jit(solution)/shard_map/ppermute | solution.py:206
Sparse Core Ops, SparseCore 0:
  72.0 41.4 all-gather.6
  115.3 34.6 all-gather.4
